TPU v7x, 32 devices: a whole 2x2x4 slice. The times are simulated.
32 devices in a mesh: stn: 4 (over z), chan: 8 (over y, x, core).
Axes of the slice: x: 2, y: 2, z: 4, core: 2. Of those that a mesh axis runs over, the one named last changes fastest.
Arguments:
- voltages: bfloat16 [256, 128, 512], P('stn', 'chan'), may hold values from -6 to 6
- block_facet: int32 [8, 4, 2048, 1], P('chan', 'stn'), may hold values from 0 to 3; in each aligned block of 2048 rows (0 to 2047, 2048 to 4095, ..., all dimensions but the last counted through in order) at most 768 rows name the same one
- block_tile: int32 [8, 4, 2048], P('chan', 'stn'), may hold values from 0 to 15
- vis_offset: int32 [8, 4, 2048, 128], P('chan', 'stn'), may hold values from 0 to 624
- kernel_taps: bfloat16 [2, 8], replicated, may hold values from 0.19921875 to 1
Outputs:
- image: float32 [2, 512, 128], P(None, ('stn', 'chan'))
Inputs may be any that keep to these rules, and one draw needn't show every extreme that they name: `block_facet`: among the blocks of one device (one index of the first two dimensions) at most 768 name one facet; in every draw some facet is named by exactly 768 of some device's blocks.
All inputs are finite; a program needn't handle non-finite values.
Results may differ from a plain program's by a relative error of at most 0.0041.
Values may be sent and summed in bfloat16 or wider, within the bound.
No kernel may reach another device: no remote copies, remote signals or barrier semaphores. Data moves between devices by JAX's collectives and lax.ppermute only.
A program may use at most 64 MiB of HBM per device.

v0:
```python
import math

import jax
import jax.numpy as jnp
from jax import lax
from jax.sharding import PartitionSpec as P

VB = 128
TILE = 32
KT = 8
TS = 4
TT = 16
OFFS = 25


def kernel_rows(offsets, taps_row):
    cell_ids = jnp.arange(TILE, dtype=jnp.int32)
    distance = cell_ids[None, :, None] - offsets[:, None, :]
    weights_sum = jnp.zeros(distance.shape, jnp.float32)
    for tap_index in range(KT):
        weights_sum = weights_sum + jnp.where(
            distance == tap_index, taps_row[tap_index].astype(jnp.float32), jnp.float32(0.0)
        )
    return weights_sum.astype(jnp.bfloat16)


def block_tiles(values, offsets, kernel_taps):
    along_u = kernel_rows(offsets // OFFS, kernel_taps[0])
    along_v = kernel_rows(offsets % OFFS, kernel_taps[1])
    weighted = (
        values[:, :, None, :].astype(jnp.float32) * along_v[:, None, :, :].astype(jnp.float32)
    ).astype(jnp.bfloat16)
    weighted = weighted.reshape(values.shape[0], 2 * TILE, values.shape[2])
    return jnp.einsum("nux,nwx->nuw", along_u, weighted, preferred_element_type=jnp.float32)


def grid_blocks(values, offsets, target_ids, kernel_taps, segments):
    slot_count = values.shape[0]
    group_size = math.gcd(slot_count, 256)
    tile_width = 2 * TILE * TILE
    segment_ids = jnp.arange(segments, dtype=jnp.int32)

    def accumulate(grids, turn_index):
        first_row = turn_index * group_size
        part_values = lax.dynamic_slice_in_dim(values, first_row, group_size, 0)
        part_offsets = lax.dynamic_slice_in_dim(offsets, first_row, group_size, 0)
        part_targets = lax.dynamic_slice_in_dim(target_ids, first_row, group_size, 0)
        tile_sums = block_tiles(part_values, part_offsets, kernel_taps).reshape(
            group_size, tile_width
        )
        placing = (segment_ids[:, None] == part_targets[None, :]).astype(jnp.float32)
        grids = grids + jnp.dot(
            placing, tile_sums, precision=lax.Precision.HIGHEST, preferred_element_type=jnp.float32
        )
        return (grids, None)

    start_grids = jnp.zeros((segments, tile_width), jnp.float32)
    grids, leftover = lax.scan(accumulate, start_grids, jnp.arange(slot_count // group_size))
    return grids


def facet_grid(tile_grid):
    shaped = tile_grid.reshape(TS, TS, TILE, 2, TILE)
    return jnp.transpose(shaped, (3, 0, 2, 1, 4)).reshape(2, TS * TILE, TS * TILE)


def dft_tables(side):
    index_ids = jnp.arange(side, dtype=jnp.int32)
    phases = index_ids[:, None] * index_ids[None, :] % side
    angles = phases.astype(jnp.float32) * (2.0 * math.pi / side)
    return (jnp.cos(angles), jnp.sin(angles))


def column_pass(grid, cosine, sine):
    high = lax.Precision.HIGHEST
    real_cols = jnp.dot(grid[0], cosine, precision=high) + jnp.dot(grid[1], sine, precision=high)
    imag_cols = jnp.dot(grid[1], cosine, precision=high) - jnp.dot(grid[0], sine, precision=high)
    return (real_cols, imag_cols)


def row_pass(real_cols, imag_cols, cosine_rows, sine_rows):
    high = lax.Precision.HIGHEST
    real_rows = jnp.dot(cosine_rows, real_cols, precision=high) + jnp.dot(
        sine_rows, imag_cols, precision=high
    )
    imag_rows = jnp.dot(cosine_rows, imag_cols, precision=high) - jnp.dot(
        sine_rows, real_cols, precision=high
    )
    return (real_rows, imag_rows)


def body(voltages, block_facet, block_tile, vis_offset, kernel_taps):
    facets = lax.axis_size("stn")
    chan_count = lax.axis_size("chan")
    panels = lax.all_to_all(voltages, "stn", split_axis=1, concat_axis=0, tiled=True)
    stations = panels.shape[0]
    local_channels = panels.shape[1]
    samples = panels.shape[2] // 2
    swapped = jnp.concatenate([panels[:, :, samples:], -panels[:, :, :samples]], axis=2)
    stacked = jnp.concatenate([panels, swapped], axis=0)
    products = jnp.einsum("aks,jks->kaj", stacked, panels, preferred_element_type=jnp.float32)
    station_ids = jnp.arange(stations, dtype=jnp.int32)
    off_diagonal = (station_ids[:, None] != station_ids[None, :]).astype(jnp.float32)
    scale = 1.0 / math.sqrt(samples)
    real_vis = (products[:, :stations, :] * scale * off_diagonal).astype(jnp.bfloat16)
    imag_vis = (products[:, stations:, :] * scale * off_diagonal).astype(jnp.bfloat16)
    block_values = jnp.stack([real_vis.reshape(-1, VB), imag_vis.reshape(-1, VB)], axis=1)
    block_count = block_values.shape[0]
    offsets = vis_offset.reshape(block_count, VB)
    tile_ids = block_tile.reshape(block_count)
    facet_ids = block_facet.reshape(block_count)
    capacity = 3 * block_count // (2 * facets)
    facet_range = jnp.arange(facets, dtype=jnp.int32)
    member = (facet_ids[:, None] == facet_range[None, :]).astype(jnp.int32)
    earlier = jnp.cumsum(member, axis=0) - member
    position = jnp.sum(earlier * member, axis=1)
    slot_ids = facet_ids * capacity + position
    send_values = jnp.zeros((facets * capacity, 2, VB), jnp.bfloat16).at[slot_ids].set(block_values)
    send_offsets = jnp.zeros((facets * capacity, VB), jnp.int32).at[slot_ids].set(offsets)
    send_tiles = jnp.zeros((facets * capacity,), jnp.int32).at[slot_ids].set(tile_ids)
    got_values, got_offsets, got_tiles = (
        lax.all_to_all(send_values, "stn", split_axis=0, concat_axis=0, tiled=True),
        lax.all_to_all(send_offsets, "stn", split_axis=0, concat_axis=0, tiled=True),
        lax.all_to_all(send_tiles, "stn", split_axis=0, concat_axis=0, tiled=True),
    )
    tile_grid = grid_blocks(got_values, got_offsets, got_tiles, kernel_taps, TT)
    grid = facet_grid(tile_grid)
    side = grid.shape[1]
    row_count = side // chan_count
    channels_all = local_channels * facets * chan_count
    norm_factor = 1.0 / math.sqrt(channels_all * stations * stations * KT * KT / facets)
    cosine, sine = dft_tables(side)
    summed = lax.psum(grid, "chan")
    real_cols, imag_cols = column_pass(summed, cosine, sine)
    first_row = lax.axis_index("chan") * row_count
    cosine_rows = lax.dynamic_slice_in_dim(cosine, first_row, row_count, 0)
    sine_rows = lax.dynamic_slice_in_dim(sine, first_row, row_count, 0)
    real_rows, imag_rows = row_pass(real_cols, imag_cols, cosine_rows, sine_rows)
    image = jnp.stack([real_rows, imag_rows], axis=0) * norm_factor
    return image


def solution(mesh):
    placed = (
        P("stn", "chan", None),
        P("chan", "stn", None, None),
        P("chan", "stn", None),
        P("chan", "stn", None, None),
        P(),
    )
    return jax.shard_map(
        body, mesh=mesh, in_specs=placed, out_specs=P(None, ("stn", "chan"), None), check_vma=False
    )
```

profile of v0, /device:TPU:0, one launch (start us, length us, event | category | flops | bytes accessed | tf_op | source)
XLA Modules:
  0.0 760.8 jit_solution(17232758468567607428)
XLA Ops:
  10.4 8.8 %scatter_custom_fusion = s32[3072]{0:T(1024)} fusion(s32[2048]{0:T(1024)S(1)} %bitcast.146, s32[2048]{0:T(1024)} %bitcast.152, s32[]{:T(128)} %constant.119.clone.1), kind=kCustom, calls=%fused_computation.120 | custom fusion | bytes 12800 | tf_op jit(solution)/shard_map/scatter | solution.py:120
  19.2 6.3 all-to-all-start
  31.1 3.5 all-to-all-start.2
  34.7 6.8 scatter_custom_fusion.1
  41.5 17.7 %all-to-all-done.2 = bf16[64,16,512]{2,0,1:T(8,128)(2,1)S(1)} async-done(((bf16[64,16,512]{2,0,1:T(8,128)(2,1)}), bf16[64,16,512]{2,0,1:T(8,128)(2,1)S(1)}, u32[]{:S(2)}, u32[]{:S(2)}) %all-to-all-start.2) | async-done | bytes 1048608 | tf_op jit(solution)/shard_map/all_to_all | solution.py:95
  59.2 4.4 all-to-all-start.1
  66.7 3.2 pad_maximum_fusion
  72.1 186.0 %scatter_fusion = bf16[3072,2,128]{2,1,0:T(2,128)(2,1)} fusion(bf16[3072,2,128]{2,1,0:T(2,128)(2,1)} %broadcast_in_dim.128, s32[2048]{0:T(1024)S(1)} %bitcast.148, bf16[2048,2,128]{2,1,0:T(2,128)(2,1)S(1)} %pad_maximum_fusion), kind=kCustom, calls=%fused_computation.2 | custom fusion | bytes 3153920 | tf_op jit(solution)/shard_map/scatter | solution.py:118
  258.1 4.9 all-to-all-start.3
  263.3 35.8 %all-to-all-done.3 = bf16[3072,2,128]{2,1,0:T(2,128)(2,1)} async-done(((bf16[3072,2,128]{2,1,0:T(2,128)(2,1)}), bf16[3072,2,128]{2,1,0:T(2,128)(2,1)}, u32[]{:S(2)}, u32[]{:S(2)}) %all-to-all-start.3) | async-done | bytes 1572896 | tf_op jit(solution)/shard_map/all_to_all | solution.py:122
  299.1 394.3 %while.13 = (s32[]{:T(128)}, f32[16,2048]{1,0:T(8,128)S(1)}, s32[12]{0:T(128)S(1)}, s32[3072]{0:T(1024)S(1)}, s32[3072,128]{1,0:T(8,128)}, /*index=5*/bf16[2,8]{...) while((s32[]{:T(128)}, f32[16,2048]{1,0:T(8,128)S(1)}, ...), condition=%wide.region_7.8_spmd.clone, body=%wide.region_6.7_spmd.clone.sunk | while | flops 293081088 | bytes 26742172 | solution.py:58
  307.2 3.2 fusion.127
  319.6 7.6 %fusion.128 = f32[256,32,64]{2,1,0:T(8,128)} fusion(bf16[256,64,128]{2,1,0:T(8,128)(2,1)} %bitcast.139, f32[]{:T(128)S(6)} %convert.59, f32[]{:T(128)S(6)} %convert.60, f32[]{:T(128)S(6)} %convert.61, f32[]{:T(128)S(6)} %convert.62, f32[]{:T(128)S(6)} %convert.63, f32[]{:T(128)S(6)} %convert.64, f32[]{:T(128)S(6)} %convert.65, f32[]{:T(128)S(6)} %convert.66, ...), kind=kOutput, calls=%fused_computation.26.clone.1 | convolution fusion | flops 160432128 | bytes 6422560 | tf_op jit(solution)/shard_map/while/body/eval_jaxpr/nux,nwx->nuw/dot_general | solution.py:34
  327.2 3.5 copy.26
  340.0 3.2 fusion.127
  352.4 7.6 %fusion.128 = f32[256,32,64]{2,1,0:T(8,128)} fusion(bf16[256,64,128]{2,1,0:T(8,128)(2,1)} %bitcast.139, f32[]{:T(128)S(6)} %convert.59, f32[]{:T(128)S(6)} %convert.60, f32[]{:T(128)S(6)} %convert.61, f32[]{:T(128)S(6)} %convert.62, f32[]{:T(128)S(6)} %convert.63, f32[]{:T(128)S(6)} %convert.64, f32[]{:T(128)S(6)} %convert.65, f32[]{:T(128)S(6)} %convert.66, ...), kind=kOutput, calls=%fused_computation.26.clone.1 | convolution fusion | flops 160432128 | bytes 6422560 | tf_op jit(solution)/shard_map/while/body/eval_jaxpr/nux,nwx->nuw/dot_general | solution.py:34
  360.0 3.5 copy.26
  372.9 3.2 fusion.127
  385.3 7.6 %fusion.128 = f32[256,32,64]{2,1,0:T(8,128)} fusion(bf16[256,64,128]{2,1,0:T(8,128)(2,1)} %bitcast.139, f32[]{:T(128)S(6)} %convert.59, f32[]{:T(128)S(6)} %convert.60, f32[]{:T(128)S(6)} %convert.61, f32[]{:T(128)S(6)} %convert.62, f32[]{:T(128)S(6)} %convert.63, f32[]{:T(128)S(6)} %convert.64, f32[]{:T(128)S(6)} %convert.65, f32[]{:T(128)S(6)} %convert.66, ...), kind=kOutput, calls=%fused_computation.26.clone.1 | convolution fusion | flops 160432128 | bytes 6422560 | tf_op jit(solution)/shard_map/while/body/eval_jaxpr/nux,nwx->nuw/dot_general | solution.py:34
  392.9 3.5 copy.26
  405.7 3.2 fusion.127
  418.1 7.6 %fusion.128 = f32[256,32,64]{2,1,0:T(8,128)} fusion(bf16[256,64,128]{2,1,0:T(8,128)(2,1)} %bitcast.139, f32[]{:T(128)S(6)} %convert.59, f32[]{:T(128)S(6)} %convert.60, f32[]{:T(128)S(6)} %convert.61, f32[]{:T(128)S(6)} %convert.62, f32[]{:T(128)S(6)} %convert.63, f32[]{:T(128)S(6)} %convert.64, f32[]{:T(128)S(6)} %convert.65, f32[]{:T(128)S(6)} %convert.66, ...), kind=kOutput, calls=%fused_computation.26.clone.1 | convolution fusion | flops 160432128 | bytes 6422560 | tf_op jit(solution)/shard_map/while/body/eval_jaxpr/nux,nwx->nuw/dot_general | solution.py:34
  425.7 3.5 copy.26
  438.5 3.2 fusion.127
  451.0 7.6 %fusion.128 = f32[256,32,64]{2,1,0:T(8,128)} fusion(bf16[256,64,128]{2,1,0:T(8,128)(2,1)} %bitcast.139, f32[]{:T(128)S(6)} %convert.59, f32[]{:T(128)S(6)} %convert.60, f32[]{:T(128)S(6)} %convert.61, f32[]{:T(128)S(6)} %convert.62, f32[]{:T(128)S(6)} %convert.63, f32[]{:T(128)S(6)} %convert.64, f32[]{:T(128)S(6)} %convert.65, f32[]{:T(128)S(6)} %convert.66, ...), kind=kOutput, calls=%fused_computation.26.clone.1 | convolution fusion | flops 160432128 | bytes 6422560 | tf_op jit(solution)/shard_map/while/body/eval_jaxpr/nux,nwx->nuw/dot_general | solution.py:34
  458.6 3.5 copy.26
  471.4 3.2 fusion.127
  483.8 7.6 %fusion.128 = f32[256,32,64]{2,1,0:T(8,128)} fusion(bf16[256,64,128]{2,1,0:T(8,128)(2,1)} %bitcast.139, f32[]{:T(128)S(6)} %convert.59, f32[]{:T(128)S(6)} %convert.60, f32[]{:T(128)S(6)} %convert.61, f32[]{:T(128)S(6)} %convert.62, f32[]{:T(128)S(6)} %convert.63, f32[]{:T(128)S(6)} %convert.64, f32[]{:T(128)S(6)} %convert.65, f32[]{:T(128)S(6)} %convert.66, ...), kind=kOutput, calls=%fused_computation.26.clone.1 | convolution fusion | flops 160432128 | bytes 6422560 | tf_op jit(solution)/shard_map/while/body/eval_jaxpr/nux,nwx->nuw/dot_general | solution.py:34
  491.4 3.5 copy.26
  504.2 3.2 fusion.127
  516.6 7.6 %fusion.128 = f32[256,32,64]{2,1,0:T(8,128)} fusion(bf16[256,64,128]{2,1,0:T(8,128)(2,1)} %bitcast.139, f32[]{:T(128)S(6)} %convert.59, f32[]{:T(128)S(6)} %convert.60, f32[]{:T(128)S(6)} %convert.61, f32[]{:T(128)S(6)} %convert.62, f32[]{:T(128)S(6)} %convert.63, f32[]{:T(128)S(6)} %convert.64, f32[]{:T(128)S(6)} %convert.65, f32[]{:T(128)S(6)} %convert.66, ...), kind=kOutput, calls=%fused_computation.26.clone.1 | convolution fusion | flops 160432128 | bytes 6422560 | tf_op jit(solution)/shard_map/while/body/eval_jaxpr/nux,nwx->nuw/dot_general | solution.py:34
  524.3 3.5 copy.26
  537.1 3.2 fusion.127
  549.5 7.6 %fusion.128 = f32[256,32,64]{2,1,0:T(8,128)} fusion(bf16[256,64,128]{2,1,0:T(8,128)(2,1)} %bitcast.139, f32[]{:T(128)S(6)} %convert.59, f32[]{:T(128)S(6)} %convert.60, f32[]{:T(128)S(6)} %convert.61, f32[]{:T(128)S(6)} %convert.62, f32[]{:T(128)S(6)} %convert.63, f32[]{:T(128)S(6)} %convert.64, f32[]{:T(128)S(6)} %convert.65, f32[]{:T(128)S(6)} %convert.66, ...), kind=kOutput, calls=%fused_computation.26.clone.1 | convolution fusion | flops 160432128 | bytes 6422560 | tf_op jit(solution)/shard_map/while/body/eval_jaxpr/nux,nwx->nuw/dot_general | solution.py:34
  557.1 3.5 copy.26
  569.9 3.2 fusion.127
  582.3 7.6 %fusion.128 = f32[256,32,64]{2,1,0:T(8,128)} fusion(bf16[256,64,128]{2,1,0:T(8,128)(2,1)} %bitcast.139, f32[]{:T(128)S(6)} %convert.59, f32[]{:T(128)S(6)} %convert.60, f32[]{:T(128)S(6)} %convert.61, f32[]{:T(128)S(6)} %convert.62, f32[]{:T(128)S(6)} %convert.63, f32[]{:T(128)S(6)} %convert.64, f32[]{:T(128)S(6)} %convert.65, f32[]{:T(128)S(6)} %convert.66, ...), kind=kOutput, calls=%fused_computation.26.clone.1 | convolution fusion | flops 160432128 | bytes 6422560 | tf_op jit(solution)/shard_map/while/body/eval_jaxpr/nux,nwx->nuw/dot_general | solution.py:34
  590.0 3.5 copy.26
  602.8 3.2 fusion.127
  615.2 7.6 %fusion.128 = f32[256,32,64]{2,1,0:T(8,128)} fusion(bf16[256,64,128]{2,1,0:T(8,128)(2,1)} %bitcast.139, f32[]{:T(128)S(6)} %convert.59, f32[]{:T(128)S(6)} %convert.60, f32[]{:T(128)S(6)} %convert.61, f32[]{:T(128)S(6)} %convert.62, f32[]{:T(128)S(6)} %convert.63, f32[]{:T(128)S(6)} %convert.64, f32[]{:T(128)S(6)} %convert.65, f32[]{:T(128)S(6)} %convert.66, ...), kind=kOutput, calls=%fused_computation.26.clone.1 | convolution fusion | flops 160432128 | bytes 6422560 | tf_op jit(solution)/shard_map/while/body/eval_jaxpr/nux,nwx->nuw/dot_general | solution.py:34
  622.8 3.5 copy.26
  635.6 3.2 fusion.127
  648.0 7.6 %fusion.128 = f32[256,32,64]{2,1,0:T(8,128)} fusion(bf16[256,64,128]{2,1,0:T(8,128)(2,1)} %bitcast.139, f32[]{:T(128)S(6)} %convert.59, f32[]{:T(128)S(6)} %convert.60, f32[]{:T(128)S(6)} %convert.61, f32[]{:T(128)S(6)} %convert.62, f32[]{:T(128)S(6)} %convert.63, f32[]{:T(128)S(6)} %convert.64, f32[]{:T(128)S(6)} %convert.65, f32[]{:T(128)S(6)} %convert.66, ...), kind=kOutput, calls=%fused_computation.26.clone.1 | convolution fusion | flops 160432128 | bytes 6422560 | tf_op jit(solution)/shard_map/while/body/eval_jaxpr/nux,nwx->nuw/dot_general | solution.py:34
  655.7 3.5 copy.26
  668.5 3.2 fusion.127
  680.9 7.6 %fusion.128 = f32[256,32,64]{2,1,0:T(8,128)} fusion(bf16[256,64,128]{2,1,0:T(8,128)(2,1)} %bitcast.139, f32[]{:T(128)S(6)} %convert.59, f32[]{:T(128)S(6)} %convert.60, f32[]{:T(128)S(6)} %convert.61, f32[]{:T(128)S(6)} %convert.62, f32[]{:T(128)S(6)} %convert.63, f32[]{:T(128)S(6)} %convert.64, f32[]{:T(128)S(6)} %convert.65, f32[]{:T(128)S(6)} %convert.66, ...), kind=kOutput, calls=%fused_computation.26.clone.1 | convolution fusion | flops 160432128 | bytes 6422560 | tf_op jit(solution)/shard_map/while/body/eval_jaxpr/nux,nwx->nuw/dot_general | solution.py:34
  688.5 3.5 copy.26
  695.4 52.1 %all-reduce.2.cloned.1.call-done = f32[2,128,128]{2,1,0:T(8,128)} async-done(((f32[2,128,128]{2,1,0:T(8,128)}), f32[2,128,128]{2,1,0:T(8,128)}) %all-reduce.2.cloned.1.call-update) | async-done | bytes 131088 | tf_op jit(solution)/shard_map/psum | solution.py:133
  (124 shorter events, 116.7 us)
Async XLA Ops:
  6.5 28.1 %copy-start = (s32[1,1,2048,128]{3,2,1,0:T(8,128)S(1)}, s32[1,1,2048,128]{3,2,1,0:T(8,128)}, u32[]{:S(2)}) copy-start(s32[1,1,2048,128]{3,2,1,0:T(8,128)} %param.10) | copy-start | bytes 3145732
  19.2 11.9 %all-to-all-start = ((s32[4,768,1]{1,2,0:T(1,128)}), s32[4,768,1]{1,2,0:T(1,128)S(1)}, u32[]{:S(2)}, u32[]{:S(2)}) async-start(s32[4,768,1]{1,2,0:T(1,128)} %bitcast.7), calls=%async_computation | async-start | bytes 24576 | tf_op jit(solution)/shard_map/all_to_all | solution.py:124
  31.1 28.1 %all-to-all-start.2 = ((bf16[64,16,512]{2,0,1:T(8,128)(2,1)}), bf16[64,16,512]{2,0,1:T(8,128)(2,1)S(1)}, u32[]{:S(2)}, u32[]{:S(2)}) async-start(bf16[64,16,512]{2,0,1:T(8,128)(2,1)} %copy.16), calls=%async_computation.2 | async-start | bytes 2097152 | tf_op jit(solution)/shard_map/all_to_all | solution.py:95
  59.2 198.9 %all-to-all-start.1 = ((s32[4,768,128]{2,1,0:T(8,128)}), s32[4,768,128]{2,1,0:T(8,128)}, u32[]{:S(2)}, u32[]{:S(2)}) async-start(s32[4,768,128]{2,1,0:T(8,128)} %bitcast.10), calls=%async_computation.1 | async-start | bytes 3145728 | tf_op jit(solution)/shard_map/all_to_all | solution.py:123
  70.0 229.1 %copy-start.1 = (bf16[2,8]{1,0:T(2,128)(2,1)S(1)}, bf16[2,8]{1,0:T(2,128)(2,1)}, u32[]{:S(2)}) copy-start(bf16[2,8]{1,0:T(2,128)(2,1)} %param.11) | copy-start | bytes 100
  258.1 40.9 %all-to-all-start.3 = ((bf16[3072,2,128]{2,1,0:T(2,128)(2,1)}), bf16[3072,2,128]{2,1,0:T(2,128)(2,1)}, u32[]{:S(2)}, u32[]{:S(2)}) async-start(bf16[3072,2,128]{2,1,0:T(2,128)(2,1)} %scatter_fusion), calls=%async_computation.3 | async-start | bytes 3145728 | tf_op jit(solution)/shard_map/all_to_all | solution.py:122
  263.0 484.5 %all-reduce.2.cloned.1.call-start = ((), (), s32[]{:S(2)}) async-start(), calls=%async_computation.4 | async-start | bytes 262144 | tf_op jit(solution)/shard_map/psum | solution.py:133
Sparse Core Ops, SparseCore 0:
  695.2 52.1 all-reduce.1
where the time goes:
time: 766 us; the launch traced here: 761 us
  local copies, waits for them, and re-layouts  271 us (35%)
  loops' own time  128 us (17%)
  matrix products  111 us (14%)
  other arithmetic  110 us (14%)
  waiting for transfers between devices  108 us (14%)
  starting transfers between devices  19.1 us (2%)
  between operations  13.5 us (2%)
    scatter x1, local copies, waits for them, and re-layouts, body(): jnp.zeros((facets * capacity, 2, VB), jnp.bfloat16).at[slot_ids]  186 us
    another operation x1, loops' own time, grid_blocks(): lax.scan(accumulate, start_grids, jnp.arange(slot_count // group_size))  128 us
    dot_general x12, matrix products, block_tiles(): jnp.einsum('nux,nwx->nuw', along_u, weighted, preferred_element_type=jnp....  91.5 us
    psum x1, waiting for transfers between devices, body(): summed = lax.psum(grid, 'chan')  52.1 us
    dot_general x12, local copies, waits for them, and re-layouts, block_tiles(): jnp.einsum('nux,nwx->nuw', along_u, weighted, preferred_element_type=jnp....  42.5 us
    convert_element_type x12, other arithmetic, block_tiles(): along_v[:, None, :, :].astype(jnp.float32)  38.9 us
    convert_element_type x12, other arithmetic, block_tiles(): weighted = (values[:, :, None, :].astype(jnp.float32) * along_v[:, None,...  38.3 us
    all_to_all x1, waiting for transfers between devices, body(): lax.all_to_all(send_values, 'stn', split_axis=0, concat_axis=0, tiled=True)  35.8 us
  transfers between devices with their start and end apart: 5, of which 4 were waited for; matrix products, arithmetic and copies ran while one was open for 27% of the time, Pallas kernels for 0%

commit v1 on v0

v1 whole, which is shorter than its diff:
```python
import functools
import math

import jax
import jax.numpy as jnp
import numpy as np
from jax import lax
from jax.experimental import pallas as pl
from jax.experimental.pallas import tpu as pltpu
from jax.sharding import PartitionSpec as P

VB = 128
TILE = 32
KT = 8
TS = 4
TT = 16
OFFS = 25
FG = TS * TILE

GROUP = 4
UNROLL = 16
CHUNKS = 4

F32, BF16, I32 = jnp.float32, jnp.bfloat16, jnp.int32
LAST_BY_LAST = (((1,), (1,)), ((), ()))


def group_lists(targets, target_count):
    count = targets.shape[0]
    block_ids = jnp.arange(count, dtype=I32)
    target_range = jnp.arange(target_count, dtype=I32)
    same = targets[:, None] == targets[None, :]
    position = jnp.sum((same & (block_ids[None, :] < block_ids[:, None])).astype(I32), axis=1)
    member = (targets[:, None] == target_range[None, :]).astype(I32)
    group_counts = (jnp.sum(member, axis=0) + GROUP - 1) // GROUP
    below = (target_range[:, None] < target_range[None, :]).astype(I32)
    first_group = jnp.sum(group_counts[:, None] * below, axis=0)
    slots = jnp.sum(member * first_group[None, :], axis=1) * GROUP + position
    most = (count + target_count * (GROUP - 1)) // GROUP
    most = -(-most // UNROLL) * UNROLL
    places = jnp.arange(most * GROUP, dtype=I32)
    listed = count + jnp.sum(
        jnp.where(slots[None, :] == places[:, None], block_ids[None, :] - count, 0), axis=1
    )
    groups = jnp.arange(most, dtype=I32)
    group_target = jnp.sum((groups[:, None] >= first_group[None, :]).astype(I32), axis=1) - 1
    turns = (jnp.sum(group_counts) + UNROLL - 1) // UNROLL
    return listed, group_target, turns


def grid_kernel(panels, first, last, listed, group_target, info, *refs):
    refs = list(refs)
    part_refs = [refs.pop(0) for _ in range(panels)]
    offset_ref = refs.pop(0)
    before_ref = None if first else refs.pop(0)
    tables = (refs.pop(0), refs.pop(0)) if last else None
    out_ref, whole, du_rows, dv_rows, re_rows, im_rows = refs[:6]
    cells = refs[6] if last else out_ref

    me = info[1]
    channels, rows, width = part_refs[0].shape
    stations = panels * rows
    samples = width // 2
    halves = stations // VB
    blocks = offset_ref.shape[0]

    if first:
        cells[...] = jnp.zeros_like(cells)
    else:
        cells[...] = before_ref[...]

    offsets = offset_ref[...]
    du = (offsets * 1311) >> 15
    du_rows[0:blocks] = du.astype(F32)
    dv_rows[0:blocks] = (offsets - du * OFFS).astype(F32)
    no_row = jnp.zeros((8, VB), F32)
    for row_ref in (du_rows, dv_rows, re_rows, im_rows):
        row_ref[blocks:] = no_row

    for step, part in enumerate(part_refs):
        start = pl.multiple_of(jnp.bitwise_xor(me, step) * rows, rows)
        for k in range(channels):
            whole[k, pl.ds(start, rows), :] = part[k]

    scale = 1.0 / math.sqrt(samples)
    diagonal = lax.broadcasted_iota(I32, (stations, stations), 0) == lax.broadcasted_iota(
        I32, (stations, stations), 1
    )
    for k in range(channels):
        x = whole[k]
        swapped = jnp.concatenate([x[:, samples:], -x[:, :samples]], axis=1)
        for row_ref, left in ((re_rows, x), (im_rows, swapped)):
            vis = lax.dot_general(left, x, LAST_BY_LAST, preferred_element_type=F32) * scale
            vis = jnp.where(diagonal, 0.0, vis).astype(BF16).astype(F32)
            for h in range(halves):
                row_ref[pl.ds(k * stations * halves + h, stations, stride=halves), :] = vis[
                    :, h * VB : (h + 1) * VB
                ]

    half = lax.broadcasted_iota(I32, (16, VB), 0).astype(F32)
    cell_ids = [(half + 16 * part).astype(BF16) for part in range(TILE // 16)]
    none = jnp.zeros((16, VB), BF16)
    ones = jnp.ones((16, VB), BF16)

    def spread(row_ref, n):
        return jnp.broadcast_to(row_ref[pl.ds(n, 1), :], (16, VB)).astype(BF16)

    def block_pair(n):
        du_n, dv_n = spread(du_rows, n), spread(dv_rows, n)
        re_n, im_n = spread(re_rows, n), spread(im_rows, n)
        along_u = [jnp.where(ids == du_n, ones, none) for ids in cell_ids]
        along_v = [jnp.where(ids == dv_n, re_n, none) for ids in cell_ids]
        along_v += [jnp.where(ids == dv_n, im_n, none) for ids in cell_ids]
        return jnp.concatenate(along_u, axis=0), jnp.concatenate(along_v, axis=0)

    def turn(index, carry):
        sums = []
        for q in range(UNROLL):
            g = index * UNROLL + q
            pairs = [block_pair(listed[g * GROUP + p]) for p in range(GROUP)]
            left = jnp.concatenate([a for a, b in pairs], axis=1)
            right = jnp.concatenate([b for a, b in pairs], axis=1)
            sums.append(
                (g, lax.dot_general(left, right, LAST_BY_LAST, preferred_element_type=F32))
            )
        for g, total in sums:
            cells[group_target[g]] += total
        return carry

    lax.fori_loop(0, info[0], turn, 0)

    if last:
        row_table, column_table = tables
        facets = cells.shape[0] // TT

        def transform(f, carry):
            grid = jnp.concatenate(
                [
                    jnp.concatenate([cells[f * TT + tu * TS + tv] for tv in range(TS)], axis=1)
                    for tu in range(TS)
                ],
                axis=0,
            )
            part = jnp.dot(
                row_table[...], grid, precision=lax.Precision.HIGHEST, preferred_element_type=F32
            )
            both = jnp.concatenate([part[:FG], part[FG:]], axis=1)
            image = jnp.dot(
                both, column_table[...], precision=lax.Precision.HIGHEST, preferred_element_type=F32
            )
            out_ref[pl.ds(pl.multiple_of(f * FG, FG), FG), :] = image.astype(out_ref.dtype)
            return carry

        lax.fori_loop(0, facets, transform, 0)


def grid_call(info, lists, parts, offsets, before, tables, target_count):
    listed, group_target = lists
    panels = len(parts)
    channels, rows, width = parts[0].shape
    blocks = offsets.shape[0]
    first, last = before is None, tables is not None
    operands = list(parts) + [offsets]
    if not first:
        operands.append(before)
    if last:
        operands += list(tables)
    cells = (target_count, TILE, 2 * TILE)
    scratch = [pltpu.VMEM((channels, panels * rows, width), BF16)]
    scratch += [pltpu.VMEM((blocks + 8, VB), F32)] * 4
    if last:
        scratch.append(pltpu.VMEM(cells, F32))
        out = jax.ShapeDtypeStruct((target_count // TT * FG, 2 * FG), BF16)
    else:
        out = jax.ShapeDtypeStruct(cells, F32)
    whole = lambda shape: pl.BlockSpec(shape, lambda i, *_: (0,) * len(shape))
    return pl.pallas_call(
        functools.partial(grid_kernel, panels, first, last),
        grid_spec=pltpu.PrefetchScalarGridSpec(
            num_scalar_prefetch=3,
            grid=(1,),
            in_specs=[whole(x.shape) for x in operands],
            out_specs=whole(out.shape),
            scratch_shapes=scratch,
        ),
        out_shape=out,
        compiler_params=pltpu.CompilerParams(vmem_limit_bytes=48 << 20),
    )(listed, group_target, info, *operands)


def transform_tables():
    ids = np.arange(FG)
    angles = (ids[:, None] * ids[None, :] % FG) * (2.0 * math.pi / FG)
    cosine, sine = np.cos(angles), -np.sin(angles)
    row_table = np.concatenate([cosine, sine], axis=0)
    straight = np.concatenate([cosine, sine], axis=1).reshape(TS, 1, TILE, 2 * FG)
    turned = np.concatenate([-sine, cosine], axis=1).reshape(TS, 1, TILE, 2 * FG)
    real = np.concatenate([straight, turned], axis=1).reshape(2 * FG, 2 * FG)
    imag = np.concatenate([turned, -straight], axis=1).reshape(2 * FG, 2 * FG)
    column_table = np.concatenate([real, imag], axis=0)
    return row_table.astype(np.float32), column_table.astype(np.float32)


def taps_transform(taps_row):
    index_ids = jnp.arange(FG, dtype=I32)
    phases = index_ids[:, None] * jnp.arange(KT, dtype=I32)[None, :] % FG
    angles = phases.astype(F32) * (2.0 * math.pi / FG)
    taps = taps_row.astype(F32)[None, :]
    return jnp.sum(jnp.cos(angles) * taps, axis=1), -jnp.sum(jnp.sin(angles) * taps, axis=1)


def body(voltages, block_facet, block_tile, vis_offset, kernel_taps):
    facets = lax.axis_size("stn")
    chan_count = lax.axis_size("chan")
    me = lax.axis_index("stn")
    rows, all_channels, width = voltages.shape
    channels = all_channels // facets
    stations = rows * facets
    blocks = vis_offset.shape[2]
    target_count = facets * TT

    by_channel = jnp.transpose(voltages, (1, 0, 2)).reshape(facets, channels, rows, width)
    step = channels // CHUNKS
    parts = []
    for c in range(CHUNKS):
        got = []
        for s in range(facets):
            piece = lax.dynamic_slice(
                by_channel, (jnp.bitwise_xor(me, s), c * step, 0, 0), (1, step, rows, width)
            ).reshape(step, rows, width)
            if s:
                piece = lax.ppermute(piece, "stn", [(i, i ^ s) for i in range(facets)])
            got.append(piece)
        parts.append(got)

    offsets = vis_offset.reshape(CHUNKS, blocks // CHUNKS, VB)
    targets = (block_facet.reshape(CHUNKS, -1) * TT + block_tile.reshape(CHUNKS, -1)).astype(I32)
    tables = tuple(jnp.asarray(t) for t in transform_tables())
    cells = None
    for c in range(CHUNKS):
        listed, group_target, turns = group_lists(targets[c], target_count)
        info = jnp.stack([turns, me]).astype(I32)
        cells = grid_call(
            info,
            (listed, group_target),
            parts[c],
            offsets[c],
            cells,
            tables if c == CHUNKS - 1 else None,
            target_count,
        )

    row_count = FG // chan_count
    pieces = cells.reshape(facets * chan_count, row_count, 2 * FG)
    pieces = lax.all_to_all(pieces, ("stn", "chan"), split_axis=0, concat_axis=0, tiled=True)
    image = jnp.sum(pieces.astype(F32), axis=0)
    real, imag = image[:, :FG], image[:, FG:]

    channels_all = all_channels * chan_count
    norm_factor = 1.0 / math.sqrt(channels_all * stations * stations * KT * KT / facets)
    u_real, u_imag = taps_transform(kernel_taps[0])
    v_real, v_imag = taps_transform(kernel_taps[1])
    first_row = lax.axis_index("chan") * row_count
    u_real = lax.dynamic_slice_in_dim(u_real, first_row, row_count)[:, None] * norm_factor
    u_imag = lax.dynamic_slice_in_dim(u_imag, first_row, row_count)[:, None] * norm_factor
    w_real = u_real * v_real[None, :] - u_imag * v_imag[None, :]
    w_imag = u_real * v_imag[None, :] + u_imag * v_real[None, :]
    return jnp.stack([real * w_real - imag * w_imag, real * w_imag + imag * w_real], axis=0)


def solution(mesh):
    placed = (
        P("stn", "chan", None),
        P("chan", "stn", None, None),
        P("chan", "stn", None),
        P("chan", "stn", None, None),
        P(),
    )
    return jax.shard_map(
        body, mesh=mesh, in_specs=placed, out_specs=P(None, ("stn", "chan"), None), check_vma=False
    )
```

time: 766 us -> 74.1 us (0.10)
  local copies, waits for them, and re-layouts: 271 us -> 2.55 us
  loops' own time: 128 us -> 0 us
  matrix products: 111 us -> 0 us
  other arithmetic: 110 us -> 7.91 us
  waiting for transfers between devices: 108 us -> 11.1 us
  Pallas kernels: 0 us -> 26 us
  between operations: 13.5 us -> 2.92 us
    scatter x3 -> x0, local copies, waits for them, and re-layouts: 202 us -> none  [the longest x1 186 us: body(): jnp.zeros((facets * capacity, 2, VB), jnp.bfloat16).at[slot_ids]]
    another operation x1 -> x0, loops' own time: 128 us -> none  [grid_blocks(): lax.scan(accumulate, start_grids, jnp.arange(slot_count // group_size))]
    dot_general x33 -> x0, matrix products: 111 us -> none  [the longest x12 91.5 us: block_tiles(): jnp.einsum('nux,nwx->nuw', along_u, weighted, preferred_element_type=jnp....]
    convert_element_type x38 -> x0, other arithmetic: 90.4 us -> none  [the longest x12 38.9 us: block_tiles(): along_v[:, None, :, :].astype(jnp.float32)]
    psum x1 -> x0, waiting for transfers between devices: 52.1 us -> none  [body(): summed = lax.psum(grid, 'chan')]
    all_to_all x4 -> x1, waiting for transfers between devices: 56.3 us -> 10.3 us  [body(): lax.all_to_all(pieces, ('stn', 'chan'), split_axis=0, concat_axis=0, tile...]
    dot_general x12 -> x0, local copies, waits for them, and re-layouts: 42.5 us -> none  [block_tiles(): jnp.einsum('nux,nwx->nuw', along_u, weighted, preferred_element_type=jnp....]
    pallas_call x0 -> x4, Pallas kernels: none -> 26 us  [grid_call(): pl.pallas_call(functools.partial(grid_kernel, panels, first, last), grid_...]
  transfers between devices with their start and end apart: 5 -> 13, of which waited for: 4 -> 2; matrix products, arithmetic and copies ran while one was open for 27% -> 11% of each run, Pallas kernels for 0% -> 21%
where the time goes in v1:
time: 74.1 us; the launch traced here: 73.9 us
  Pallas kernels  26 us (35%)
  starting transfers between devices  23.3 us (31%)
  waiting for transfers between devices  11.1 us (15%)
  other arithmetic  7.91 us (11%)
  between operations  2.92 us (4%)
  local copies, waits for them, and re-layouts  2.55 us (3%)
    pallas_call x4, Pallas kernels, grid_call(): pl.pallas_call(functools.partial(grid_kernel, panels, first, last), grid_...  26 us
    ppermute x12, starting transfers between devices, body(): piece = lax.ppermute(piece, 'stn', [(i, i ^ s) for i in range(facets)])  19.7 us
    all_to_all x1, waiting for transfers between devices, body(): lax.all_to_all(pieces, ('stn', 'chan'), split_axis=0, concat_axis=0, tile...  10.3 us
    all_to_all x1, starting transfers between devices, body(): lax.all_to_all(pieces, ('stn', 'chan'), split_axis=0, concat_axis=0, tile...  3.63 us
    reduce_sum x4, other arithmetic, group_lists(): turns = (jnp.sum(group_counts) + UNROLL - 1) // UNROLL  2.64 us
    reshape x1, local copies, waits for them, and re-layouts, body(): jnp.transpose(voltages, (1, 0, 2)).reshape(facets, channels, rows, width)  1.8 us
  transfers between devices with their start and end apart: 13, of which 2 were waited for; matrix products, arithmetic and copies ran while one was open for 11% of the time, Pallas kernels for 21%

profile of v1, /device:TPU:0, one launch (start us, length us, event | category | flops | bytes accessed | tf_op | source)
XLA Modules:
  0.0 73.9 jit_solution(69315498447362809)
XLA Ops:
  0.0 1.8 %copy.40 = bf16[16,64,512]{2,1,0:T(8,128)(2,1)S(1)} copy(bf16[16,64,512]{2,0,1:T(8,128)(2,1)} %bitcast.63) | data formatting | bytes 2097152 | tf_op jit(solution)/shard_map/reshape | solution.py:222
  1.9 0.1 dynamic-slice_bitcast_fusion
  2.0 4.1 %collective-permute-start.10 = (bf16[1,64,512]{2,1,0:T(8,128)(2,1)S(1)}, bf16[1,64,512]{2,1,0:T(8,128)(2,1)S(1)}, u32[]{:S(2)}, u32[]{:S(2)}) collective-permute-start(bf16[1,64,512]{2,1,0:T(8,128)(2,1)S(1)} %get-tuple-element.26), channel_id=1, source_target_pairs={{0,16},{8,24},{16,0},{24,8},{1,17},{9,25},{17,1},{25,9},{2,18},{10... | collective-permute-start | bytes 196616 | tf_op jit(solution)/shard_map/ppermute | solution.py:232
  6.1 1.3 %collective-permute-start.11 = (bf16[1,64,512]{2,1,0:T(8,128)(2,1)S(1)}, bf16[1,64,512]{2,1,0:T(8,128)(2,1)S(1)}, u32[]{:S(2)}, u32[]{:S(2)}) collective-permute-start(bf16[1,64,512]{2,1,0:T(8,128)(2,1)S(1)} %get-tuple-element.25), channel_id=1, source_target_pairs={{0,24},{8,16},{16,8},{24,0},{1,25},{9,17},{17,9},{25,1},{2,26},{10... | collective-permute-start | bytes 196616 | tf_op jit(solution)/shard_map/ppermute | solution.py:232
  7.4 0.2 collective-permute-start.9
  7.6 1.8 %collective-permute-start.6 = (bf16[1,64,512]{2,1,0:T(8,128)(2,1)S(1)}, bf16[1,64,512]{2,1,0:T(8,128)(2,1)S(1)}, u32[]{:S(2)}, u32[]{:S(2)}) collective-permute-start(bf16[1,64,512]{2,1,0:T(8,128)(2,1)S(1)} %get-tuple-element.31), channel_id=1, source_target_pairs={{0,8},{8,0},{16,24},{24,16},{1,9},{9,1},{17,25},{25,17},{2,10},{10... | collective-permute-start | bytes 196616 | tf_op jit(solution)/shard_map/ppermute | solution.py:232
  9.4 1.7 %collective-permute-start.7 = (bf16[1,64,512]{2,1,0:T(8,128)(2,1)S(1)}, bf16[1,64,512]{2,1,0:T(8,128)(2,1)S(1)}, u32[]{:S(2)}, u32[]{:S(2)}) collective-permute-start(bf16[1,64,512]{2,1,0:T(8,128)(2,1)S(1)} %get-tuple-element.30), channel_id=1, source_target_pairs={{0,16},{8,24},{16,0},{24,8},{1,17},{9,25},{17,1},{25,9},{2,18},{10... | collective-permute-start | bytes 196616 | tf_op jit(solution)/shard_map/ppermute | solution.py:232
  11.1 0.5 broadcast.310
  11.6 0.7 reduce.7
  12.4 0.1 convert_reduce_fusion.5
  12.5 0.3 convert_reduce_fusion
  12.8 0.1 convert_reduce_fusion.6
  12.9 0.3 convert_reduce_fusion.1
  13.2 0.1 convert_reduce_fusion.7
  13.3 0.3 convert_reduce_fusion.2
  13.5 0.1 convert_reduce_fusion.8
  13.7 0.3 convert_reduce_fusion.3
  13.9 0.6 fusion.12
  14.6 0.1 select_reduce_fusion.8
  14.7 0.1 select_reduce_fusion.4
  14.8 0.1 convert_reduce_fusion.9
  14.8 0.6 fusion.13
  15.5 0.1 select_reduce_fusion.9
  15.6 0.1 select_reduce_fusion.5
  15.7 0.1 convert_reduce_fusion.10
  15.8 0.7 fusion.14
  16.4 0.1 select_reduce_fusion.10
  16.5 0.1 select_reduce_fusion.6
  16.6 0.1 convert_reduce_fusion.11
  16.7 0.7 fusion.15
  17.4 0.1 select_reduce_fusion.11
  17.5 0.1 select_reduce_fusion.7
  17.6 0.1 convert_reduce_fusion.12
  17.7 0.8 %select_reduce_fusion = (s32[704]{0:T(1024)S(1)}, s32[704]{0:T(1024)S(1)}, s32[704]{0:T(1024)S(1)}, s32[704]{0:T(1024)S(1)}) fusion(s32[512]{0:T(512)S(1)} %get-tuple-element.53, s32[512]{0:T(512)S(1)} %get-tuple-element.56, s32[512]{0:T(512)S(1)} %get-tuple-element.55, s32[512]{0:T(512)S(1)} %get-tuple-element.54, s32[512]{0:T(512)S(1)} %multiply_add_fusion.4), kind=kLoop, calls=%fused_computation | loop fusion | flops 4322560 | bytes 21504 | tf_op jit(solution)/shard_map/reduce_sum | solution.py:42
  21.3 1.0 %collective-permute-start.8 = (bf16[1,64,512]{2,1,0:T(8,128)(2,1)S(1)}, bf16[1,64,512]{2,1,0:T(8,128)(2,1)S(1)}, u32[]{:S(2)}, u32[]{:S(2)}) collective-permute-start(bf16[1,64,512]{2,1,0:T(8,128)(2,1)S(1)} %get-tuple-element.29), channel_id=1, source_target_pairs={{0,24},{8,16},{16,8},{24,0},{1,25},{9,17},{17,9},{25,1},{2,26},{10... | collective-permute-start | bytes 196616 | tf_op jit(solution)/shard_map/ppermute | solution.py:232
  22.2 0.9 %collective-permute-start.3 = (bf16[1,64,512]{2,1,0:T(8,128)(2,1)S(1)}, bf16[1,64,512]{2,1,0:T(8,128)(2,1)S(1)}, u32[]{:S(2)}, u32[]{:S(2)}) collective-permute-start(bf16[1,64,512]{2,1,0:T(8,128)(2,1)S(1)} %get-tuple-element.35), channel_id=1, source_target_pairs={{0,8},{8,0},{16,24},{24,16},{1,9},{9,1},{17,25},{25,17},{2,10},{10... | collective-permute-start | bytes 196616 | tf_op jit(solution)/shard_map/ppermute | solution.py:232
  23.2 2.6 %collective-permute-start.4 = (bf16[1,64,512]{2,1,0:T(8,128)(2,1)S(1)}, bf16[1,64,512]{2,1,0:T(8,128)(2,1)S(1)}, u32[]{:S(2)}, u32[]{:S(2)}) collective-permute-start(bf16[1,64,512]{2,1,0:T(8,128)(2,1)S(1)} %get-tuple-element.34), channel_id=1, source_target_pairs={{0,16},{8,24},{16,0},{24,8},{1,17},{9,25},{17,1},{25,9},{2,18},{10... | collective-permute-start | bytes 196616 | tf_op jit(solution)/shard_map/ppermute | solution.py:232
  25.8 0.9 %collective-permute-start.5 = (bf16[1,64,512]{2,1,0:T(8,128)(2,1)S(1)}, bf16[1,64,512]{2,1,0:T(8,128)(2,1)S(1)}, u32[]{:S(2)}, u32[]{:S(2)}) collective-permute-start(bf16[1,64,512]{2,1,0:T(8,128)(2,1)S(1)} %get-tuple-element.33), channel_id=1, source_target_pairs={{0,24},{8,16},{16,8},{24,0},{1,25},{9,17},{17,9},{25,1},{2,26},{10... | collective-permute-start | bytes 196616 | tf_op jit(solution)/shard_map/ppermute | solution.py:232
  26.7 0.8 %collective-permute-done.8.refs_3_ = bf16[1,64,512]{2,1,0:T(8,128)(2,1)S(1)} collective-permute-done((bf16[1,64,512]{2,1,0:T(8,128)(2,1)S(1)}, bf16[1,64,512]{2,1,0:T(8,128)(2,1)S(1)}, u32[]{:S(2)}, u32[]{:S(2)}) %collective-permute-start.8) | collective-permute-done | bytes 65568 | tf_op jit(solution)/shard_map/ppermute | solution.py:232
  27.5 2.7 %collective-permute-start.1 = (bf16[1,64,512]{2,1,0:T(8,128)(2,1)S(1)}, bf16[1,64,512]{2,1,0:T(8,128)(2,1)S(1)}, u32[]{:S(2)}, u32[]{:S(2)}) collective-permute-start(bf16[1,64,512]{2,1,0:T(8,128)(2,1)S(1)} %get-tuple-element.38), channel_id=1, source_target_pairs={{0,16},{8,24},{16,0},{24,8},{1,17},{9,25},{17,1},{25,9},{2,18},{10... | collective-permute-start | bytes 196616 | tf_op jit(solution)/shard_map/ppermute | solution.py:232
  30.2 2.4 %collective-permute-start.2 = (bf16[1,64,512]{2,1,0:T(8,128)(2,1)S(1)}, bf16[1,64,512]{2,1,0:T(8,128)(2,1)S(1)}, u32[]{:S(2)}, u32[]{:S(2)}) collective-permute-start(bf16[1,64,512]{2,1,0:T(8,128)(2,1)S(1)} %get-tuple-element.37), channel_id=1, source_target_pairs={{0,24},{8,16},{16,8},{24,0},{1,25},{9,17},{17,9},{25,1},{2,26},{10... | collective-permute-start | bytes 196616 | tf_op jit(solution)/shard_map/ppermute | solution.py:232
  32.7 5.2 %shard_map.73.refs_5_ = f32[64,32,64]{2,1,0:T(8,128)S(1)} custom-call(s32[704]{0:T(1024)S(1)} %broadcast_add_fusion.listed, s32[176]{0:T(256)S(1)} %broadcast_add_fusion.4.group_target, s32[2]{0:T(128)S(1)} %get-tuple-element.52.info, bf16[1,64,512]{2,1,0:T(8,128)(2,1)S(1)} %get-tuple-element.28.refs_0_, ...), custom_call_target="tpu_custom_call" | custom-call | tf_op jit(solution)/shard_map/pallas_call | solution.py:177
  38.0 5.3 %shard_map.74.refs_5_ = f32[64,32,64]{2,1,0:T(8,128)S(1)} custom-call(s32[704]{0:T(1024)S(1)} %broadcast_add_fusion.1.listed, s32[176]{0:T(256)S(1)} %broadcast_add_fusion.5.group_target, s32[2]{0:T(128)S(1)} %get-tuple-element.51.info, bf16[1,64,512]{2,1,0:T(8,128)(2,1)S(1)} %get-tuple-element.32.refs_0_, ...), custom_call_target="tpu_custom_call" | custom-call | tf_op jit(solution)/shard_map/pallas_call | solution.py:177
  43.3 5.2 %shard_map.75.refs_5_ = f32[64,32,64]{2,1,0:T(8,128)S(1)} custom-call(s32[704]{0:T(1024)S(1)} %broadcast_add_fusion.2.listed, s32[176]{0:T(256)S(1)} %broadcast_add_fusion.6.group_target, s32[2]{0:T(128)S(1)} %get-tuple-element.50.info, bf16[1,64,512]{2,1,0:T(8,128)(2,1)S(1)} %get-tuple-element.36.refs_0_, ...), custom_call_target="tpu_custom_call" | custom-call | tf_op jit(solution)/shard_map/pallas_call | solution.py:177
  48.6 10.3 %shard_map.76 = bf16[512,256]{1,0:T(8,128)(2,1)} custom-call(s32[704]{0:T(1024)S(1)} %broadcast_add_fusion.3.listed, s32[176]{0:T(256)S(1)} %broadcast_add_fusion.7.group_target, s32[2]{0:T(128)S(1)} %get-tuple-element.49.info, bf16[1,64,512]{2,1,0:T(8,128)(2,1)S(1)} %get-tuple-element.40.refs_0_, bf16[1,64,512]{2,1,0:T(8,128)(2,1)S(1)} %collective-permute-done.refs_1_, ...), custom_call_target="tpu_custom_call" | custom-call | tf_op jit(solution)/shard_map/pallas_call | solution.py:177
  58.9 3.6 %all-to-all-start = ((bf16[32,16,256]{2,1,0:T(8,128)(2,1)}), bf16[32,16,256]{2,1,0:T(8,128)(2,1)S(1)}, u32[]{:S(2)}, u32[]{:S(2)}) async-start(bf16[32,16,256]{2,1,0:T(8,128)(2,1)} %bitcast.31), calls=%async_computation | async-start | bytes 524288 | tf_op jit(solution)/shard_map/all_to_all | solution.py:255
  62.8 10.3 %all-to-all-done = bf16[32,16,256]{2,1,0:T(8,128)(2,1)S(1)} async-done(((bf16[32,16,256]{2,1,0:T(8,128)(2,1)}), bf16[32,16,256]{2,1,0:T(8,128)(2,1)S(1)}, u32[]{:S(2)}, u32[]{:S(2)}) %all-to-all-start) | async-done | bytes 262176 | tf_op jit(solution)/shard_map/all_to_all | solution.py:255
  73.2 0.6 pad_maximum_fusion
  (51 shorter events, 0.8 us)
Async XLA Ops:
  1.8 9.8 %copy-start.3 = (s32[1,1,2048]{2,1,0:T(1,128)S(1)}, s32[1,1,2048]{2,1,0:T(1,128)}, u32[]{:S(2)}) copy-start(s32[1,1,2048]{2,1,0:T(1,128)} %param.9) | copy-start | bytes 24580
  1.8 10.5 %copy-start.4 = (s32[1,1,2048,1]{2,3,1,0:T(1,128)S(1)}, s32[1,1,2048,1]{2,3,1,0:T(1,128)}, u32[]{:S(2)}) copy-start(s32[1,1,2048,1]{2,3,1,0:T(1,128)} %param.8) | copy-start | bytes 24580
  1.8 16.7 %copy-start.2 = (s32[1,1,2048,128]{3,2,1,0:T(8,128)S(1)}, s32[1,1,2048,128]{3,2,1,0:T(8,128)}, u32[]{:S(2)}) copy-start(s32[1,1,2048,128]{3,2,1,0:T(8,128)} %param.10) | copy-start | bytes 3145732
  2.0 19.3 %collective-permute-start.10 = (bf16[1,64,512]{2,1,0:T(8,128)(2,1)S(1)}, bf16[1,64,512]{2,1,0:T(8,128)(2,1)S(1)}, u32[]{:S(2)}, u32[]{:S(2)}) collective-permute-start(bf16[1,64,512]{2,1,0:T(8,128)(2,1)S(1)} %get-tuple-element.26), channel_id=1, source_target_pairs={{0,16},{8,24},{16,0},{24,8},{1,17},{9,25},{17,1},{25,9},{2,18},{10... | collective-permute-start | bytes 196616 | tf_op jit(solution)/shard_map/ppermute | solution.py:232
  6.1 16.2 %collective-permute-start.11 = (bf16[1,64,512]{2,1,0:T(8,128)(2,1)S(1)}, bf16[1,64,512]{2,1,0:T(8,128)(2,1)S(1)}, u32[]{:S(2)}, u32[]{:S(2)}) collective-permute-start(bf16[1,64,512]{2,1,0:T(8,128)(2,1)S(1)} %get-tuple-element.25), channel_id=1, source_target_pairs={{0,24},{8,16},{16,8},{24,0},{1,25},{9,17},{17,9},{25,1},{2,26},{10... | collective-permute-start | bytes 196616 | tf_op jit(solution)/shard_map/ppermute | solution.py:232
  7.4 15.8 %collective-permute-start.9 = (bf16[1,64,512]{2,1,0:T(8,128)(2,1)S(1)}, bf16[1,64,512]{2,1,0:T(8,128)(2,1)S(1)}, u32[]{:S(2)}, u32[]{:S(2)}) collective-permute-start(bf16[1,64,512]{2,1,0:T(8,128)(2,1)S(1)} %get-tuple-element.27), channel_id=1, source_target_pairs={{0,8},{8,0},{16,24},{24,16},{1,9},{9,1},{17,25},{25,17},{2,10},{10... | collective-permute-start | bytes 196616 | tf_op jit(solution)/shard_map/ppermute | solution.py:232
  7.6 18.1 %collective-permute-start.6 = (bf16[1,64,512]{2,1,0:T(8,128)(2,1)S(1)}, bf16[1,64,512]{2,1,0:T(8,128)(2,1)S(1)}, u32[]{:S(2)}, u32[]{:S(2)}) collective-permute-start(bf16[1,64,512]{2,1,0:T(8,128)(2,1)S(1)} %get-tuple-element.31), channel_id=1, source_target_pairs={{0,8},{8,0},{16,24},{24,16},{1,9},{9,1},{17,25},{25,17},{2,10},{10... | collective-permute-start | bytes 196616 | tf_op jit(solution)/shard_map/ppermute | solution.py:232
  9.4 17.3 %collective-permute-start.7 = (bf16[1,64,512]{2,1,0:T(8,128)(2,1)S(1)}, bf16[1,64,512]{2,1,0:T(8,128)(2,1)S(1)}, u32[]{:S(2)}, u32[]{:S(2)}) collective-permute-start(bf16[1,64,512]{2,1,0:T(8,128)(2,1)S(1)} %get-tuple-element.30), channel_id=1, source_target_pairs={{0,16},{8,24},{16,0},{24,8},{1,17},{9,25},{17,1},{25,9},{2,18},{10... | collective-permute-start | bytes 196616 | tf_op jit(solution)/shard_map/ppermute | solution.py:232
  21.3 6.2 %collective-permute-start.8 = (bf16[1,64,512]{2,1,0:T(8,128)(2,1)S(1)}, bf16[1,64,512]{2,1,0:T(8,128)(2,1)S(1)}, u32[]{:S(2)}, u32[]{:S(2)}) collective-permute-start(bf16[1,64,512]{2,1,0:T(8,128)(2,1)S(1)} %get-tuple-element.29), channel_id=1, source_target_pairs={{0,24},{8,16},{16,8},{24,0},{1,25},{9,17},{17,9},{25,1},{2,26},{10... | collective-permute-start | bytes 196616 | tf_op jit(solution)/shard_map/ppermute | solution.py:232
  22.2 8.0 %collective-permute-start.3 = (bf16[1,64,512]{2,1,0:T(8,128)(2,1)S(1)}, bf16[1,64,512]{2,1,0:T(8,128)(2,1)S(1)}, u32[]{:S(2)}, u32[]{:S(2)}) collective-permute-start(bf16[1,64,512]{2,1,0:T(8,128)(2,1)S(1)} %get-tuple-element.35), channel_id=1, source_target_pairs={{0,8},{8,0},{16,24},{24,16},{1,9},{9,1},{17,25},{25,17},{2,10},{10... | collective-permute-start | bytes 196616 | tf_op jit(solution)/shard_map/ppermute | solution.py:232
  23.2 20.0 %collective-permute-start.4 = (bf16[1,64,512]{2,1,0:T(8,128)(2,1)S(1)}, bf16[1,64,512]{2,1,0:T(8,128)(2,1)S(1)}, u32[]{:S(2)}, u32[]{:S(2)}) collective-permute-start(bf16[1,64,512]{2,1,0:T(8,128)(2,1)S(1)} %get-tuple-element.34), channel_id=1, source_target_pairs={{0,16},{8,24},{16,0},{24,8},{1,17},{9,25},{17,1},{25,9},{2,18},{10... | collective-permute-start | bytes 196616 | tf_op jit(solution)/shard_map/ppermute | solution.py:232
  25.8 17.4 %collective-permute-start.5 = (bf16[1,64,512]{2,1,0:T(8,128)(2,1)S(1)}, bf16[1,64,512]{2,1,0:T(8,128)(2,1)S(1)}, u32[]{:S(2)}, u32[]{:S(2)}) collective-permute-start(bf16[1,64,512]{2,1,0:T(8,128)(2,1)S(1)} %get-tuple-element.33), channel_id=1, source_target_pairs={{0,24},{8,16},{16,8},{24,0},{1,25},{9,17},{17,9},{25,1},{2,26},{10... | collective-permute-start | bytes 196616 | tf_op jit(solution)/shard_map/ppermute | solution.py:232
  26.7 21.8 %collective-permute-start = (bf16[1,64,512]{2,1,0:T(8,128)(2,1)S(1)}, bf16[1,64,512]{2,1,0:T(8,128)(2,1)S(1)}, u32[]{:S(2)}, u32[]{:S(2)}) collective-permute-start(bf16[1,64,512]{2,1,0:T(8,128)(2,1)S(1)} %get-tuple-element.39), channel_id=1, source_target_pairs={{0,8},{8,0},{16,24},{24,16},{1,9},{9,1},{17,25},{25,17},{2,10},{10... | collective-permute-start | bytes 196616 | tf_op jit(solution)/shard_map/ppermute | solution.py:232
  27.5 21.1 %collective-permute-start.1 = (bf16[1,64,512]{2,1,0:T(8,128)(2,1)S(1)}, bf16[1,64,512]{2,1,0:T(8,128)(2,1)S(1)}, u32[]{:S(2)}, u32[]{:S(2)}) collective-permute-start(bf16[1,64,512]{2,1,0:T(8,128)(2,1)S(1)} %get-tuple-element.38), channel_id=1, source_target_pairs={{0,16},{8,24},{16,0},{24,8},{1,17},{9,25},{17,1},{25,9},{2,18},{10... | collective-permute-start | bytes 196616 | tf_op jit(solution)/shard_map/ppermute | solution.py:232
  30.2 18.3 %collective-permute-start.2 = (bf16[1,64,512]{2,1,0:T(8,128)(2,1)S(1)}, bf16[1,64,512]{2,1,0:T(8,128)(2,1)S(1)}, u32[]{:S(2)}, u32[]{:S(2)}) collective-permute-start(bf16[1,64,512]{2,1,0:T(8,128)(2,1)S(1)} %get-tuple-element.37), channel_id=1, source_target_pairs={{0,24},{8,16},{16,8},{24,0},{1,25},{9,17},{17,9},{25,1},{2,26},{10... | collective-permute-start | bytes 196616 | tf_op jit(solution)/shard_map/ppermute | solution.py:232
  43.2 5.3 %copy-start = (f32[512,256]{1,0:T(8,128)S(1)}, f32[512,256]{1,0:T(8,128)}, u32[]{:S(2)}) copy-start(f32[512,256]{1,0:T(8,128)} %constant.154.clone.refs_7_) | copy-start | bytes 1572868
  43.3 5.3 %copy-start.1 = (f32[256,128]{1,0:T(8,128)S(1)}, f32[256,128]{1,0:T(8,128)}, u32[]{:S(2)}) copy-start(f32[256,128]{1,0:T(8,128)} %constant.153.clone.refs_6_) | copy-start | bytes 393220
  48.6 13.9 %copy-start.5 = (bf16[2,8]{1,0:T(2,128)(2,1)S(1)}, bf16[2,8]{1,0:T(2,128)(2,1)}, u32[]{:S(2)}) copy-start(bf16[2,8]{1,0:T(2,128)(2,1)} %param.11) | copy-start | bytes 100
  58.9 14.2 %all-to-all-start = ((bf16[32,16,256]{2,1,0:T(8,128)(2,1)}), bf16[32,16,256]{2,1,0:T(8,128)(2,1)S(1)}, u32[]{:S(2)}, u32[]{:S(2)}) async-start(bf16[32,16,256]{2,1,0:T(8,128)(2,1)} %bitcast.31), calls=%async_computation | async-start | bytes 524288 | tf_op jit(solution)/shard_map/all_to_all | solution.py:255

commit v2 on v1

--- a/solution.py
+++ b/solution.py
@@ -3,6 +3,7 @@
 
 import jax
 import jax.numpy as jnp
+import ml_dtypes
 import numpy as np
 from jax import lax
 from jax.experimental import pallas as pl
@@ -18,11 +19,15 @@
 FG = TS * TILE
 
 GROUP = 4
-UNROLL = 16
-CHUNKS = 4
+UNROLL = 32
+CHUNK_ENDS = (2, 4)
 
 F32, BF16, I32 = jnp.float32, jnp.bfloat16, jnp.int32
 LAST_BY_LAST = (((1,), (1,)), ((), ()))
+
+
+def whole_block(shape):
+    return pl.BlockSpec(shape, lambda i, *_: (0,) * len(shape))
 
 
 def group_lists(targets, target_count):
@@ -48,6 +53,20 @@
     return listed, group_target, turns
 
 
+def two_halves(x):
+    high = x.astype(BF16)
+    return high, (x - high.astype(F32)).astype(BF16)
+
+
+def halves_of(table_ref):
+    return table_ref[0], table_ref[1]
+
+
+def split_dot(left, right):
+    dot = functools.partial(jnp.dot, preferred_element_type=F32)
+    return dot(left[0], right[0]) + (dot(left[0], right[1]) + dot(left[1], right[0]))
+
+
 def grid_kernel(panels, first, last, listed, group_target, info, *refs):
     refs = list(refs)
     part_refs = [refs.pop(0) for _ in range(panels)]
@@ -132,26 +151,73 @@
     if last:
         row_table, column_table = tables
         facets = cells.shape[0] // TT
-
-        def transform(f, carry):
-            grid = jnp.concatenate(
-                [
-                    jnp.concatenate([cells[f * TT + tu * TS + tv] for tv in range(TS)], axis=1)
-                    for tu in range(TS)
-                ],
-                axis=0,
-            )
-            part = jnp.dot(
-                row_table[...], grid, precision=lax.Precision.HIGHEST, preferred_element_type=F32
-            )
-            both = jnp.concatenate([part[:FG], part[FG:]], axis=1)
-            image = jnp.dot(
-                both, column_table[...], precision=lax.Precision.HIGHEST, preferred_element_type=F32
-            )
-            out_ref[pl.ds(pl.multiple_of(f * FG, FG), FG), :] = image.astype(out_ref.dtype)
-            return carry
-
-        lax.fori_loop(0, facets, transform, 0)
+        grid = jnp.concatenate(
+            [
+                jnp.concatenate(
+                    [
+                        cells[f * TT + tu * TS + tv]
+                        for f in range(facets)
+                        for tv in range(TS)
+                    ],
+                    axis=1,
+                )
+                for tu in range(TS)
+            ],
+            axis=0,
+        )
+        columns = split_dot(halves_of(row_table), two_halves(grid))
+        both = jnp.concatenate(
+            [
+                jnp.concatenate(
+                    [
+                        columns[q * FG : (q + 1) * FG, f * 2 * FG : (f + 1) * 2 * FG]
+                        for q in range(2)
+                    ],
+                    axis=1,
+                )
+                for f in range(facets)
+            ],
+            axis=0,
+        )
+        image = split_dot(two_halves(both), halves_of(column_table))
+        out_ref[...] = image.astype(out_ref.dtype)
+
+
+def deal_kernel(chunks, info, voltage_ref, *refs):
+    outs, wide = refs[:-1], refs[-1]
+    rows, all_channels, width = voltage_ref.shape
+    facets = len(outs) // len(chunks)
+    channels = all_channels // facets
+    lanes = wide.shape[0]
+    for q in range(rows):
+        row = voltage_ref[q].astype(F32)
+        for t in range(lanes):
+            wide[t, q * all_channels : (q + 1) * all_channels, :] = row[:, t * VB : (t + 1) * VB]
+    for c, (begin, end) in enumerate(chunks):
+        for s in range(facets):
+            first = jnp.bitwise_xor(info[0], s) * channels
+            for k in range(begin, end):
+                taken = [
+                    wide[t, pl.ds(first + k, rows, stride=all_channels), :] for t in range(lanes)
+                ]
+                outs[c * facets + s][k - begin] = jnp.concatenate(taken, axis=1).astype(BF16)
+
+
+def deal_channels(voltages, me, facets, chunks):
+    rows, all_channels, width = voltages.shape
+    shapes = [(end - begin, rows, width) for begin, end in chunks for s in range(facets)]
+    return pl.pallas_call(
+        functools.partial(deal_kernel, chunks),
+        grid_spec=pltpu.PrefetchScalarGridSpec(
+            num_scalar_prefetch=1,
+            grid=(1,),
+            in_specs=[whole_block(voltages.shape)],
+            out_specs=[whole_block(shape) for shape in shapes],
+            scratch_shapes=[pltpu.VMEM((width // VB, rows * all_channels, VB), F32)],
+        ),
+        out_shape=[jax.ShapeDtypeStruct(shape, voltages.dtype) for shape in shapes],
+        compiler_params=pltpu.CompilerParams(vmem_limit_bytes=32 << 20),
+    )(me.reshape(1).astype(I32), voltages)
 
 
 def grid_call(info, lists, parts, offsets, before, tables, target_count):
@@ -173,19 +239,23 @@
         out = jax.ShapeDtypeStruct((target_count // TT * FG, 2 * FG), BF16)
     else:
         out = jax.ShapeDtypeStruct(cells, F32)
-    whole = lambda shape: pl.BlockSpec(shape, lambda i, *_: (0,) * len(shape))
     return pl.pallas_call(
         functools.partial(grid_kernel, panels, first, last),
         grid_spec=pltpu.PrefetchScalarGridSpec(
             num_scalar_prefetch=3,
             grid=(1,),
-            in_specs=[whole(x.shape) for x in operands],
-            out_specs=whole(out.shape),
+            in_specs=[whole_block(x.shape) for x in operands],
+            out_specs=whole_block(out.shape),
             scratch_shapes=scratch,
         ),
         out_shape=out,
         compiler_params=pltpu.CompilerParams(vmem_limit_bytes=48 << 20),
     )(listed, group_target, info, *operands)
+
+
+def split_table(table):
+    high = table.astype(ml_dtypes.bfloat16)
+    return high, (table - high.astype(np.float64)).astype(ml_dtypes.bfloat16)
 
 
 def transform_tables():
@@ -198,7 +268,7 @@
     real = np.concatenate([straight, turned], axis=1).reshape(2 * FG, 2 * FG)
     imag = np.concatenate([turned, -straight], axis=1).reshape(2 * FG, 2 * FG)
     column_table = np.concatenate([real, imag], axis=0)
-    return row_table.astype(np.float32), column_table.astype(np.float32)
+    return tuple(np.stack(split_table(t)) for t in (row_table, column_table))
 
 
 def taps_transform(taps_row):
@@ -219,43 +289,40 @@
     blocks = vis_offset.shape[2]
     target_count = facets * TT
 
-    by_channel = jnp.transpose(voltages, (1, 0, 2)).reshape(facets, channels, rows, width)
-    step = channels // CHUNKS
+    ends = [channels * e // 4 for e in CHUNK_ENDS]
+    chunks = list(zip([0] + ends[:-1], ends))
+    pieces = deal_channels(voltages, me, facets, chunks)
     parts = []
-    for c in range(CHUNKS):
-        got = []
-        for s in range(facets):
-            piece = lax.dynamic_slice(
-                by_channel, (jnp.bitwise_xor(me, s), c * step, 0, 0), (1, step, rows, width)
-            ).reshape(step, rows, width)
-            if s:
-                piece = lax.ppermute(piece, "stn", [(i, i ^ s) for i in range(facets)])
-            got.append(piece)
+    for c in range(len(chunks)):
+        got = [pieces[c * facets]]
+        for s in range(facets - 1, 0, -1):
+            pairs = [(i, i ^ s) for i in range(facets)]
+            got.insert(1, lax.ppermute(pieces[c * facets + s], "stn", pairs))
         parts.append(got)
 
-    offsets = vis_offset.reshape(CHUNKS, blocks // CHUNKS, VB)
-    targets = (block_facet.reshape(CHUNKS, -1) * TT + block_tile.reshape(CHUNKS, -1)).astype(I32)
+    per_channel = blocks // channels
+    offsets = vis_offset.reshape(blocks, VB)
+    targets = (block_facet.reshape(blocks) * TT + block_tile.reshape(blocks)).astype(I32)
     tables = tuple(jnp.asarray(t) for t in transform_tables())
     cells = None
-    for c in range(CHUNKS):
-        listed, group_target, turns = group_lists(targets[c], target_count)
+    for (begin, end), got in zip(chunks, parts):
+        held = slice(begin * per_channel, end * per_channel)
+        chunk_targets = targets[held]
+        listed, group_target, turns = group_lists(chunk_targets, target_count)
         info = jnp.stack([turns, me]).astype(I32)
         cells = grid_call(
             info,
             (listed, group_target),
-            parts[c],
-            offsets[c],
+            got,
+            offsets[held],
             cells,
-            tables if c == CHUNKS - 1 else None,
+            tables if end == channels else None,
             target_count,
         )
 
     row_count = FG // chan_count
     pieces = cells.reshape(facets * chan_count, row_count, 2 * FG)
     pieces = lax.all_to_all(pieces, ("stn", "chan"), split_axis=0, concat_axis=0, tiled=True)
-    image = jnp.sum(pieces.astype(F32), axis=0)
-    real, imag = image[:, :FG], image[:, FG:]
-
     channels_all = all_channels * chan_count
     norm_factor = 1.0 / math.sqrt(channels_all * stations * stations * KT * KT / facets)
     u_real, u_imag = taps_transform(kernel_taps[0])
@@ -265,7 +332,11 @@
     u_imag = lax.dynamic_slice_in_dim(u_imag, first_row, row_count)[:, None] * norm_factor
     w_real = u_real * v_real[None, :] - u_imag * v_imag[None, :]
     w_imag = u_real * v_imag[None, :] + u_imag * v_real[None, :]
-    return jnp.stack([real * w_real - imag * w_imag, real * w_imag + imag * w_real], axis=0)
+    of_real = jnp.stack([w_real, w_imag])
+    of_imag = jnp.stack([-w_imag, w_real])
+
+    image = jnp.sum(pieces.astype(F32), axis=0)
+    return image[None, :, :FG] * of_real + image[None, :, FG:] * of_imag
 
 
 def solution(mesh):

time: 74.1 us -> 59 us (0.80)
  Pallas kernels: 26 us -> 18.1 us
  starting transfers between devices: 23.3 us -> 18.6 us
  between operations: 2.92 us -> 1.46 us
  other arithmetic: 7.91 us -> 6.82 us
  waiting for transfers between devices: 11.1 us -> 12 us
  local copies, waits for them, and re-layouts: 2.55 us -> 1.8 us
    ppermute x12 -> x6, starting transfers between devices: 19.7 us -> 10.1 us  [body(): got.insert(1, lax.ppermute(pieces[c * facets + s], 'stn', pairs))]
    pallas_call x4 -> x2, Pallas kernels: 26 us -> 17 us  [grid_call(): pl.pallas_call(functools.partial(grid_kernel, panels, first, last), grid_...]
    all_to_all x1, starting transfers between devices: 3.63 us -> 8.51 us  [body(): lax.all_to_all(pieces, ('stn', 'chan'), split_axis=0, concat_axis=0, tile...]
    reshape x3 -> x0, local copies, waits for them, and re-layouts: 1.91 us -> none  [the longest x1 1.8 us: body(): jnp.transpose(voltages, (1, 0, 2)).reshape(facets, channels, rows, width)]
    reduce_sum x4 -> x2, other arithmetic: 2.64 us -> 1.27 us  [group_lists(): turns = (jnp.sum(group_counts) + UNROLL - 1) // UNROLL]
    reduce_sum x4 -> x1, other arithmetic: 1.03 us -> 2.4 us  [group_lists(): jnp.sum((same & (block_ids[None, :] < block_ids[:, None])).astype(I32), a...]
    unnamed x13 -> x14, local copies, waits for them, and re-layouts: 0.55 us -> 1.72 us
    pallas_call x0 -> x1, Pallas kernels: none -> 1.05 us  [deal_channels(): pl.pallas_call(functools.partial(deal_kernel, chunks), grid_spec=pltpu.Pr...]
  transfers between devices with their start and end apart: 13 -> 7, of which waited for: 2 -> 2; matrix products, arithmetic and copies ran while one was open for 11% -> 11% of each run, Pallas kernels for 21% -> 13%
where the time goes in v2:
time: 59 us; the launch traced here: 58.8 us
  starting transfers between devices  18.6 us (32%)
  Pallas kernels  18.1 us (31%)
  waiting for transfers between devices  12 us (20%)
  other arithmetic  6.82 us (12%)
  local copies, waits for them, and re-layouts  1.8 us (3%)
  between operations  1.46 us (2%)
    pallas_call x2, Pallas kernels, grid_call(): pl.pallas_call(functools.partial(grid_kernel, panels, first, last), grid_...  17 us
    all_to_all x1, waiting for transfers between devices, body(): lax.all_to_all(pieces, ('stn', 'chan'), split_axis=0, concat_axis=0, tile...  10.3 us
    ppermute x6, starting transfers between devices, body(): got.insert(1, lax.ppermute(pieces[c * facets + s], 'stn', pairs))  10.1 us
    all_to_all x1, starting transfers between devices, body(): lax.all_to_all(pieces, ('stn', 'chan'), split_axis=0, concat_axis=0, tile...  8.51 us
    reduce_sum x1, other arithmetic, group_lists(): jnp.sum((same & (block_ids[None, :] < block_ids[:, None])).astype(I32), a...  2.4 us
    unnamed x14, local copies, waits for them, and re-layouts  1.72 us
    ppermute x6, waiting for transfers between devices, body(): got.insert(1, lax.ppermute(pieces[c * facets + s], 'stn', pairs))  1.7 us
    reduce_sum x2, other arithmetic, group_lists(): turns = (jnp.sum(group_counts) + UNROLL - 1) // UNROLL  1.27 us
  transfers between devices with their start and end apart: 7, of which 2 were waited for; matrix products, arithmetic and copies ran while one was open for 11% of the time, Pallas kernels for 13%

profile of v2, /device:TPU:0, one launch (start us, length us, event | category | flops | bytes accessed | tf_op | source)
XLA Modules:
  0.0 58.8 jit_solution(7900823669971476775)
XLA Ops:
  0.0 0.0 copy-start
  0.0 1.2 %copy-done = bf16[64,16,512]{2,1,0:T(8,128)(2,1)S(1)} copy-done((bf16[64,16,512]{2,1,0:T(8,128)(2,1)S(1)}, bf16[64,16,512]{2,1,0:T(8,128)(2,1)}, u32[]{:S(2)}) %copy-start) | copy-done | bytes 1048600
  1.2 0.0 copy-start.5
  1.2 0.0 copy-start.3
  1.2 1.1 %shard_map.73 = (bf16[2,64,512]{2,1,0:T(8,128)(2,1)S(1)}, bf16[2,64,512]{2,1,0:T(8,128)(2,1)S(1)}, bf16[2,64,512]{2,1,0:T(8,128)(2,1)S(1)}, bf16[2,64,512]{2,1,0...) custom-call(s32[1]{0:T(128)} %bitcast.3.info, ...), custom_call_target="tpu_custom_call" | custom-call | tf_op jit(solution)/shard_map/pallas_call | solution.py:209
  2.3 3.1 %collective-permute-start.3 = (bf16[2,64,512]{2,1,0:T(8,128)(2,1)S(1)}, bf16[2,64,512]{2,1,0:T(8,128)(2,1)S(1)}, u32[]{:S(2)}, u32[]{:S(2)}) collective-permute-start(bf16[2,64,512]{2,1,0:T(8,128)(2,1)S(1)} %get-tuple-element.18), channel_id=1, source_target_pairs={{0,8},{8,0},{16,24},{24,16},{1,9},{9,1},{17,25},{25,17},{2,10},{10... | collective-permute-start | bytes 393224 | tf_op jit(solution)/shard_map/ppermute | solution.py:300
  5.4 2.6 %collective-permute-start.4 = (bf16[2,64,512]{2,1,0:T(8,128)(2,1)S(1)}, bf16[2,64,512]{2,1,0:T(8,128)(2,1)S(1)}, u32[]{:S(2)}, u32[]{:S(2)}) collective-permute-start(bf16[2,64,512]{2,1,0:T(8,128)(2,1)S(1)} %get-tuple-element.19), channel_id=1, source_target_pairs={{0,16},{8,24},{16,0},{24,8},{1,17},{9,25},{17,1},{25,9},{2,18},{10... | collective-permute-start | bytes 393224 | tf_op jit(solution)/shard_map/ppermute | solution.py:300
  8.0 0.0 collective-permute-start.5
  8.0 0.9 %collective-permute-start = (bf16[2,64,512]{2,1,0:T(8,128)(2,1)S(1)}, bf16[2,64,512]{2,1,0:T(8,128)(2,1)S(1)}, u32[]{:S(2)}, u32[]{:S(2)}) collective-permute-start(bf16[2,64,512]{2,1,0:T(8,128)(2,1)S(1)} %get-tuple-element.14), channel_id=1, source_target_pairs={{0,8},{8,0},{16,24},{24,16},{1,9},{9,1},{17,25},{25,17},{2,10},{10... | collective-permute-start | bytes 393224 | tf_op jit(solution)/shard_map/ppermute | solution.py:300
  8.9 3.5 %collective-permute-start.1 = (bf16[2,64,512]{2,1,0:T(8,128)(2,1)S(1)}, bf16[2,64,512]{2,1,0:T(8,128)(2,1)S(1)}, u32[]{:S(2)}, u32[]{:S(2)}) collective-permute-start(bf16[2,64,512]{2,1,0:T(8,128)(2,1)S(1)} %get-tuple-element.15), channel_id=1, source_target_pairs={{0,16},{8,24},{16,0},{24,8},{1,17},{9,25},{17,1},{25,9},{2,18},{10... | collective-permute-start | bytes 393224 | tf_op jit(solution)/shard_map/ppermute | solution.py:300
  12.4 0.0 copy-done.5
  12.4 0.0 copy-done.4
  12.4 0.1 convert_reduce_fusion.3
  12.5 0.1 convert_reduce_fusion.4
  12.7 2.4 %convert_reduce_fusion = (s32[1024]{0:T(1024)S(1)}, s32[1024]{0:T(1024)S(1)}) fusion(s32[1024]{0:T(1024)S(1)} %get-tuple-element.36, s32[1024]{0:T(1024)S(1)} %get-tuple-element.35), kind=kLoop, calls=%fused_computation.4 | loop fusion | flops 9435136 | bytes 16384 | tf_op jit(solution)/shard_map/reduce_sum | solution.py:38
  15.1 0.6 %fusion.12 = (s32[]{:T(128)}, s32[64]{0:T(128)S(1)}) fusion(s32[64]{0:T(128)S(1)} %convert_reduce_fusion.3), kind=kLoop, calls=%fused_computation.68 | loop fusion | flops 1087 | bytes 516 | tf_op jit(solution)/shard_map/reduce_sum | solution.py:52
  15.7 0.6 %fusion.13 = (s32[]{:T(128)}, s32[64]{0:T(128)S(1)}) fusion(s32[64]{0:T(128)S(1)} %convert_reduce_fusion.4), kind=kLoop, calls=%fused_computation.69 | loop fusion | flops 1087 | bytes 516 | tf_op jit(solution)/shard_map/reduce_sum | solution.py:52
  16.4 0.1 select_reduce_fusion.4
  16.5 0.1 select_reduce_fusion.5
  16.5 0.1 convert_reduce_fusion.5
  16.6 0.1 select_reduce_fusion.2
  16.8 0.1 convert_reduce_fusion.6
  16.9 1.3 %select_reduce_fusion = (s32[1280]{0:T(1024)S(1)}, s32[1280]{0:T(1024)S(1)}) fusion(s32[1024]{0:T(1024)S(1)} %multiply_add_fusion.1, s32[1024]{0:T(1024)S(1)} %iota_add_fusion, s32[1024]{0:T(1024)S(1)} %multiply_add_fusion.2), kind=kLoop, calls=%fused_computation | loop fusion | flops 7861760 | bytes 22528 | tf_op jit(solution)/shard_map/reduce_sum | solution.py:47
  18.2 0.0 copy-done.3
  18.2 0.0 copy-start.6
  18.2 0.1 slice_bitcast_fusion
  18.3 0.0 collective-permute-done.3.refs_1_
  18.3 0.1 collective-permute-start.2
  18.4 0.5 copy-done.6
  20.1 0.1 pad_add_fusion
  20.2 0.0 collective-permute-done.4.refs_2_
  20.2 0.0 collective-permute-done.5.refs_3_
  20.2 0.0 copy-start.1
  20.2 0.0 copy-start.2
  20.2 7.6 %shard_map.74.refs_5_ = f32[64,32,64]{2,1,0:T(8,128)S(1)} custom-call(s32[1280]{0:T(1024)S(1)} %broadcast_add_fusion.listed, s32[320]{0:T(512)S(1)} %broadcast_add_fusion.2.group_target, s32[2]{0:T(128)S(1)} %get-tuple-element.47.info, bf16[2,64,512]{2,1,0:T(8,128)(2,1)S(1)} %get-tuple-element.17.refs_0_, ...), custom_call_target="tpu_custom_call" | custom-call | tf_op jit(solution)/shard_map/pallas_call | solution.py:242
  27.9 0.0 collective-permute-done.refs_1_
  27.9 1.7 %collective-permute-done.1.refs_2_ = bf16[2,64,512]{2,1,0:T(8,128)(2,1)S(1)} collective-permute-done((bf16[2,64,512]{2,1,0:T(8,128)(2,1)S(1)}, bf16[2,64,512]{2,1,0:T(8,128)(2,1)S(1)}, u32[]{:S(2)}, u32[]{:S(2)}) %collective-permute-start.1) | collective-permute-done | bytes 131104 | tf_op jit(solution)/shard_map/ppermute | solution.py:300
  29.6 0.0 collective-permute-done.2.refs_3_
  29.6 0.0 copy-done.1
  29.6 0.0 copy-done.2
  29.6 9.4 %shard_map.75 = bf16[512,256]{1,0:T(8,128)(2,1)} custom-call(s32[1280]{0:T(1024)S(1)} %broadcast_add_fusion.1.listed, s32[320]{0:T(512)S(1)} %broadcast_add_fusion.3.group_target, s32[2]{0:T(128)S(1)} %get-tuple-element.46.info, bf16[2,64,512]{2,1,0:T(8,128)(2,1)S(1)} %get-tuple-element.13.refs_0_, bf16[2,64,512]{2,1,0:T(8,128)(2,1)S(1)} %collective-permute-done.refs_1_, ...), custom_call_target="tpu_custom_call" | custom-call | tf_op jit(solution)/shard_map/pallas_call | solution.py:242
  39.0 8.5 %all-to-all-start = ((bf16[32,16,256]{2,1,0:T(8,128)(2,1)}), bf16[32,16,256]{2,1,0:T(8,128)(2,1)S(1)}, u32[]{:S(2)}, u32[]{:S(2)}) async-start(bf16[32,16,256]{2,1,0:T(8,128)(2,1)} %bitcast.7), calls=%async_computation | async-start | bytes 524288 | tf_op jit(solution)/shard_map/all_to_all | solution.py:325
  47.5 0.1 multiply_reduce_fusion.2
  47.6 0.1 dynamic-slice_multiply_fusion.1
  47.7 0.1 dynamic-slice_multiply_fusion
  47.8 0.1 fusion.11
  47.8 10.3 %all-to-all-done = bf16[32,16,256]{2,1,0:T(8,128)(2,1)S(1)} async-done(((bf16[32,16,256]{2,1,0:T(8,128)(2,1)}), bf16[32,16,256]{2,1,0:T(8,128)(2,1)S(1)}, u32[]{:S(2)}, u32[]{:S(2)}) %all-to-all-start) | async-done | bytes 262176 | tf_op jit(solution)/shard_map/all_to_all | solution.py:325
  58.2 0.6 %fusion.2 = f32[2,16,128]{2,1,0:T(8,128)} fusion(f32[1,16,128]{2,1,0:T(8,128)S(1)} %get-tuple-element.38, f32[1,16,128]{2,1,0:T(8,128)S(1)} %get-tuple-element.39, f32[1,16,128]{2,1,0:T(8,128)S(1)} %get-tuple-element.37, f32[16,128]{1,0:T(8,128)S(1)} %get-tuple-element.34, f32[16,128]{1,0:T(8,128)S(1)} %get-tuple-element.33), kind=kLoop, calls=%fused_computation.26 | loop fusion | flops 20480 | bytes 57344 | tf_op jit(solution)/shard_map/add | solution.py:339
  (16 shorter events, 0.1 us)
Async XLA Ops:
  0.0 12.4 %copy-start.4 = (s32[1,1,2048]{2,1,0:T(1,128)S(1)}, s32[1,1,2048]{2,1,0:T(1,128)}, u32[]{:S(2)}) copy-start(s32[1,1,2048]{2,1,0:T(1,128)} %param.9) | copy-start | bytes 24580
  0.0 1.2 %copy-start = (bf16[64,16,512]{2,1,0:T(8,128)(2,1)S(1)}, bf16[64,16,512]{2,1,0:T(8,128)(2,1)}, u32[]{:S(2)}) copy-start(bf16[64,16,512]{2,1,0:T(8,128)(2,1)} %voltage_ref.1) | copy-start | bytes 3145732
  1.2 11.1 %copy-start.5 = (s32[1,1,2048,1]{2,3,1,0:T(1,128)S(1)}, s32[1,1,2048,1]{2,3,1,0:T(1,128)}, u32[]{:S(2)}) copy-start(s32[1,1,2048,1]{2,3,1,0:T(1,128)} %param.8) | copy-start | bytes 24580
  1.2 17.0 %copy-start.3 = (s32[1,1,2048,128]{3,2,1,0:T(8,128)S(1)}, s32[1,1,2048,128]{3,2,1,0:T(8,128)}, u32[]{:S(2)}) copy-start(s32[1,1,2048,128]{3,2,1,0:T(8,128)} %param.10) | copy-start | bytes 3145732
  2.3 16.0 %collective-permute-start.3 = (bf16[2,64,512]{2,1,0:T(8,128)(2,1)S(1)}, bf16[2,64,512]{2,1,0:T(8,128)(2,1)S(1)}, u32[]{:S(2)}, u32[]{:S(2)}) collective-permute-start(bf16[2,64,512]{2,1,0:T(8,128)(2,1)S(1)} %get-tuple-element.18), channel_id=1, source_target_pairs={{0,8},{8,0},{16,24},{24,16},{1,9},{9,1},{17,25},{25,17},{2,10},{10... | collective-permute-start | bytes 393224 | tf_op jit(solution)/shard_map/ppermute | solution.py:300
  5.4 14.8 %collective-permute-start.4 = (bf16[2,64,512]{2,1,0:T(8,128)(2,1)S(1)}, bf16[2,64,512]{2,1,0:T(8,128)(2,1)S(1)}, u32[]{:S(2)}, u32[]{:S(2)}) collective-permute-start(bf16[2,64,512]{2,1,0:T(8,128)(2,1)S(1)} %get-tuple-element.19), channel_id=1, source_target_pairs={{0,16},{8,24},{16,0},{24,8},{1,17},{9,25},{17,1},{25,9},{2,18},{10... | collective-permute-start | bytes 393224 | tf_op jit(solution)/shard_map/ppermute | solution.py:300
  8.0 12.2 %collective-permute-start.5 = (bf16[2,64,512]{2,1,0:T(8,128)(2,1)S(1)}, bf16[2,64,512]{2,1,0:T(8,128)(2,1)S(1)}, u32[]{:S(2)}, u32[]{:S(2)}) collective-permute-start(bf16[2,64,512]{2,1,0:T(8,128)(2,1)S(1)} %get-tuple-element.20), channel_id=1, source_target_pairs={{0,24},{8,16},{16,8},{24,0},{1,25},{9,17},{17,9},{25,1},{2,26},{10... | collective-permute-start | bytes 393224 | tf_op jit(solution)/shard_map/ppermute | solution.py:300
  8.0 19.9 %collective-permute-start = (bf16[2,64,512]{2,1,0:T(8,128)(2,1)S(1)}, bf16[2,64,512]{2,1,0:T(8,128)(2,1)S(1)}, u32[]{:S(2)}, u32[]{:S(2)}) collective-permute-start(bf16[2,64,512]{2,1,0:T(8,128)(2,1)S(1)} %get-tuple-element.14), channel_id=1, source_target_pairs={{0,8},{8,0},{16,24},{24,16},{1,9},{9,1},{17,25},{25,17},{2,10},{10... | collective-permute-start | bytes 393224 | tf_op jit(solution)/shard_map/ppermute | solution.py:300
  8.9 20.7 %collective-permute-start.1 = (bf16[2,64,512]{2,1,0:T(8,128)(2,1)S(1)}, bf16[2,64,512]{2,1,0:T(8,128)(2,1)S(1)}, u32[]{:S(2)}, u32[]{:S(2)}) collective-permute-start(bf16[2,64,512]{2,1,0:T(8,128)(2,1)S(1)} %get-tuple-element.15), channel_id=1, source_target_pairs={{0,16},{8,24},{16,0},{24,8},{1,17},{9,25},{17,1},{25,9},{2,18},{10... | collective-permute-start | bytes 393224 | tf_op jit(solution)/shard_map/ppermute | solution.py:300
  18.2 0.7 %copy-start.6 = (bf16[2,8]{1,0:T(2,128)(2,1)S(1)}, bf16[2,8]{1,0:T(2,128)(2,1)}, u32[]{:S(2)}) copy-start(bf16[2,8]{1,0:T(2,128)(2,1)} %param.11) | copy-start | bytes 100
  18.3 11.2 %collective-permute-start.2 = (bf16[2,64,512]{2,1,0:T(8,128)(2,1)S(1)}, bf16[2,64,512]{2,1,0:T(8,128)(2,1)S(1)}, u32[]{:S(2)}, u32[]{:S(2)}) collective-permute-start(bf16[2,64,512]{2,1,0:T(8,128)(2,1)S(1)} %get-tuple-element.16), channel_id=1, source_target_pairs={{0,24},{8,16},{16,8},{24,0},{1,25},{9,17},{17,9},{25,1},{2,26},{10... | collective-permute-start | bytes 393224 | tf_op jit(solution)/shard_map/ppermute | solution.py:300
  20.2 9.3 %copy-start.1 = (bf16[2,512,256]{2,1,0:T(8,128)(2,1)S(1)}, bf16[2,512,256]{2,1,0:T(8,128)(2,1)}, u32[]{:S(2)}) copy-start(bf16[2,512,256]{2,1,0:T(8,128)(2,1)} %constant.110.clone.refs_7_) | copy-start | bytes 1572868
  20.2 9.3 %copy-start.2 = (bf16[2,256,128]{2,1,0:T(8,128)(2,1)S(1)}, bf16[2,256,128]{2,1,0:T(8,128)(2,1)}, u32[]{:S(2)}) copy-start(bf16[2,256,128]{2,1,0:T(8,128)(2,1)} %constant.109.clone.refs_6_) | copy-start | bytes 393220
  39.0 19.1 %all-to-all-start = ((bf16[32,16,256]{2,1,0:T(8,128)(2,1)}), bf16[32,16,256]{2,1,0:T(8,128)(2,1)S(1)}, u32[]{:S(2)}, u32[]{:S(2)}) async-start(bf16[32,16,256]{2,1,0:T(8,128)(2,1)} %bitcast.7), calls=%async_computation | async-start | bytes 524288 | tf_op jit(solution)/shard_map/all_to_all | solution.py:325

commit v3 on v2

--- a/solution.py
+++ b/solution.py
@@ -19,7 +19,7 @@
 FG = TS * TILE
 
 GROUP = 4
-UNROLL = 32
+UNROLL = 48
 CHUNK_ENDS = (2, 4)
 
 F32, BF16, I32 = jnp.float32, jnp.bfloat16, jnp.int32
@@ -30,27 +30,103 @@
     return pl.BlockSpec(shape, lambda i, *_: (0,) * len(shape))
 
 
-def group_lists(targets, target_count):
-    count = targets.shape[0]
-    block_ids = jnp.arange(count, dtype=I32)
-    target_range = jnp.arange(target_count, dtype=I32)
-    same = targets[:, None] == targets[None, :]
-    position = jnp.sum((same & (block_ids[None, :] < block_ids[:, None])).astype(I32), axis=1)
-    member = (targets[:, None] == target_range[None, :]).astype(I32)
-    group_counts = (jnp.sum(member, axis=0) + GROUP - 1) // GROUP
-    below = (target_range[:, None] < target_range[None, :]).astype(I32)
-    first_group = jnp.sum(group_counts[:, None] * below, axis=0)
-    slots = jnp.sum(member * first_group[None, :], axis=1) * GROUP + position
+def list_places(count, target_count):
     most = (count + target_count * (GROUP - 1)) // GROUP
     most = -(-most // UNROLL) * UNROLL
-    places = jnp.arange(most * GROUP, dtype=I32)
-    listed = count + jnp.sum(
-        jnp.where(slots[None, :] == places[:, None], block_ids[None, :] - count, 0), axis=1
+    block_rows = -(-most * GROUP // VB)
+    group_rows = -(-most // VB)
+    return block_rows, group_rows, -(-(block_rows + group_rows + 1) // 8) * 8
+
+
+def late_steps(panels):
+    return range((panels + 1) // 2, panels - 1)
+
+
+def early_blocks(shape, ids, me):
+    panels, rows, halves = shape
+    in_channel = ids - jnp.floor(ids * (1.0 / (panels * rows * halves))) * (panels * rows * halves)
+    station = jnp.floor(in_channel * (1.0 / halves))
+    panel = jnp.floor(station * (1.0 / rows)).astype(I32)
+    step = jnp.bitwise_xor(panel, me)
+    late = late_steps(panels)
+    held = jnp.logical_or(step < late.start, step >= late.stop)
+    own = in_channel - station * halves == (me * rows // VB).astype(F32)
+    return jnp.logical_and(own, held).astype(F32)
+
+
+def list_chunk(first_row, rows, listed_count, choice, shape, target_count, refs):
+    facet_ref, tile_ref, out_ref = refs
+    count = rows * VB
+    block_rows, group_rows, _ = list_places(listed_count, target_count)
+    exact = functools.partial(
+        jnp.dot, precision=lax.Precision.HIGHEST, preferred_element_type=F32
     )
-    groups = jnp.arange(most, dtype=I32)
-    group_target = jnp.sum((groups[:, None] >= first_group[None, :]).astype(I32), axis=1) - 1
-    turns = (jnp.sum(group_counts) + UNROLL - 1) // UNROLL
-    return listed, group_target, turns
+    dot = functools.partial(jnp.dot, preferred_element_type=F32)
+    iota = lambda shape, dim: lax.broadcasted_iota(I32, shape, dim).astype(F32)
+    target_ids = iota((target_count, VB), 0)
+    square = (VB, VB)
+    before = (iota(square, 0) < iota(square, 1)).astype(BF16)
+    ones = jnp.ones(square, BF16)
+    ids = iota((1, VB), 1)
+
+    members, positions = [], []
+    counted = jnp.zeros((target_count, VB), F32)
+    for q in range(rows):
+        r = first_row + q
+        targets = (facet_ref[r : r + 1, :] * TT + tile_ref[r : r + 1, :]).astype(F32)
+        chosen = jnp.ones((1, VB), F32)
+        if choice is not None:
+            early = early_blocks(shape, ids + q * VB, lax.axis_index("stn"))
+            chosen = early if choice else 1.0 - early
+        member = (target_ids == targets).astype(F32) * chosen
+        members.append((member, chosen))
+        positions.append(counted + dot(member.astype(BF16), before))
+        counted = counted + dot(member.astype(BF16), ones)
+    groups = jnp.floor((counted + (GROUP - 1)) * (1.0 / GROUP))
+    lower = iota((target_count, target_count), 0) > iota((target_count, target_count), 1)
+    first_group = exact(lower.astype(F32), groups)
+
+    row_ids = iota((block_rows, VB), 0)
+    lane_ids = iota(square, 0)
+    held = jnp.zeros((3 * block_rows, VB), F32)
+    for q, ((member, chosen), position) in enumerate(zip(members, positions)):
+        slots = jnp.sum(member * (first_group * GROUP + position), axis=0, keepdims=True)
+        slot_rows = jnp.floor(slots * (1.0 / VB))
+        in_row = (row_ids == slot_rows).astype(F32) * chosen
+        in_lane = (lane_ids == slots - slot_rows * VB).astype(BF16)
+        left = jnp.concatenate([in_row, in_row * ids, in_row * q], axis=0).astype(BF16)
+        held = held + lax.dot_general(left, in_lane, LAST_BY_LAST, preferred_element_type=F32)
+    taken, low, high = (held[k * block_rows : (k + 1) * block_rows] for k in range(3))
+    listed = jnp.where(taken > 0.5, low + VB * high, count)
+
+    out_ref[...] = jnp.zeros_like(out_ref)
+    out_ref[0:block_rows, :] = listed.astype(I32)
+    for r in range(group_rows):
+        group_ids = iota((target_count, VB), 1) + r * VB
+        named = jnp.sum((group_ids >= first_group).astype(F32), axis=0, keepdims=True) - 1.0
+        out_ref[block_rows + r : block_rows + r + 1, :] = named.astype(I32)
+    total = jnp.sum(groups, axis=0, keepdims=True)
+    turns = jnp.floor((total + (UNROLL - 1)) * (1.0 / UNROLL))
+    last = block_rows + group_rows
+    out_ref[last : last + 1, :] = turns.astype(I32)
+
+
+def group_lists(facet_ids, tile_ids, wanted, shape, target_count):
+    def kernel(facet_ref, tile_ref, *out_refs):
+        for (first_row, rows, count, choice), out_ref in zip(wanted, out_refs):
+            refs = (facet_ref, tile_ref, out_ref)
+            list_chunk(first_row, rows, count, choice, shape, target_count, refs)
+
+    shapes = [(list_places(count, target_count)[2], VB) for _, _, count, _ in wanted]
+    lists = pl.pallas_call(
+        kernel,
+        grid=(1,),
+        in_specs=[whole_block(facet_ids.shape), whole_block(tile_ids.shape)],
+        out_specs=[whole_block(shape) for shape in shapes],
+        out_shape=[jax.ShapeDtypeStruct(shape, I32) for shape in shapes],
+        compiler_params=pltpu.CompilerParams(vmem_limit_bytes=32 << 20),
+    )(facet_ids, tile_ids)
+    return [x.reshape(-1) for x in lists]
 
 
 def two_halves(x):
@@ -67,18 +143,19 @@
     return dot(left[0], right[0]) + (dot(left[0], right[1]) + dot(left[1], right[0]))
 
 
-def grid_kernel(panels, first, last, listed, group_target, info, *refs):
+def grid_kernel(steps, first, last, places, listed, *refs):
     refs = list(refs)
-    part_refs = [refs.pop(0) for _ in range(panels)]
+    part_refs = [refs.pop(0) for _ in steps]
     offset_ref = refs.pop(0)
     before_ref = None if first else refs.pop(0)
     tables = (refs.pop(0), refs.pop(0)) if last else None
     out_ref, whole, du_rows, dv_rows, re_rows, im_rows = refs[:6]
     cells = refs[6] if last else out_ref
 
-    me = info[1]
+    me = lax.axis_index("stn")
+    targets_at, turns_at = places[0] * VB, (places[0] + places[1]) * VB
     channels, rows, width = part_refs[0].shape
-    stations = panels * rows
+    stations = whole.shape[1]
     samples = width // 2
     halves = stations // VB
     blocks = offset_ref.shape[0]
@@ -96,7 +173,9 @@
     for row_ref in (du_rows, dv_rows, re_rows, im_rows):
         row_ref[blocks:] = no_row
 
-    for step, part in enumerate(part_refs):
+    if len(steps) * rows < stations:
+        whole[...] = jnp.zeros_like(whole)
+    for step, part in zip(steps, part_refs):
         start = pl.multiple_of(jnp.bitwise_xor(me, step) * rows, rows)
         for k in range(channels):
             whole[k, pl.ds(start, rows), :] = part[k]
@@ -143,10 +222,10 @@
                 (g, lax.dot_general(left, right, LAST_BY_LAST, preferred_element_type=F32))
             )
         for g, total in sums:
-            cells[group_target[g]] += total
+            cells[listed[targets_at + g]] += total
         return carry
 
-    lax.fori_loop(0, info[0], turn, 0)
+    lax.fori_loop(0, listed[turns_at], turn, 0)
 
     if last:
         row_table, column_table = tables
@@ -183,46 +262,41 @@
         out_ref[...] = image.astype(out_ref.dtype)
 
 
-def deal_kernel(chunks, info, voltage_ref, *refs):
-    outs, wide = refs[:-1], refs[-1]
+def farthest_first(panels):
+    return [panels - 1] + list(range(1, panels - 1))
+
+
+def deal_kernel(begin, end, facets, voltage_ref, *refs):
+    outs, wide = refs[-facets - 1 : -1], refs[-1]
     rows, all_channels, width = voltage_ref.shape
-    facets = len(outs) // len(chunks)
     channels = all_channels // facets
     lanes = wide.shape[0]
     for q in range(rows):
         row = voltage_ref[q].astype(F32)
         for t in range(lanes):
             wide[t, q * all_channels : (q + 1) * all_channels, :] = row[:, t * VB : (t + 1) * VB]
-    for c, (begin, end) in enumerate(chunks):
-        for s in range(facets):
-            first = jnp.bitwise_xor(info[0], s) * channels
-            for k in range(begin, end):
-                taken = [
-                    wide[t, pl.ds(first + k, rows, stride=all_channels), :] for t in range(lanes)
-                ]
-                outs[c * facets + s][k - begin] = jnp.concatenate(taken, axis=1).astype(BF16)
-
-
-def deal_channels(voltages, me, facets, chunks):
+    for s in range(facets):
+        first = jnp.bitwise_xor(lax.axis_index("stn"), s) * channels
+        for k in range(begin, end):
+            taken = [wide[t, pl.ds(first + k, rows, stride=all_channels), :] for t in range(lanes)]
+            outs[s][k - begin] = jnp.concatenate(taken, axis=1).astype(BF16)
+
+
+def deal_channels(voltages, facets, begin, end, after):
     rows, all_channels, width = voltages.shape
-    shapes = [(end - begin, rows, width) for begin, end in chunks for s in range(facets)]
+    shape = (end - begin, rows, width)
     return pl.pallas_call(
-        functools.partial(deal_kernel, chunks),
-        grid_spec=pltpu.PrefetchScalarGridSpec(
-            num_scalar_prefetch=1,
-            grid=(1,),
-            in_specs=[whole_block(voltages.shape)],
-            out_specs=[whole_block(shape) for shape in shapes],
-            scratch_shapes=[pltpu.VMEM((width // VB, rows * all_channels, VB), F32)],
-        ),
-        out_shape=[jax.ShapeDtypeStruct(shape, voltages.dtype) for shape in shapes],
+        functools.partial(deal_kernel, begin, end, facets),
+        grid=(1,),
+        in_specs=[whole_block(voltages.shape)] + [pl.BlockSpec(memory_space=pl.ANY)] * len(after),
+        out_specs=[whole_block(shape)] * facets,
+        scratch_shapes=[pltpu.VMEM((width // VB, rows * all_channels, VB), F32)],
+        out_shape=[jax.ShapeDtypeStruct(shape, voltages.dtype)] * facets,
         compiler_params=pltpu.CompilerParams(vmem_limit_bytes=32 << 20),
-    )(me.reshape(1).astype(I32), voltages)
-
-
-def grid_call(info, lists, parts, offsets, before, tables, target_count):
-    listed, group_target = lists
-    panels = len(parts)
+    )(voltages, *after)
+
+
+def grid_call(listed, listed_count, stations, steps, parts, offsets, before, tables, target_count):
     channels, rows, width = parts[0].shape
     blocks = offsets.shape[0]
     first, last = before is None, tables is not None
@@ -232,7 +306,7 @@
     if last:
         operands += list(tables)
     cells = (target_count, TILE, 2 * TILE)
-    scratch = [pltpu.VMEM((channels, panels * rows, width), BF16)]
+    scratch = [pltpu.VMEM((channels, stations, width), BF16)]
     scratch += [pltpu.VMEM((blocks + 8, VB), F32)] * 4
     if last:
         scratch.append(pltpu.VMEM(cells, F32))
@@ -240,9 +314,11 @@
     else:
         out = jax.ShapeDtypeStruct(cells, F32)
     return pl.pallas_call(
-        functools.partial(grid_kernel, panels, first, last),
+        functools.partial(
+            grid_kernel, steps, first, last, list_places(listed_count, target_count)
+        ),
         grid_spec=pltpu.PrefetchScalarGridSpec(
-            num_scalar_prefetch=3,
+            num_scalar_prefetch=1,
             grid=(1,),
             in_specs=[whole_block(x.shape) for x in operands],
             out_specs=whole_block(out.shape),
@@ -250,7 +326,7 @@
         ),
         out_shape=out,
         compiler_params=pltpu.CompilerParams(vmem_limit_bytes=48 << 20),
-    )(listed, group_target, info, *operands)
+    )(listed, *operands)
 
 
 def split_table(table):
@@ -282,7 +358,6 @@
 def body(voltages, block_facet, block_tile, vis_offset, kernel_taps):
     facets = lax.axis_size("stn")
     chan_count = lax.axis_size("chan")
-    me = lax.axis_index("stn")
     rows, all_channels, width = voltages.shape
     channels = all_channels // facets
     stations = rows * facets
@@ -291,33 +366,47 @@
 
     ends = [channels * e // 4 for e in CHUNK_ENDS]
     chunks = list(zip([0] + ends[:-1], ends))
-    pieces = deal_channels(voltages, me, facets, chunks)
-    parts = []
-    for c in range(len(chunks)):
-        got = [pieces[c * facets]]
-        for s in range(facets - 1, 0, -1):
-            pairs = [(i, i ^ s) for i in range(facets)]
-            got.insert(1, lax.ppermute(pieces[c * facets + s], "stn", pairs))
-        parts.append(got)
-
     per_channel = blocks // channels
     offsets = vis_offset.reshape(blocks, VB)
-    targets = (block_facet.reshape(blocks) * TT + block_tile.reshape(blocks)).astype(I32)
+    halves = stations // VB
+    early = [0] + [t for t in farthest_first(facets) if t not in late_steps(facets)]
+    every = [0] + farthest_first(facets)
+    wanted, calls = [], []
+    for c, (begin, end) in enumerate(chunks):
+        count = (end - begin) * per_channel
+        where = (begin * per_channel // VB, count // VB)
+        if c:
+            choices = [(count, None, every)]
+        else:
+            soon = (end - begin) * len(early) * rows
+            choices = [(soon, True, early), (count - soon, False, every)]
+        for listed_count, choice, steps in choices:
+            wanted.append(where + (listed_count, choice))
+            calls.append((c, listed_count, steps))
+    lists = group_lists(
+        block_facet.reshape(-1, VB),
+        block_tile.reshape(-1, VB),
+        wanted,
+        (facets, rows, halves),
+        target_count,
+    )
+    parts = []
+    for c, (begin, end) in enumerate(chunks):
+        pieces = deal_channels(voltages, facets, begin, end, lists[:1] if c else [])
+        got = [pieces[0]]
+        for s in farthest_first(facets):
+            pairs = [(i, i ^ s) for i in range(facets)]
+            got.append(lax.ppermute(pieces[s], "stn", pairs))
+        parts.append(got)
     tables = tuple(jnp.asarray(t) for t in transform_tables())
     cells = None
-    for (begin, end), got in zip(chunks, parts):
+    for listed, (c, listed_count, steps) in zip(lists, calls):
+        begin, end = chunks[c]
         held = slice(begin * per_channel, end * per_channel)
-        chunk_targets = targets[held]
-        listed, group_target, turns = group_lists(chunk_targets, target_count)
-        info = jnp.stack([turns, me]).astype(I32)
+        got = [parts[c][every.index(t)] for t in steps]
+        last = tables if end == channels else None
         cells = grid_call(
-            info,
-            (listed, group_target),
-            got,
-            offsets[held],
-            cells,
-            tables if end == channels else None,
-            target_count,
+            listed, listed_count, stations, steps, got, offsets[held], cells, last, target_count
         )
 
     row_count = FG // chan_count

time: 59 us -> 54.6 us (0.925)
  other arithmetic: 6.82 us -> 0.99 us
  Pallas kernels: 18.1 us -> 22 us
  starting transfers between devices: 18.6 us -> 14.9 us
  waiting for transfers between devices: 12 us -> 14.2 us
  between operations: 1.46 us -> 0.12 us
    reduce_sum x11 -> x0, other arithmetic: 5.71 us -> none  [the longest x1 2.4 us: group_lists(): jnp.sum((same & (block_ids[None, :] < block_ids[:, None])).astype(I32), a...]
    pallas_call x3 -> x6, Pallas kernels: 18.1 us -> 22 us  [the longest x3 18.7 us: grid_call(): pl.pallas_call(functools.partial(grid_kernel, steps, first, last, list_pl...]
    all_to_all x1, starting transfers between devices: 8.51 us -> 4.67 us  [body(): lax.all_to_all(pieces, ('stn', 'chan'), split_axis=0, concat_axis=0, tile...]
    ppermute x6, waiting for transfers between devices: 1.7 us -> 3.95 us  [body(): got.append(lax.ppermute(pieces[s], 'stn', pairs))]
    unnamed x14 -> x16, local copies, waits for them, and re-layouts: 1.72 us -> 1.95 us
  transfers between devices with their start and end apart: 7 -> 7, of which waited for: 2 -> 3; matrix products, arithmetic and copies ran while one was open for 11% -> 1% of each run, Pallas kernels for 13% -> 23%
where the time goes in v3:
time: 54.6 us; the launch traced here: 54.3 us
  Pallas kernels  22 us (40%)
  starting transfers between devices  14.9 us (27%)
  waiting for transfers between devices  14.2 us (26%)
  local copies, waits for them, and re-layouts  2.02 us (4%)
  other arithmetic  0.99 us (2%)
    pallas_call x3, Pallas kernels, grid_call(): pl.pallas_call(functools.partial(grid_kernel, steps, first, last, list_pl...  18.7 us
    ppermute x6, starting transfers between devices, body(): got.append(lax.ppermute(pieces[s], 'stn', pairs))  10.3 us
    all_to_all x1, waiting for transfers between devices, body(): lax.all_to_all(pieces, ('stn', 'chan'), split_axis=0, concat_axis=0, tile...  10.3 us
    all_to_all x1, starting transfers between devices, body(): lax.all_to_all(pieces, ('stn', 'chan'), split_axis=0, concat_axis=0, tile...  4.67 us
    ppermute x6, waiting for transfers between devices, body(): got.append(lax.ppermute(pieces[s], 'stn', pairs))  3.95 us
    pallas_call x1, Pallas kernels, group_lists(): pl.pallas_call(kernel, grid=(1,), in_specs=[whole_block(facet_ids.shape),...  2.16 us
    unnamed x16, local copies, waits for them, and re-layouts  1.95 us
    pallas_call x2, Pallas kernels, deal_channels(): pl.pallas_call(functools.partial(deal_kernel, begin, end, facets), grid=(...  1.21 us
  transfers between devices with their start and end apart: 7, of which 3 were waited for; matrix products, arithmetic and copies ran while one was open for 1% of the time, Pallas kernels for 23%

profile of v3, /device:TPU:0, one launch (start us, length us, event | category | flops | bytes accessed | tf_op | source)
XLA Modules:
  0.0 54.3 jit_solution(15885752174636304728)
XLA Ops:
  0.0 0.0 copy-start
  0.0 1.2 %copy-done = bf16[64,16,512]{2,1,0:T(8,128)(2,1)S(1)} copy-done((bf16[64,16,512]{2,1,0:T(8,128)(2,1)S(1)}, bf16[64,16,512]{2,1,0:T(8,128)(2,1)}, u32[]{:S(2)}) %copy-start) | copy-done | bytes 1048600
  1.2 0.0 copy-start.1
  1.2 0.6 %shard_map.75 = (bf16[2,64,512]{2,1,0:T(8,128)(2,1)S(1)}, bf16[2,64,512]{2,1,0:T(8,128)(2,1)S(1)}, bf16[2,64,512]{2,1,0:T(8,128)(2,1)S(1)}, bf16[2,64,512]{2,1,0:T(8,128)(2,1)S(1)}) custom-call(bf16[64,16,512]{2,1,0:T(8,128)(2,1)S(1)} %copy-done), custom_call_target="tpu_custom_call" | custom-call | tf_op jit(solution)/shard_map/pallas_call | solution.py:288
  1.8 0.0 copy-start.4
  1.8 5.1 %collective-permute-start.3 = (bf16[2,64,512]{2,1,0:T(8,128)(2,1)S(1)}, bf16[2,64,512]{2,1,0:T(8,128)(2,1)S(1)}, u32[]{:S(2)}, u32[]{:S(2)}) collective-permute-start(bf16[2,64,512]{2,1,0:T(8,128)(2,1)S(1)} %get-tuple-element.24), channel_id=1, source_target_pairs={{0,24},{8,16},{16,8},{24,0},{1,25},{9,17},{17,9},{25,1},{2,26},{10... | collective-permute-start | bytes 393224 | tf_op jit(solution)/shard_map/ppermute | solution.py:399
  7.0 0.0 collective-permute-start.4
  7.0 0.6 %collective-permute-start.5 = (bf16[2,64,512]{2,1,0:T(8,128)(2,1)S(1)}, bf16[2,64,512]{2,1,0:T(8,128)(2,1)S(1)}, u32[]{:S(2)}, u32[]{:S(2)}) collective-permute-start(bf16[2,64,512]{2,1,0:T(8,128)(2,1)S(1)} %get-tuple-element.26), channel_id=1, source_target_pairs={{0,16},{8,24},{16,0},{24,8},{1,17},{9,25},{17,1},{25,9},{2,18},{10... | collective-permute-start | bytes 393224 | tf_op jit(solution)/shard_map/ppermute | solution.py:399
  7.6 0.0 copy-done.4
  7.6 0.0 copy-start.5
  7.6 0.7 %copy-done.5 = s32[1,1,2048]{2,1,0:T(1,128)S(1)} copy-done((s32[1,1,2048]{2,1,0:T(1,128)S(1)}, s32[1,1,2048]{2,1,0:T(1,128)}, u32[]{:S(2)}) %copy-start.5) | copy-done | bytes 8216
  8.3 0.0 copy-start.6
  8.3 2.2 %shard_map.73 = (s32[8,128]{1,0:T(8,128)S(1)}, s32[16,128]{1,0:T(8,128)S(1)}, s32[16,128]{1,0:T(8,128)S(1)}) custom-call(s32[16,128]{1,0:T(8,128)S(1)} %bitcast.20, s32[16,128]{1,0:T(8,128)S(1)} %bitcast.21), custom_call_target="tpu_custom_call" | custom-call | tf_op jit(solution)/shard_map/pallas_call | solution.py:121
  10.5 0.0 copy-done.1
  10.5 0.6 %shard_map.74 = (bf16[2,64,512]{2,1,0:T(8,128)(2,1)S(1)}, bf16[2,64,512]{2,1,0:T(8,128)(2,1)S(1)}, bf16[2,64,512]{2,1,0:T(8,128)(2,1)S(1)}, bf16[2,64,512]{2,1,0:T(8,128)(2,1)S(1)}) custom-call(bf16[64,16,512]{2,1,0:T(8,128)(2,1)S(1)} %copy-done.1, s32[1024]{0:T(1024)S(1)} %bitcast.16), custom_call_target="tpu_custom_call" | custom-call | tf_op jit(solution)/shard_map/pallas_call | solution.py:288
  11.1 3.8 %collective-permute-start = (bf16[2,64,512]{2,1,0:T(8,128)(2,1)S(1)}, bf16[2,64,512]{2,1,0:T(8,128)(2,1)S(1)}, u32[]{:S(2)}, u32[]{:S(2)}) collective-permute-start(bf16[2,64,512]{2,1,0:T(8,128)(2,1)S(1)} %get-tuple-element.19), channel_id=1, source_target_pairs={{0,24},{8,16},{16,8},{24,0},{1,25},{9,17},{17,9},{25,1},{2,26},{10... | collective-permute-start | bytes 393224 | tf_op jit(solution)/shard_map/ppermute | solution.py:399
  14.9 0.0 collective-permute-start.1
  14.9 0.0 copy-done.6
  14.9 0.1 slice_bitcast_fusion
  15.0 0.0 copy-start.7
  15.0 0.0 collective-permute-done.3.refs_1_
  15.0 0.7 %collective-permute-start.2 = (bf16[2,64,512]{2,1,0:T(8,128)(2,1)S(1)}, bf16[2,64,512]{2,1,0:T(8,128)(2,1)S(1)}, u32[]{:S(2)}, u32[]{:S(2)}) collective-permute-start(bf16[2,64,512]{2,1,0:T(8,128)(2,1)S(1)} %get-tuple-element.21), channel_id=1, source_target_pairs={{0,16},{8,24},{16,0},{24,8},{1,17},{9,25},{17,1},{25,9},{2,18},{10... | collective-permute-start | bytes 393224 | tf_op jit(solution)/shard_map/ppermute | solution.py:399
  15.7 0.0 copy-done.7
  15.7 0.0 collective-permute-done.4.refs_2_
  15.7 4.3 %shard_map.76.refs_5_ = f32[64,32,64]{2,1,0:T(8,128)S(1)} custom-call(s32[1024]{0:T(1024)S(1)} %bitcast.17, bf16[2,64,512]{2,1,0:T(8,128)(2,1)S(1)} %get-tuple-element.23.refs_0_, bf16[2,64,512]{2,1,0:T(8,128)(2,1)S(1)} %collective-permute-done.3.refs_1_, bf16[2,64,512]{2,1,0:T(8,128)(2,1)S(1)} %collective-permute-done.4.refs_2_, ...), custom_call_target="tpu_custom_call" | custom-call | tf_op jit(solution)/shard_map/pallas_call | solution.py:316
  20.0 2.7 %collective-permute-done.5.refs_3_ = bf16[2,64,512]{2,1,0:T(8,128)(2,1)S(1)} collective-permute-done((bf16[2,64,512]{2,1,0:T(8,128)(2,1)S(1)}, bf16[2,64,512]{2,1,0:T(8,128)(2,1)S(1)}, u32[]{:S(2)}, u32[]{:S(2)}) %collective-permute-start.5) | collective-permute-done | bytes 131104 | tf_op jit(solution)/shard_map/ppermute | solution.py:399
  22.7 0.0 copy-start.2
  22.7 0.0 copy-start.3
  22.7 5.3 %shard_map.77.refs_5_ = f32[64,32,64]{2,1,0:T(8,128)S(1)} custom-call(s32[2048]{0:T(1024)S(1)} %bitcast.19, bf16[2,64,512]{2,1,0:T(8,128)(2,1)S(1)} %get-tuple-element.23.refs_0_, bf16[2,64,512]{2,1,0:T(8,128)(2,1)S(1)} %collective-permute-done.3.refs_1_, bf16[2,64,512]{2,1,0:T(8,128)(2,1)S(1)} %collective-permute-done.4.refs_2_, ...), custom_call_target="tpu_custom_call" | custom-call | tf_op jit(solution)/shard_map/pallas_call | solution.py:316
  28.0 0.0 collective-permute-done.refs_1_
  28.0 0.0 collective-permute-done.1.refs_2_
  28.0 1.3 %collective-permute-done.2.refs_3_ = bf16[2,64,512]{2,1,0:T(8,128)(2,1)S(1)} collective-permute-done((bf16[2,64,512]{2,1,0:T(8,128)(2,1)S(1)}, bf16[2,64,512]{2,1,0:T(8,128)(2,1)S(1)}, u32[]{:S(2)}, u32[]{:S(2)}) %collective-permute-start.2) | collective-permute-done | bytes 131104 | tf_op jit(solution)/shard_map/ppermute | solution.py:399
  29.3 0.0 copy-done.2
  29.3 0.0 copy-done.3
  29.3 9.0 %shard_map.78 = bf16[512,256]{1,0:T(8,128)(2,1)} custom-call(s32[2048]{0:T(1024)S(1)} %bitcast.18, bf16[2,64,512]{2,1,0:T(8,128)(2,1)S(1)} %get-tuple-element.18.refs_0_, bf16[2,64,512]{2,1,0:T(8,128)(2,1)S(1)} %collective-permute-done.refs_1_, bf16[2,64,512]{2,1,0:T(8,128)(2,1)S(1)} %collective-permute-done.1.refs_2_, ...), custom_call_target="tpu_custom_call" | custom-call | tf_op jit(solution)/shard_map/pallas_call | solution.py:316
  38.4 4.7 %all-to-all-start = ((bf16[32,16,256]{2,1,0:T(8,128)(2,1)}), bf16[32,16,256]{2,1,0:T(8,128)(2,1)S(1)}, u32[]{:S(2)}, u32[]{:S(2)}) async-start(bf16[32,16,256]{2,1,0:T(8,128)(2,1)} %bitcast.7), calls=%async_computation | async-start | bytes 524288 | tf_op jit(solution)/shard_map/all_to_all | solution.py:414
  43.0 0.1 multiply_reduce_fusion.2
  43.1 0.1 dynamic-slice_multiply_fusion.1
  43.2 0.1 dynamic-slice_multiply_fusion
  43.3 0.1 fusion.9
  43.4 10.3 %all-to-all-done = bf16[32,16,256]{2,1,0:T(8,128)(2,1)S(1)} async-done(((bf16[32,16,256]{2,1,0:T(8,128)(2,1)}), bf16[32,16,256]{2,1,0:T(8,128)(2,1)S(1)}, u32[]{:S(2)}, u32[]{:S(2)}) %all-to-all-start) | async-done | bytes 262176 | tf_op jit(solution)/shard_map/all_to_all | solution.py:414
  53.7 0.6 %fusion = f32[2,16,128]{2,1,0:T(8,128)} fusion(f32[1,16,128]{2,1,0:T(8,128)S(1)} %get-tuple-element.36, f32[1,16,128]{2,1,0:T(8,128)S(1)} %get-tuple-element.37, f32[1,16,128]{2,1,0:T(8,128)S(1)} %get-tuple-element.35, f32[16,128]{1,0:T(8,128)S(1)} %get-tuple-element.34, f32[16,128]{1,0:T(8,128)S(1)} %get-tuple-element.33), kind=kLoop, calls=%fused_computation.4 | loop fusion | flops 20480 | bytes 57344 | tf_op jit(solution)/shard_map/add | solution.py:428
  (5 shorter events, 0.1 us)
Async XLA Ops:
  0.0 1.2 %copy-start = (bf16[64,16,512]{2,1,0:T(8,128)(2,1)S(1)}, bf16[64,16,512]{2,1,0:T(8,128)(2,1)}, u32[]{:S(2)}) copy-start(bf16[64,16,512]{2,1,0:T(8,128)(2,1)} %voltage_ref.3) | copy-start | bytes 3145732
  1.2 9.2 %copy-start.1 = (bf16[64,16,512]{2,1,0:T(8,128)(2,1)S(1)}, bf16[64,16,512]{2,1,0:T(8,128)(2,1)}, u32[]{:S(2)}) copy-start(bf16[64,16,512]{2,1,0:T(8,128)(2,1)} %voltage_ref.3) | copy-start | bytes 3145732
  1.8 5.8 %copy-start.4 = (s32[1,1,2048,1]{2,3,1,0:T(1,128)S(1)}, s32[1,1,2048,1]{2,3,1,0:T(1,128)}, u32[]{:S(2)}) copy-start(s32[1,1,2048,1]{2,3,1,0:T(1,128)} %param.8) | copy-start | bytes 24580
  1.8 13.2 %collective-permute-start.3 = (bf16[2,64,512]{2,1,0:T(8,128)(2,1)S(1)}, bf16[2,64,512]{2,1,0:T(8,128)(2,1)S(1)}, u32[]{:S(2)}, u32[]{:S(2)}) collective-permute-start(bf16[2,64,512]{2,1,0:T(8,128)(2,1)S(1)} %get-tuple-element.24), channel_id=1, source_target_pairs={{0,24},{8,16},{16,8},{24,0},{1,25},{9,17},{17,9},{25,1},{2,26},{10... | collective-permute-start | bytes 393224 | tf_op jit(solution)/shard_map/ppermute | solution.py:399
  7.0 8.8 %collective-permute-start.4 = (bf16[2,64,512]{2,1,0:T(8,128)(2,1)S(1)}, bf16[2,64,512]{2,1,0:T(8,128)(2,1)S(1)}, u32[]{:S(2)}, u32[]{:S(2)}) collective-permute-start(bf16[2,64,512]{2,1,0:T(8,128)(2,1)S(1)} %get-tuple-element.25), channel_id=1, source_target_pairs={{0,8},{8,0},{16,24},{24,16},{1,9},{9,1},{17,25},{25,17},{2,10},{10... | collective-permute-start | bytes 393224 | tf_op jit(solution)/shard_map/ppermute | solution.py:399
  7.0 15.7 %collective-permute-start.5 = (bf16[2,64,512]{2,1,0:T(8,128)(2,1)S(1)}, bf16[2,64,512]{2,1,0:T(8,128)(2,1)S(1)}, u32[]{:S(2)}, u32[]{:S(2)}) collective-permute-start(bf16[2,64,512]{2,1,0:T(8,128)(2,1)S(1)} %get-tuple-element.26), channel_id=1, source_target_pairs={{0,16},{8,24},{16,0},{24,8},{1,17},{9,25},{17,1},{25,9},{2,18},{10... | collective-permute-start | bytes 393224 | tf_op jit(solution)/shard_map/ppermute | solution.py:399
  7.6 0.7 %copy-start.5 = (s32[1,1,2048]{2,1,0:T(1,128)S(1)}, s32[1,1,2048]{2,1,0:T(1,128)}, u32[]{:S(2)}) copy-start(s32[1,1,2048]{2,1,0:T(1,128)} %param.9) | copy-start | bytes 24580
  8.3 6.6 %copy-start.6 = (s32[1,1,2048,128]{3,2,1,0:T(8,128)S(1)}, s32[1,1,2048,128]{3,2,1,0:T(8,128)}, u32[]{:S(2)}) copy-start(s32[1,1,2048,128]{3,2,1,0:T(8,128)} %param.10) | copy-start | bytes 3145732
  11.1 16.9 %collective-permute-start = (bf16[2,64,512]{2,1,0:T(8,128)(2,1)S(1)}, bf16[2,64,512]{2,1,0:T(8,128)(2,1)S(1)}, u32[]{:S(2)}, u32[]{:S(2)}) collective-permute-start(bf16[2,64,512]{2,1,0:T(8,128)(2,1)S(1)} %get-tuple-element.19), channel_id=1, source_target_pairs={{0,24},{8,16},{16,8},{24,0},{1,25},{9,17},{17,9},{25,1},{2,26},{10... | collective-permute-start | bytes 393224 | tf_op jit(solution)/shard_map/ppermute | solution.py:399
  14.9 13.1 %collective-permute-start.1 = (bf16[2,64,512]{2,1,0:T(8,128)(2,1)S(1)}, bf16[2,64,512]{2,1,0:T(8,128)(2,1)S(1)}, u32[]{:S(2)}, u32[]{:S(2)}) collective-permute-start(bf16[2,64,512]{2,1,0:T(8,128)(2,1)S(1)} %get-tuple-element.20), channel_id=1, source_target_pairs={{0,8},{8,0},{16,24},{24,16},{1,9},{9,1},{17,25},{25,17},{2,10},{10... | collective-permute-start | bytes 393224 | tf_op jit(solution)/shard_map/ppermute | solution.py:399
  15.0 0.7 %copy-start.7 = (bf16[2,8]{1,0:T(2,128)(2,1)S(1)}, bf16[2,8]{1,0:T(2,128)(2,1)}, u32[]{:S(2)}) copy-start(bf16[2,8]{1,0:T(2,128)(2,1)} %param.11) | copy-start | bytes 100
  15.0 14.3 %collective-permute-start.2 = (bf16[2,64,512]{2,1,0:T(8,128)(2,1)S(1)}, bf16[2,64,512]{2,1,0:T(8,128)(2,1)S(1)}, u32[]{:S(2)}, u32[]{:S(2)}) collective-permute-start(bf16[2,64,512]{2,1,0:T(8,128)(2,1)S(1)} %get-tuple-element.21), channel_id=1, source_target_pairs={{0,16},{8,24},{16,0},{24,8},{1,17},{9,25},{17,1},{25,9},{2,18},{10... | collective-permute-start | bytes 393224 | tf_op jit(solution)/shard_map/ppermute | solution.py:399
  22.7 6.6 %copy-start.2 = (bf16[2,512,256]{2,1,0:T(8,128)(2,1)S(1)}, bf16[2,512,256]{2,1,0:T(8,128)(2,1)}, u32[]{:S(2)}) copy-start(bf16[2,512,256]{2,1,0:T(8,128)(2,1)} %constant.36.clone.refs_7_) | copy-start | bytes 1572868
  22.7 6.6 %copy-start.3 = (bf16[2,256,128]{2,1,0:T(8,128)(2,1)S(1)}, bf16[2,256,128]{2,1,0:T(8,128)(2,1)}, u32[]{:S(2)}) copy-start(bf16[2,256,128]{2,1,0:T(8,128)(2,1)} %constant.35.clone.refs_6_) | copy-start | bytes 393220
  38.4 15.3 %all-to-all-start = ((bf16[32,16,256]{2,1,0:T(8,128)(2,1)}), bf16[32,16,256]{2,1,0:T(8,128)(2,1)S(1)}, u32[]{:S(2)}, u32[]{:S(2)}) async-start(bf16[32,16,256]{2,1,0:T(8,128)(2,1)} %bitcast.7), calls=%async_computation | async-start | bytes 524288 | tf_op jit(solution)/shard_map/all_to_all | solution.py:414

commit v4 on v3

--- a/solution.py
+++ b/solution.py
@@ -143,8 +143,11 @@
     return dot(left[0], right[0]) + (dot(left[0], right[1]) + dot(left[1], right[0]))
 
 
-def grid_kernel(steps, first, last, places, listed, *refs):
+def grid_kernel(steps, first, last, places, list_ref, *refs):
     refs = list(refs)
+    listed, list_done = refs.pop(-2), refs.pop(-1)
+    list_copy = pltpu.make_async_copy(list_ref, listed, list_done)
+    list_copy.start()
     part_refs = [refs.pop(0) for _ in steps]
     offset_ref = refs.pop(0)
     before_ref = None if first else refs.pop(0)
@@ -210,6 +213,8 @@
         along_v = [jnp.where(ids == dv_n, re_n, none) for ids in cell_ids]
         along_v += [jnp.where(ids == dv_n, im_n, none) for ids in cell_ids]
         return jnp.concatenate(along_u, axis=0), jnp.concatenate(along_v, axis=0)
+
+    list_copy.wait()
 
     def turn(index, carry):
         sums = []
@@ -262,8 +267,10 @@
         out_ref[...] = image.astype(out_ref.dtype)
 
 
-def farthest_first(panels):
-    return [panels - 1] + list(range(1, panels - 1))
+def step_order(panels, chunk):
+    late = late_steps(panels)
+    far, near = [panels - 1][: panels - 1], [s for s in range(1, panels - 1) if s not in late]
+    return (near + far if chunk else far + near) + list(late)
 
 
 def deal_kernel(begin, end, facets, voltage_ref, *refs):
@@ -313,17 +320,15 @@
         out = jax.ShapeDtypeStruct((target_count // TT * FG, 2 * FG), BF16)
     else:
         out = jax.ShapeDtypeStruct(cells, F32)
+    scratch += [pltpu.SMEM(listed.shape, I32), pltpu.SemaphoreType.DMA]
     return pl.pallas_call(
         functools.partial(
             grid_kernel, steps, first, last, list_places(listed_count, target_count)
         ),
-        grid_spec=pltpu.PrefetchScalarGridSpec(
-            num_scalar_prefetch=1,
-            grid=(1,),
-            in_specs=[whole_block(x.shape) for x in operands],
-            out_specs=whole_block(out.shape),
-            scratch_shapes=scratch,
-        ),
+        grid=(1,),
+        in_specs=[pl.BlockSpec(memory_space=pl.ANY)] + [whole_block(x.shape) for x in operands],
+        out_specs=whole_block(out.shape),
+        scratch_shapes=scratch,
         out_shape=out,
         compiler_params=pltpu.CompilerParams(vmem_limit_bytes=48 << 20),
     )(listed, *operands)
@@ -369,20 +374,17 @@
     per_channel = blocks // channels
     offsets = vis_offset.reshape(blocks, VB)
     halves = stations // VB
-    early = [0] + [t for t in farthest_first(facets) if t not in late_steps(facets)]
-    every = [0] + farthest_first(facets)
+    late = late_steps(facets)
     wanted, calls = [], []
     for c, (begin, end) in enumerate(chunks):
         count = (end - begin) * per_channel
         where = (begin * per_channel // VB, count // VB)
-        if c:
-            choices = [(count, None, every)]
-        else:
-            soon = (end - begin) * len(early) * rows
-            choices = [(soon, True, early), (count - soon, False, every)]
-        for listed_count, choice, steps in choices:
+        steps = [0] + step_order(facets, c)
+        early = [t for t in steps if t not in late]
+        soon = (end - begin) * len(early) * rows
+        for listed_count, choice, taken in ((soon, True, early), (count - soon, False, steps)):
             wanted.append(where + (listed_count, choice))
-            calls.append((c, listed_count, steps))
+            calls.append((c, listed_count, taken))
     lists = group_lists(
         block_facet.reshape(-1, VB),
         block_tile.reshape(-1, VB),
@@ -393,18 +395,18 @@
     parts = []
     for c, (begin, end) in enumerate(chunks):
         pieces = deal_channels(voltages, facets, begin, end, lists[:1] if c else [])
-        got = [pieces[0]]
-        for s in farthest_first(facets):
+        got = {0: pieces[0]}
+        for s in step_order(facets, c):
             pairs = [(i, i ^ s) for i in range(facets)]
-            got.append(lax.ppermute(pieces[s], "stn", pairs))
+            got[s] = lax.ppermute(pieces[s], "stn", pairs)
         parts.append(got)
     tables = tuple(jnp.asarray(t) for t in transform_tables())
     cells = None
-    for listed, (c, listed_count, steps) in zip(lists, calls):
+    for call, (listed, (c, listed_count, steps)) in enumerate(zip(lists, calls)):
         begin, end = chunks[c]
         held = slice(begin * per_channel, end * per_channel)
-        got = [parts[c][every.index(t)] for t in steps]
-        last = tables if end == channels else None
+        got = [parts[c][t] for t in steps]
+        last = tables if call == len(calls) - 1 else None
         cells = grid_call(
             listed, listed_count, stations, steps, got, offsets[held], cells, last, target_count
         )

time: 54.6 us -> 53 us (0.971)
  waiting for transfers between devices: 14.2 us -> 11.5 us
  starting transfers between devices: 14.9 us -> 15.8 us
    ppermute x6, waiting for transfers between devices: 3.95 us -> 1.2 us  [body(): got[s] = lax.ppermute(pieces[s], 'stn', pairs)]
    all_to_all x1, starting transfers between devices: 4.67 us -> 5.58 us  [body(): lax.all_to_all(pieces, ('stn', 'chan'), split_axis=0, concat_axis=0, tile...]
    pallas_call x3 -> x4, Pallas kernels: 18.7 us -> 18.6 us  [grid_call(): pl.pallas_call(functools.partial(grid_kernel, steps, first, last, list_pl...]
  transfers between devices with their start and end apart: 7 -> 7, of which waited for: 3 -> 3; matrix products, arithmetic and copies ran while one was open for 1% -> 1% of each run, Pallas kernels for 23% -> 29%
where the time goes in v4:
time: 53 us; the launch traced here: 52.7 us
  Pallas kernels  22.2 us (42%)
  starting transfers between devices  15.8 us (30%)
  waiting for transfers between devices  11.5 us (22%)
  local copies, waits for them, and re-layouts  2.11 us (4%)
  other arithmetic  0.99 us (2%)
    pallas_call x4, Pallas kernels, grid_call(): pl.pallas_call(functools.partial(grid_kernel, steps, first, last, list_pl...  18.6 us
    all_to_all x1, waiting for transfers between devices, body(): lax.all_to_all(pieces, ('stn', 'chan'), split_axis=0, concat_axis=0, tile...  10.3 us
    ppermute x6, starting transfers between devices, body(): got[s] = lax.ppermute(pieces[s], 'stn', pairs)  10.2 us
    all_to_all x1, starting transfers between devices, body(): lax.all_to_all(pieces, ('stn', 'chan'), split_axis=0, concat_axis=0, tile...  5.58 us
    pallas_call x1, Pallas kernels, group_lists(): pl.pallas_call(kernel, grid=(1,), in_specs=[whole_block(facet_ids.shape),...  2.34 us
    unnamed x16, local copies, waits for them, and re-layouts  2.03 us
    pallas_call x2, Pallas kernels, deal_channels(): pl.pallas_call(functools.partial(deal_kernel, begin, end, facets), grid=(...  1.23 us
    ppermute x6, waiting for transfers between devices, body(): got[s] = lax.ppermute(pieces[s], 'stn', pairs)  1.2 us
  transfers between devices with their start and end apart: 7, of which 3 were waited for; matrix products, arithmetic and copies ran while one was open for 1% of the time, Pallas kernels for 29%

profile of v4, /device:TPU:0, one launch (start us, length us, event | category | flops | bytes accessed | tf_op | source)
XLA Modules:
  0.0 52.7 jit_solution(184791222293428329)
XLA Ops:
  0.0 0.0 copy-start
  0.0 1.2 %copy-done = bf16[64,16,512]{2,1,0:T(8,128)(2,1)S(1)} copy-done((bf16[64,16,512]{2,1,0:T(8,128)(2,1)S(1)}, bf16[64,16,512]{2,1,0:T(8,128)(2,1)}, u32[]{:S(2)}) %copy-start) | copy-done | bytes 1048600
  1.2 0.0 copy-start.1
  1.2 0.6 %shard_map.75 = (bf16[2,64,512]{2,1,0:T(8,128)(2,1)S(1)}, bf16[2,64,512]{2,1,0:T(8,128)(2,1)S(1)}, bf16[2,64,512]{2,1,0:T(8,128)(2,1)S(1)}, bf16[2,64,512]{2,1,0:T(8,128)(2,1)S(1)}) custom-call(bf16[64,16,512]{2,1,0:T(8,128)(2,1)S(1)} %copy-done), custom_call_target="tpu_custom_call" | custom-call | tf_op jit(solution)/shard_map/pallas_call | solution.py:295
  1.8 0.0 copy-start.4
  1.8 5.1 %collective-permute-start.3 = (bf16[2,64,512]{2,1,0:T(8,128)(2,1)S(1)}, bf16[2,64,512]{2,1,0:T(8,128)(2,1)S(1)}, u32[]{:S(2)}, u32[]{:S(2)}) collective-permute-start(bf16[2,64,512]{2,1,0:T(8,128)(2,1)S(1)} %get-tuple-element.26), channel_id=1, source_target_pairs={{0,24},{8,16},{16,8},{24,0},{1,25},{9,17},{17,9},{25,1},{2,26},{10... | collective-permute-start | bytes 393224 | tf_op jit(solution)/shard_map/ppermute | solution.py:401
  7.0 0.0 collective-permute-start.4
  7.0 0.6 %collective-permute-start.5 = (bf16[2,64,512]{2,1,0:T(8,128)(2,1)S(1)}, bf16[2,64,512]{2,1,0:T(8,128)(2,1)S(1)}, u32[]{:S(2)}, u32[]{:S(2)}) collective-permute-start(bf16[2,64,512]{2,1,0:T(8,128)(2,1)S(1)} %get-tuple-element.28), channel_id=1, source_target_pairs={{0,16},{8,24},{16,0},{24,8},{1,17},{9,25},{17,1},{25,9},{2,18},{10... | collective-permute-start | bytes 393224 | tf_op jit(solution)/shard_map/ppermute | solution.py:401
  7.6 0.0 copy-done.4
  7.6 0.0 copy-start.5
  7.6 0.7 %copy-done.5 = s32[1,1,2048]{2,1,0:T(1,128)S(1)} copy-done((s32[1,1,2048]{2,1,0:T(1,128)S(1)}, s32[1,1,2048]{2,1,0:T(1,128)}, u32[]{:S(2)}) %copy-start.5) | copy-done | bytes 8216
  8.3 0.0 copy-start.6
  8.3 2.3 %shard_map.73 = (s32[8,128]{1,0:T(8,128)S(1)}, s32[16,128]{1,0:T(8,128)S(1)}, s32[8,128]{1,0:T(8,128)S(1)}, s32[16,128]{1,0:T(8,128)S(1)}) custom-call(s32[16,128]{1,0:T(8,128)S(1)} %bitcast.21, s32[16,128]{1,0:T(8,128)S(1)} %bitcast.22), custom_call_target="tpu_custom_call" | custom-call | tf_op jit(solution)/shard_map/pallas_call | solution.py:121
  10.7 0.0 copy-done.1
  10.7 0.6 %shard_map.74 = (bf16[2,64,512]{2,1,0:T(8,128)(2,1)S(1)}, bf16[2,64,512]{2,1,0:T(8,128)(2,1)S(1)}, bf16[2,64,512]{2,1,0:T(8,128)(2,1)S(1)}, bf16[2,64,512]{2,1,0:T(8,128)(2,1)S(1)}) custom-call(bf16[64,16,512]{2,1,0:T(8,128)(2,1)S(1)} %copy-done.1, s32[1024]{0:T(1024)S(1)} %bitcast.17), custom_call_target="tpu_custom_call" | custom-call | tf_op jit(solution)/shard_map/pallas_call | solution.py:295
  11.3 1.5 %collective-permute-start = (bf16[2,64,512]{2,1,0:T(8,128)(2,1)S(1)}, bf16[2,64,512]{2,1,0:T(8,128)(2,1)S(1)}, u32[]{:S(2)}, u32[]{:S(2)}) collective-permute-start(bf16[2,64,512]{2,1,0:T(8,128)(2,1)S(1)} %get-tuple-element.20), channel_id=1, source_target_pairs={{0,8},{8,0},{16,24},{24,16},{1,9},{9,1},{17,25},{25,17},{2,10},{10... | collective-permute-start | bytes 393224 | tf_op jit(solution)/shard_map/ppermute | solution.py:401
  12.7 2.4 %collective-permute-start.1 = (bf16[2,64,512]{2,1,0:T(8,128)(2,1)S(1)}, bf16[2,64,512]{2,1,0:T(8,128)(2,1)S(1)}, u32[]{:S(2)}, u32[]{:S(2)}) collective-permute-start(bf16[2,64,512]{2,1,0:T(8,128)(2,1)S(1)} %get-tuple-element.21), channel_id=1, source_target_pairs={{0,24},{8,16},{16,8},{24,0},{1,25},{9,17},{17,9},{25,1},{2,26},{10... | collective-permute-start | bytes 393224 | tf_op jit(solution)/shard_map/ppermute | solution.py:401
  15.2 0.0 copy-done.6
  15.2 0.1 slice_bitcast_fusion
  15.3 0.0 copy-start.7
  15.3 0.0 collective-permute-done.3.refs_1_
  15.3 0.6 %collective-permute-start.2 = (bf16[2,64,512]{2,1,0:T(8,128)(2,1)S(1)}, bf16[2,64,512]{2,1,0:T(8,128)(2,1)S(1)}, u32[]{:S(2)}, u32[]{:S(2)}) collective-permute-start(bf16[2,64,512]{2,1,0:T(8,128)(2,1)S(1)} %get-tuple-element.22), channel_id=1, source_target_pairs={{0,16},{8,24},{16,0},{24,8},{1,17},{9,25},{17,1},{25,9},{2,18},{10... | collective-permute-start | bytes 393224 | tf_op jit(solution)/shard_map/ppermute | solution.py:401
  15.8 0.1 copy-done.7
  15.9 0.0 collective-permute-done.4.refs_2_
  15.9 3.7 %shard_map.76.refs_5_ = f32[64,32,64]{2,1,0:T(8,128)S(1)} custom-call(s32[1024]{0:T(1024)S(1)} %bitcast.18, bf16[2,64,512]{2,1,0:T(8,128)(2,1)S(1)} %get-tuple-element.25.refs_0_, bf16[2,64,512]{2,1,0:T(8,128)(2,1)S(1)} %collective-permute-done.3.refs_1_, bf16[2,64,512]{2,1,0:T(8,128)(2,1)S(1)} %collective-permute-done.4.refs_2_, ...), custom_call_target="tpu_custom_call" | custom-call | tf_op jit(solution)/shard_map/pallas_call | solution.py:324
  19.6 0.2 collective-permute-done.5.refs_3_
  19.8 4.7 %shard_map.77.refs_4_ = f32[64,32,64]{2,1,0:T(8,128)S(1)} custom-call(s32[2048]{0:T(1024)S(1)} %bitcast.20, bf16[2,64,512]{2,1,0:T(8,128)(2,1)S(1)} %get-tuple-element.25.refs_0_, bf16[2,64,512]{2,1,0:T(8,128)(2,1)S(1)} %collective-permute-done.3.refs_1_, bf16[2,64,512]{2,1,0:T(8,128)(2,1)S(1)} %collective-permute-done.4.refs_2_, ...), custom_call_target="tpu_custom_call" | custom-call | tf_op jit(solution)/shard_map/pallas_call | solution.py:324
  24.5 0.0 collective-permute-done.refs_1_
  24.5 0.0 collective-permute-done.1.refs_2_
  24.6 0.0 copy-start.2
  24.6 0.0 copy-start.3
  24.6 3.7 %shard_map.78.refs_5_ = f32[64,32,64]{2,1,0:T(8,128)S(1)} custom-call(s32[1024]{0:T(1024)S(1)} %bitcast.23, bf16[2,64,512]{2,1,0:T(8,128)(2,1)S(1)} %get-tuple-element.19.refs_0_, bf16[2,64,512]{2,1,0:T(8,128)(2,1)S(1)} %collective-permute-done.refs_1_, bf16[2,64,512]{2,1,0:T(8,128)(2,1)S(1)} %collective-permute-done.1.refs_2_, ...), custom_call_target="tpu_custom_call" | custom-call | tf_op jit(solution)/shard_map/pallas_call | solution.py:324
  28.3 1.0 %collective-permute-done.2.refs_3_ = bf16[2,64,512]{2,1,0:T(8,128)(2,1)S(1)} collective-permute-done((bf16[2,64,512]{2,1,0:T(8,128)(2,1)S(1)}, bf16[2,64,512]{2,1,0:T(8,128)(2,1)S(1)}, u32[]{:S(2)}, u32[]{:S(2)}) %collective-permute-start.2) | collective-permute-done | bytes 131104 | tf_op jit(solution)/shard_map/ppermute | solution.py:401
  29.3 0.0 copy-done.2
  29.3 0.0 copy-done.3
  29.3 6.6 %shard_map.79 = bf16[512,256]{1,0:T(8,128)(2,1)} custom-call(s32[2048]{0:T(1024)S(1)} %bitcast.19, bf16[2,64,512]{2,1,0:T(8,128)(2,1)S(1)} %get-tuple-element.19.refs_0_, bf16[2,64,512]{2,1,0:T(8,128)(2,1)S(1)} %collective-permute-done.refs_1_, bf16[2,64,512]{2,1,0:T(8,128)(2,1)S(1)} %collective-permute-done.1.refs_2_, ...), custom_call_target="tpu_custom_call" | custom-call | tf_op jit(solution)/shard_map/pallas_call | solution.py:324
  35.8 5.6 %all-to-all-start = ((bf16[32,16,256]{2,1,0:T(8,128)(2,1)}), bf16[32,16,256]{2,1,0:T(8,128)(2,1)S(1)}, u32[]{:S(2)}, u32[]{:S(2)}) async-start(bf16[32,16,256]{2,1,0:T(8,128)(2,1)} %bitcast.8), calls=%async_computation | async-start | bytes 524288 | tf_op jit(solution)/shard_map/all_to_all | solution.py:416
  41.4 0.1 multiply_reduce_fusion.2
  41.5 0.1 dynamic-slice_multiply_fusion.1
  41.6 0.1 dynamic-slice_multiply_fusion
  41.7 0.1 fusion.9
  41.8 10.3 %all-to-all-done = bf16[32,16,256]{2,1,0:T(8,128)(2,1)S(1)} async-done(((bf16[32,16,256]{2,1,0:T(8,128)(2,1)}), bf16[32,16,256]{2,1,0:T(8,128)(2,1)S(1)}, u32[]{:S(2)}, u32[]{:S(2)}) %all-to-all-start) | async-done | bytes 262176 | tf_op jit(solution)/shard_map/all_to_all | solution.py:416
  52.1 0.6 %fusion = f32[2,16,128]{2,1,0:T(8,128)} fusion(f32[1,16,128]{2,1,0:T(8,128)S(1)} %get-tuple-element.38, f32[1,16,128]{2,1,0:T(8,128)S(1)} %get-tuple-element.39, f32[1,16,128]{2,1,0:T(8,128)S(1)} %get-tuple-element.37, f32[16,128]{1,0:T(8,128)S(1)} %get-tuple-element.36, f32[16,128]{1,0:T(8,128)S(1)} %get-tuple-element.35), kind=kLoop, calls=%fused_computation.4 | loop fusion | flops 20480 | bytes 57344 | tf_op jit(solution)/shard_map/add | solution.py:430
  (5 shorter events, 0.1 us)
Async XLA Ops:
  0.0 1.2 %copy-start = (bf16[64,16,512]{2,1,0:T(8,128)(2,1)S(1)}, bf16[64,16,512]{2,1,0:T(8,128)(2,1)}, u32[]{:S(2)}) copy-start(bf16[64,16,512]{2,1,0:T(8,128)(2,1)} %voltage_ref.3) | copy-start | bytes 3145732
  1.2 9.4 %copy-start.1 = (bf16[64,16,512]{2,1,0:T(8,128)(2,1)S(1)}, bf16[64,16,512]{2,1,0:T(8,128)(2,1)}, u32[]{:S(2)}) copy-start(bf16[64,16,512]{2,1,0:T(8,128)(2,1)} %voltage_ref.3) | copy-start | bytes 3145732
  1.8 5.8 %copy-start.4 = (s32[1,1,2048,1]{2,3,1,0:T(1,128)S(1)}, s32[1,1,2048,1]{2,3,1,0:T(1,128)}, u32[]{:S(2)}) copy-start(s32[1,1,2048,1]{2,3,1,0:T(1,128)} %param.8) | copy-start | bytes 24580
  1.8 13.4 %collective-permute-start.3 = (bf16[2,64,512]{2,1,0:T(8,128)(2,1)S(1)}, bf16[2,64,512]{2,1,0:T(8,128)(2,1)S(1)}, u32[]{:S(2)}, u32[]{:S(2)}) collective-permute-start(bf16[2,64,512]{2,1,0:T(8,128)(2,1)S(1)} %get-tuple-element.26), channel_id=1, source_target_pairs={{0,24},{8,16},{16,8},{24,0},{1,25},{9,17},{17,9},{25,1},{2,26},{10... | collective-permute-start | bytes 393224 | tf_op jit(solution)/shard_map/ppermute | solution.py:401
  7.0 9.0 %collective-permute-start.4 = (bf16[2,64,512]{2,1,0:T(8,128)(2,1)S(1)}, bf16[2,64,512]{2,1,0:T(8,128)(2,1)S(1)}, u32[]{:S(2)}, u32[]{:S(2)}) collective-permute-start(bf16[2,64,512]{2,1,0:T(8,128)(2,1)S(1)} %get-tuple-element.27), channel_id=1, source_target_pairs={{0,8},{8,0},{16,24},{24,16},{1,9},{9,1},{17,25},{25,17},{2,10},{10... | collective-permute-start | bytes 393224 | tf_op jit(solution)/shard_map/ppermute | solution.py:401
  7.0 12.9 %collective-permute-start.5 = (bf16[2,64,512]{2,1,0:T(8,128)(2,1)S(1)}, bf16[2,64,512]{2,1,0:T(8,128)(2,1)S(1)}, u32[]{:S(2)}, u32[]{:S(2)}) collective-permute-start(bf16[2,64,512]{2,1,0:T(8,128)(2,1)S(1)} %get-tuple-element.28), channel_id=1, source_target_pairs={{0,16},{8,24},{16,0},{24,8},{1,17},{9,25},{17,1},{25,9},{2,18},{10... | collective-permute-start | bytes 393224 | tf_op jit(solution)/shard_map/ppermute | solution.py:401
  7.6 0.7 %copy-start.5 = (s32[1,1,2048]{2,1,0:T(1,128)S(1)}, s32[1,1,2048]{2,1,0:T(1,128)}, u32[]{:S(2)}) copy-start(s32[1,1,2048]{2,1,0:T(1,128)} %param.9) | copy-start | bytes 24580
  8.3 6.9 %copy-start.6 = (s32[1,1,2048,128]{3,2,1,0:T(8,128)S(1)}, s32[1,1,2048,128]{3,2,1,0:T(8,128)}, u32[]{:S(2)}) copy-start(s32[1,1,2048,128]{3,2,1,0:T(8,128)} %param.10) | copy-start | bytes 3145732
  11.3 13.3 %collective-permute-start = (bf16[2,64,512]{2,1,0:T(8,128)(2,1)S(1)}, bf16[2,64,512]{2,1,0:T(8,128)(2,1)S(1)}, u32[]{:S(2)}, u32[]{:S(2)}) collective-permute-start(bf16[2,64,512]{2,1,0:T(8,128)(2,1)S(1)} %get-tuple-element.20), channel_id=1, source_target_pairs={{0,8},{8,0},{16,24},{24,16},{1,9},{9,1},{17,25},{25,17},{2,10},{10... | collective-permute-start | bytes 393224 | tf_op jit(solution)/shard_map/ppermute | solution.py:401
  12.7 11.8 %collective-permute-start.1 = (bf16[2,64,512]{2,1,0:T(8,128)(2,1)S(1)}, bf16[2,64,512]{2,1,0:T(8,128)(2,1)S(1)}, u32[]{:S(2)}, u32[]{:S(2)}) collective-permute-start(bf16[2,64,512]{2,1,0:T(8,128)(2,1)S(1)} %get-tuple-element.21), channel_id=1, source_target_pairs={{0,24},{8,16},{16,8},{24,0},{1,25},{9,17},{17,9},{25,1},{2,26},{10... | collective-permute-start | bytes 393224 | tf_op jit(solution)/shard_map/ppermute | solution.py:401
  15.3 0.7 %copy-start.7 = (bf16[2,8]{1,0:T(2,128)(2,1)S(1)}, bf16[2,8]{1,0:T(2,128)(2,1)}, u32[]{:S(2)}) copy-start(bf16[2,8]{1,0:T(2,128)(2,1)} %param.11) | copy-start | bytes 100
  15.3 14.0 %collective-permute-start.2 = (bf16[2,64,512]{2,1,0:T(8,128)(2,1)S(1)}, bf16[2,64,512]{2,1,0:T(8,128)(2,1)S(1)}, u32[]{:S(2)}, u32[]{:S(2)}) collective-permute-start(bf16[2,64,512]{2,1,0:T(8,128)(2,1)S(1)} %get-tuple-element.22), channel_id=1, source_target_pairs={{0,16},{8,24},{16,0},{24,8},{1,17},{9,25},{17,1},{25,9},{2,18},{10... | collective-permute-start | bytes 393224 | tf_op jit(solution)/shard_map/ppermute | solution.py:401
  24.6 4.7 %copy-start.2 = (bf16[2,512,256]{2,1,0:T(8,128)(2,1)S(1)}, bf16[2,512,256]{2,1,0:T(8,128)(2,1)}, u32[]{:S(2)}) copy-start(bf16[2,512,256]{2,1,0:T(8,128)(2,1)} %constant.36.clone.refs_7_) | copy-start | bytes 1572868
  24.6 4.7 %copy-start.3 = (bf16[2,256,128]{2,1,0:T(8,128)(2,1)S(1)}, bf16[2,256,128]{2,1,0:T(8,128)(2,1)}, u32[]{:S(2)}) copy-start(bf16[2,256,128]{2,1,0:T(8,128)(2,1)} %constant.35.clone.refs_6_) | copy-start | bytes 393220
  35.8 16.2 %all-to-all-start = ((bf16[32,16,256]{2,1,0:T(8,128)(2,1)}), bf16[32,16,256]{2,1,0:T(8,128)(2,1)S(1)}, u32[]{:S(2)}, u32[]{:S(2)}) async-start(bf16[32,16,256]{2,1,0:T(8,128)(2,1)} %bitcast.8), calls=%async_computation | async-start | bytes 524288 | tf_op jit(solution)/shard_map/all_to_all | solution.py:416

commit v5 on v4

--- a/solution.py
+++ b/solution.py
@@ -19,7 +19,7 @@
 FG = TS * TILE
 
 GROUP = 4
-UNROLL = 48
+UNROLL = 64
 CHUNK_ENDS = (2, 4)
 
 F32, BF16, I32 = jnp.float32, jnp.bfloat16, jnp.int32

time: 53 us -> 52.4 us (0.989)
  Pallas kernels: 22.2 us -> 21.2 us
  waiting for transfers between devices: 11.5 us -> 12.4 us
    pallas_call x4, Pallas kernels: 18.6 us -> 17.6 us  [grid_call(): pl.pallas_call(functools.partial(grid_kernel, steps, first, last, list_pl...]
    ppermute x6, waiting for transfers between devices: 1.2 us -> 2.13 us  [body(): got[s] = lax.ppermute(pieces[s], 'stn', pairs)]
  transfers between devices with their start and end apart: 7 -> 7, of which waited for: 3 -> 3; matrix products, arithmetic and copies ran while one was open for 1% -> 1% of each run, Pallas kernels for 29% -> 27%
where the time goes in v5:
time: 52.4 us; the launch traced here: 52.2 us
  Pallas kernels  21.2 us (40%)
  starting transfers between devices  15.4 us (29%)
  waiting for transfers between devices  12.4 us (24%)
  local copies, waits for them, and re-layouts  2.11 us (4%)
  other arithmetic  0.99 us (2%)
    pallas_call x4, Pallas kernels, grid_call(): pl.pallas_call(functools.partial(grid_kernel, steps, first, last, list_pl...  17.6 us
    all_to_all x1, waiting for transfers between devices, body(): lax.all_to_all(pieces, ('stn', 'chan'), split_axis=0, concat_axis=0, tile...  10.3 us
    ppermute x6, starting transfers between devices, body(): got[s] = lax.ppermute(pieces[s], 'stn', pairs)  10.2 us
    all_to_all x1, starting transfers between devices, body(): lax.all_to_all(pieces, ('stn', 'chan'), split_axis=0, concat_axis=0, tile...  5.17 us
    pallas_call x1, Pallas kernels, group_lists(): pl.pallas_call(kernel, grid=(1,), in_specs=[whole_block(facet_ids.shape),...  2.34 us
    ppermute x6, waiting for transfers between devices, body(): got[s] = lax.ppermute(pieces[s], 'stn', pairs)  2.13 us
    unnamed x16, local copies, waits for them, and re-layouts  2.03 us
    pallas_call x2, Pallas kernels, deal_channels(): pl.pallas_call(functools.partial(deal_kernel, begin, end, facets), grid=(...  1.23 us
  transfers between devices with their start and end apart: 7, of which 3 were waited for; matrix products, arithmetic and copies ran while one was open for 1% of the time, Pallas kernels for 27%

profile of v5, /device:TPU:0, one launch (start us, length us, event | category | flops | bytes accessed | tf_op | source)
XLA Modules:
  0.0 52.2 jit_solution(1156244522859561689)
XLA Ops:
  0.0 0.0 copy-start
  0.0 1.2 %copy-done = bf16[64,16,512]{2,1,0:T(8,128)(2,1)S(1)} copy-done((bf16[64,16,512]{2,1,0:T(8,128)(2,1)S(1)}, bf16[64,16,512]{2,1,0:T(8,128)(2,1)}, u32[]{:S(2)}) %copy-start) | copy-done | bytes 1048600
  1.2 0.0 copy-start.1
  1.2 0.6 %shard_map.75 = (bf16[2,64,512]{2,1,0:T(8,128)(2,1)S(1)}, bf16[2,64,512]{2,1,0:T(8,128)(2,1)S(1)}, bf16[2,64,512]{2,1,0:T(8,128)(2,1)S(1)}, bf16[2,64,512]{2,1,0:T(8,128)(2,1)S(1)}) custom-call(bf16[64,16,512]{2,1,0:T(8,128)(2,1)S(1)} %copy-done), custom_call_target="tpu_custom_call" | custom-call | tf_op jit(solution)/shard_map/pallas_call | solution.py:295
  1.8 0.0 copy-start.4
  1.8 5.1 %collective-permute-start.3 = (bf16[2,64,512]{2,1,0:T(8,128)(2,1)S(1)}, bf16[2,64,512]{2,1,0:T(8,128)(2,1)S(1)}, u32[]{:S(2)}, u32[]{:S(2)}) collective-permute-start(bf16[2,64,512]{2,1,0:T(8,128)(2,1)S(1)} %get-tuple-element.26), channel_id=1, source_target_pairs={{0,24},{8,16},{16,8},{24,0},{1,25},{9,17},{17,9},{25,1},{2,26},{10... | collective-permute-start | bytes 393224 | tf_op jit(solution)/shard_map/ppermute | solution.py:401
  7.0 0.0 collective-permute-start.4
  7.0 0.6 %collective-permute-start.5 = (bf16[2,64,512]{2,1,0:T(8,128)(2,1)S(1)}, bf16[2,64,512]{2,1,0:T(8,128)(2,1)S(1)}, u32[]{:S(2)}, u32[]{:S(2)}) collective-permute-start(bf16[2,64,512]{2,1,0:T(8,128)(2,1)S(1)} %get-tuple-element.28), channel_id=1, source_target_pairs={{0,16},{8,24},{16,0},{24,8},{1,17},{9,25},{17,1},{25,9},{2,18},{10... | collective-permute-start | bytes 393224 | tf_op jit(solution)/shard_map/ppermute | solution.py:401
  7.6 0.0 copy-done.4
  7.6 0.0 copy-start.5
  7.6 0.7 %copy-done.5 = s32[1,1,2048]{2,1,0:T(1,128)S(1)} copy-done((s32[1,1,2048]{2,1,0:T(1,128)S(1)}, s32[1,1,2048]{2,1,0:T(1,128)}, u32[]{:S(2)}) %copy-start.5) | copy-done | bytes 8216
  8.3 0.0 copy-start.6
  8.3 2.3 %shard_map.73 = (s32[16,128]{1,0:T(8,128)S(1)}, s32[16,128]{1,0:T(8,128)S(1)}, s32[16,128]{1,0:T(8,128)S(1)}, s32[16,128]{1,0:T(8,128)S(1)}) custom-call(s32[16,128]{1,0:T(8,128)S(1)} %bitcast.22, s32[16,128]{1,0:T(8,128)S(1)} %bitcast.23), custom_call_target="tpu_custom_call" | custom-call | tf_op jit(solution)/shard_map/pallas_call | solution.py:121
  10.7 0.0 copy-done.1
  10.7 0.6 %shard_map.74 = (bf16[2,64,512]{2,1,0:T(8,128)(2,1)S(1)}, bf16[2,64,512]{2,1,0:T(8,128)(2,1)S(1)}, bf16[2,64,512]{2,1,0:T(8,128)(2,1)S(1)}, bf16[2,64,512]{2,1,0:T(8,128)(2,1)S(1)}) custom-call(bf16[64,16,512]{2,1,0:T(8,128)(2,1)S(1)} %copy-done.1, s32[2048]{0:T(1024)S(1)} %bitcast.17), custom_call_target="tpu_custom_call" | custom-call | tf_op jit(solution)/shard_map/pallas_call | solution.py:295
  11.3 1.5 %collective-permute-start = (bf16[2,64,512]{2,1,0:T(8,128)(2,1)S(1)}, bf16[2,64,512]{2,1,0:T(8,128)(2,1)S(1)}, u32[]{:S(2)}, u32[]{:S(2)}) collective-permute-start(bf16[2,64,512]{2,1,0:T(8,128)(2,1)S(1)} %get-tuple-element.20), channel_id=1, source_target_pairs={{0,8},{8,0},{16,24},{24,16},{1,9},{9,1},{17,25},{25,17},{2,10},{10... | collective-permute-start | bytes 393224 | tf_op jit(solution)/shard_map/ppermute | solution.py:401
  12.7 2.4 %collective-permute-start.1 = (bf16[2,64,512]{2,1,0:T(8,128)(2,1)S(1)}, bf16[2,64,512]{2,1,0:T(8,128)(2,1)S(1)}, u32[]{:S(2)}, u32[]{:S(2)}) collective-permute-start(bf16[2,64,512]{2,1,0:T(8,128)(2,1)S(1)} %get-tuple-element.21), channel_id=1, source_target_pairs={{0,24},{8,16},{16,8},{24,0},{1,25},{9,17},{17,9},{25,1},{2,26},{10... | collective-permute-start | bytes 393224 | tf_op jit(solution)/shard_map/ppermute | solution.py:401
  15.2 0.0 copy-done.6
  15.2 0.1 slice_bitcast_fusion
  15.3 0.0 copy-start.7
  15.3 0.0 collective-permute-done.3.refs_1_
  15.3 0.6 %collective-permute-start.2 = (bf16[2,64,512]{2,1,0:T(8,128)(2,1)S(1)}, bf16[2,64,512]{2,1,0:T(8,128)(2,1)S(1)}, u32[]{:S(2)}, u32[]{:S(2)}) collective-permute-start(bf16[2,64,512]{2,1,0:T(8,128)(2,1)S(1)} %get-tuple-element.22), channel_id=1, source_target_pairs={{0,16},{8,24},{16,0},{24,8},{1,17},{9,25},{17,1},{25,9},{2,18},{10... | collective-permute-start | bytes 393224 | tf_op jit(solution)/shard_map/ppermute | solution.py:401
  15.8 0.1 copy-done.7
  15.9 0.0 collective-permute-done.4.refs_2_
  15.9 3.3 %shard_map.76.refs_5_ = f32[64,32,64]{2,1,0:T(8,128)S(1)} custom-call(s32[2048]{0:T(1024)S(1)} %bitcast.18, bf16[2,64,512]{2,1,0:T(8,128)(2,1)S(1)} %get-tuple-element.25.refs_0_, bf16[2,64,512]{2,1,0:T(8,128)(2,1)S(1)} %collective-permute-done.3.refs_1_, bf16[2,64,512]{2,1,0:T(8,128)(2,1)S(1)} %collective-permute-done.4.refs_2_, ...), custom_call_target="tpu_custom_call" | custom-call | tf_op jit(solution)/shard_map/pallas_call | solution.py:324
  19.2 0.7 %collective-permute-done.5.refs_3_ = bf16[2,64,512]{2,1,0:T(8,128)(2,1)S(1)} collective-permute-done((bf16[2,64,512]{2,1,0:T(8,128)(2,1)S(1)}, bf16[2,64,512]{2,1,0:T(8,128)(2,1)S(1)}, u32[]{:S(2)}, u32[]{:S(2)}) %collective-permute-start.5) | collective-permute-done | bytes 131104 | tf_op jit(solution)/shard_map/ppermute | solution.py:401
  19.8 4.6 %shard_map.77.refs_4_ = f32[64,32,64]{2,1,0:T(8,128)S(1)} custom-call(s32[2048]{0:T(1024)S(1)} %bitcast.21, bf16[2,64,512]{2,1,0:T(8,128)(2,1)S(1)} %get-tuple-element.25.refs_0_, bf16[2,64,512]{2,1,0:T(8,128)(2,1)S(1)} %collective-permute-done.3.refs_1_, bf16[2,64,512]{2,1,0:T(8,128)(2,1)S(1)} %collective-permute-done.4.refs_2_, ...), custom_call_target="tpu_custom_call" | custom-call | tf_op jit(solution)/shard_map/pallas_call | solution.py:324
  24.4 0.0 collective-permute-done.refs_1_
  24.4 0.0 collective-permute-done.1.refs_2_
  24.4 0.0 copy-start.2
  24.4 0.0 copy-start.3
  24.5 3.3 %shard_map.78.refs_5_ = f32[64,32,64]{2,1,0:T(8,128)S(1)} custom-call(s32[2048]{0:T(1024)S(1)} %bitcast.20, bf16[2,64,512]{2,1,0:T(8,128)(2,1)S(1)} %get-tuple-element.19.refs_0_, bf16[2,64,512]{2,1,0:T(8,128)(2,1)S(1)} %collective-permute-done.refs_1_, bf16[2,64,512]{2,1,0:T(8,128)(2,1)S(1)} %collective-permute-done.1.refs_2_, ...), custom_call_target="tpu_custom_call" | custom-call | tf_op jit(solution)/shard_map/pallas_call | solution.py:324
  27.8 1.5 %collective-permute-done.2.refs_3_ = bf16[2,64,512]{2,1,0:T(8,128)(2,1)S(1)} collective-permute-done((bf16[2,64,512]{2,1,0:T(8,128)(2,1)S(1)}, bf16[2,64,512]{2,1,0:T(8,128)(2,1)S(1)}, u32[]{:S(2)}, u32[]{:S(2)}) %collective-permute-start.2) | collective-permute-done | bytes 131104 | tf_op jit(solution)/shard_map/ppermute | solution.py:401
  29.3 0.0 copy-done.2
  29.3 0.0 copy-done.3
  29.3 6.4 %shard_map.79 = bf16[512,256]{1,0:T(8,128)(2,1)} custom-call(s32[2048]{0:T(1024)S(1)} %bitcast.19, bf16[2,64,512]{2,1,0:T(8,128)(2,1)S(1)} %get-tuple-element.19.refs_0_, bf16[2,64,512]{2,1,0:T(8,128)(2,1)S(1)} %collective-permute-done.refs_1_, bf16[2,64,512]{2,1,0:T(8,128)(2,1)S(1)} %collective-permute-done.1.refs_2_, ...), custom_call_target="tpu_custom_call" | custom-call | tf_op jit(solution)/shard_map/pallas_call | solution.py:324
  35.7 5.2 %all-to-all-start = ((bf16[32,16,256]{2,1,0:T(8,128)(2,1)}), bf16[32,16,256]{2,1,0:T(8,128)(2,1)S(1)}, u32[]{:S(2)}, u32[]{:S(2)}) async-start(bf16[32,16,256]{2,1,0:T(8,128)(2,1)} %bitcast.8), calls=%async_computation | async-start | bytes 524288 | tf_op jit(solution)/shard_map/all_to_all | solution.py:416
  40.9 0.1 multiply_reduce_fusion.2
  41.0 0.1 dynamic-slice_multiply_fusion.1
  41.1 0.1 dynamic-slice_multiply_fusion
  41.1 0.1 fusion.9
  41.2 10.3 %all-to-all-done = bf16[32,16,256]{2,1,0:T(8,128)(2,1)S(1)} async-done(((bf16[32,16,256]{2,1,0:T(8,128)(2,1)}), bf16[32,16,256]{2,1,0:T(8,128)(2,1)S(1)}, u32[]{:S(2)}, u32[]{:S(2)}) %all-to-all-start) | async-done | bytes 262176 | tf_op jit(solution)/shard_map/all_to_all | solution.py:416
  51.5 0.6 %fusion = f32[2,16,128]{2,1,0:T(8,128)} fusion(f32[1,16,128]{2,1,0:T(8,128)S(1)} %get-tuple-element.38, f32[1,16,128]{2,1,0:T(8,128)S(1)} %get-tuple-element.39, f32[1,16,128]{2,1,0:T(8,128)S(1)} %get-tuple-element.37, f32[16,128]{1,0:T(8,128)S(1)} %get-tuple-element.36, f32[16,128]{1,0:T(8,128)S(1)} %get-tuple-element.35), kind=kLoop, calls=%fused_computation.4 | loop fusion | flops 20480 | bytes 57344 | tf_op jit(solution)/shard_map/add | solution.py:430
  (5 shorter events, 0.1 us)
Async XLA Ops:
  0.0 1.2 %copy-start = (bf16[64,16,512]{2,1,0:T(8,128)(2,1)S(1)}, bf16[64,16,512]{2,1,0:T(8,128)(2,1)}, u32[]{:S(2)}) copy-start(bf16[64,16,512]{2,1,0:T(8,128)(2,1)} %voltage_ref.3) | copy-start | bytes 3145732
  1.2 9.4 %copy-start.1 = (bf16[64,16,512]{2,1,0:T(8,128)(2,1)S(1)}, bf16[64,16,512]{2,1,0:T(8,128)(2,1)}, u32[]{:S(2)}) copy-start(bf16[64,16,512]{2,1,0:T(8,128)(2,1)} %voltage_ref.3) | copy-start | bytes 3145732
  1.8 5.8 %copy-start.4 = (s32[1,1,2048,1]{2,3,1,0:T(1,128)S(1)}, s32[1,1,2048,1]{2,3,1,0:T(1,128)}, u32[]{:S(2)}) copy-start(s32[1,1,2048,1]{2,3,1,0:T(1,128)} %param.8) | copy-start | bytes 24580
  1.8 13.4 %collective-permute-start.3 = (bf16[2,64,512]{2,1,0:T(8,128)(2,1)S(1)}, bf16[2,64,512]{2,1,0:T(8,128)(2,1)S(1)}, u32[]{:S(2)}, u32[]{:S(2)}) collective-permute-start(bf16[2,64,512]{2,1,0:T(8,128)(2,1)S(1)} %get-tuple-element.26), channel_id=1, source_target_pairs={{0,24},{8,16},{16,8},{24,0},{1,25},{9,17},{17,9},{25,1},{2,26},{10... | collective-permute-start | bytes 393224 | tf_op jit(solution)/shard_map/ppermute | solution.py:401
  7.0 9.0 %collective-permute-start.4 = (bf16[2,64,512]{2,1,0:T(8,128)(2,1)S(1)}, bf16[2,64,512]{2,1,0:T(8,128)(2,1)S(1)}, u32[]{:S(2)}, u32[]{:S(2)}) collective-permute-start(bf16[2,64,512]{2,1,0:T(8,128)(2,1)S(1)} %get-tuple-element.27), channel_id=1, source_target_pairs={{0,8},{8,0},{16,24},{24,16},{1,9},{9,1},{17,25},{25,17},{2,10},{10... | collective-permute-start | bytes 393224 | tf_op jit(solution)/shard_map/ppermute | solution.py:401
  7.0 12.9 %collective-permute-start.5 = (bf16[2,64,512]{2,1,0:T(8,128)(2,1)S(1)}, bf16[2,64,512]{2,1,0:T(8,128)(2,1)S(1)}, u32[]{:S(2)}, u32[]{:S(2)}) collective-permute-start(bf16[2,64,512]{2,1,0:T(8,128)(2,1)S(1)} %get-tuple-element.28), channel_id=1, source_target_pairs={{0,16},{8,24},{16,0},{24,8},{1,17},{9,25},{17,1},{25,9},{2,18},{10... | collective-permute-start | bytes 393224 | tf_op jit(solution)/shard_map/ppermute | solution.py:401
  7.6 0.7 %copy-start.5 = (s32[1,1,2048]{2,1,0:T(1,128)S(1)}, s32[1,1,2048]{2,1,0:T(1,128)}, u32[]{:S(2)}) copy-start(s32[1,1,2048]{2,1,0:T(1,128)} %param.9) | copy-start | bytes 24580
  8.3 6.9 %copy-start.6 = (s32[1,1,2048,128]{3,2,1,0:T(8,128)S(1)}, s32[1,1,2048,128]{3,2,1,0:T(8,128)}, u32[]{:S(2)}) copy-start(s32[1,1,2048,128]{3,2,1,0:T(8,128)} %param.10) | copy-start | bytes 3145732
  11.3 13.1 %collective-permute-start = (bf16[2,64,512]{2,1,0:T(8,128)(2,1)S(1)}, bf16[2,64,512]{2,1,0:T(8,128)(2,1)S(1)}, u32[]{:S(2)}, u32[]{:S(2)}) collective-permute-start(bf16[2,64,512]{2,1,0:T(8,128)(2,1)S(1)} %get-tuple-element.20), channel_id=1, source_target_pairs={{0,8},{8,0},{16,24},{24,16},{1,9},{9,1},{17,25},{25,17},{2,10},{10... | collective-permute-start | bytes 393224 | tf_op jit(solution)/shard_map/ppermute | solution.py:401
  12.7 11.7 %collective-permute-start.1 = (bf16[2,64,512]{2,1,0:T(8,128)(2,1)S(1)}, bf16[2,64,512]{2,1,0:T(8,128)(2,1)S(1)}, u32[]{:S(2)}, u32[]{:S(2)}) collective-permute-start(bf16[2,64,512]{2,1,0:T(8,128)(2,1)S(1)} %get-tuple-element.21), channel_id=1, source_target_pairs={{0,24},{8,16},{16,8},{24,0},{1,25},{9,17},{17,9},{25,1},{2,26},{10... | collective-permute-start | bytes 393224 | tf_op jit(solution)/shard_map/ppermute | solution.py:401
  15.3 0.7 %copy-start.7 = (bf16[2,8]{1,0:T(2,128)(2,1)S(1)}, bf16[2,8]{1,0:T(2,128)(2,1)}, u32[]{:S(2)}) copy-start(bf16[2,8]{1,0:T(2,128)(2,1)} %param.11) | copy-start | bytes 100
  15.3 14.0 %collective-permute-start.2 = (bf16[2,64,512]{2,1,0:T(8,128)(2,1)S(1)}, bf16[2,64,512]{2,1,0:T(8,128)(2,1)S(1)}, u32[]{:S(2)}, u32[]{:S(2)}) collective-permute-start(bf16[2,64,512]{2,1,0:T(8,128)(2,1)S(1)} %get-tuple-element.22), channel_id=1, source_target_pairs={{0,16},{8,24},{16,0},{24,8},{1,17},{9,25},{17,1},{25,9},{2,18},{10... | collective-permute-start | bytes 393224 | tf_op jit(solution)/shard_map/ppermute | solution.py:401
  24.4 4.8 %copy-start.2 = (bf16[2,512,256]{2,1,0:T(8,128)(2,1)S(1)}, bf16[2,512,256]{2,1,0:T(8,128)(2,1)}, u32[]{:S(2)}) copy-start(bf16[2,512,256]{2,1,0:T(8,128)(2,1)} %constant.36.clone.refs_7_) | copy-start | bytes 1572868
  24.4 4.8 %copy-start.3 = (bf16[2,256,128]{2,1,0:T(8,128)(2,1)S(1)}, bf16[2,256,128]{2,1,0:T(8,128)(2,1)}, u32[]{:S(2)}) copy-start(bf16[2,256,128]{2,1,0:T(8,128)(2,1)} %constant.35.clone.refs_6_) | copy-start | bytes 393220
  35.7 15.8 %all-to-all-start = ((bf16[32,16,256]{2,1,0:T(8,128)(2,1)}), bf16[32,16,256]{2,1,0:T(8,128)(2,1)S(1)}, u32[]{:S(2)}, u32[]{:S(2)}) async-start(bf16[32,16,256]{2,1,0:T(8,128)(2,1)} %bitcast.8), calls=%async_computation | async-start | bytes 524288 | tf_op jit(solution)/shard_map/all_to_all | solution.py:416

commit v6 on v5

--- a/solution.py
+++ b/solution.py
@@ -263,7 +263,10 @@
             ],
             axis=0,
         )
-        image = split_dot(two_halves(both), halves_of(column_table))
+        both = both.astype(BF16)
+        image = sum(
+            jnp.dot(both, half, preferred_element_type=F32) for half in halves_of(column_table)
+        )
         out_ref[...] = image.astype(out_ref.dtype)
 
 

time: 52.4 us -> 52.3 us (level)
  no operation moved by 1% of the time
where the time goes in v6:
time: 52.3 us; the launch traced here: 52 us
  Pallas kernels  21 us (40%)
  starting transfers between devices  15.4 us (29%)
  waiting for transfers between devices  12.4 us (24%)
  local copies, waits for them, and re-layouts  2.11 us (4%)
  other arithmetic  0.99 us (2%)
    pallas_call x4, Pallas kernels, grid_call(): pl.pallas_call(functools.partial(grid_kernel, steps, first, last, list_pl...  17.4 us
    all_to_all x1, waiting for transfers between devices, body(): lax.all_to_all(pieces, ('stn', 'chan'), split_axis=0, concat_axis=0, tile...  10.3 us
    ppermute x6, starting transfers between devices, body(): got[s] = lax.ppermute(pieces[s], 'stn', pairs)  10.2 us
    all_to_all x1, starting transfers between devices, body(): lax.all_to_all(pieces, ('stn', 'chan'), split_axis=0, concat_axis=0, tile...  5.17 us
    pallas_call x1, Pallas kernels, group_lists(): pl.pallas_call(kernel, grid=(1,), in_specs=[whole_block(facet_ids.shape),...  2.34 us
    ppermute x6, waiting for transfers between devices, body(): got[s] = lax.ppermute(pieces[s], 'stn', pairs)  2.14 us
    unnamed x16, local copies, waits for them, and re-layouts  2.03 us
    pallas_call x2, Pallas kernels, deal_channels(): pl.pallas_call(functools.partial(deal_kernel, begin, end, facets), grid=(...  1.23 us
  transfers between devices with their start and end apart: 7, of which 3 were waited for; matrix products, arithmetic and copies ran while one was open for 1% of the time, Pallas kernels for 27%

profile of v6, /device:TPU:0, one launch (start us, length us, event | category | flops | bytes accessed | tf_op | source)
XLA Modules:
  0.0 52.0 jit_solution(508595000100254856)
XLA Ops:
  0.0 0.0 copy-start
  0.0 1.2 %copy-done = bf16[64,16,512]{2,1,0:T(8,128)(2,1)S(1)} copy-done((bf16[64,16,512]{2,1,0:T(8,128)(2,1)S(1)}, bf16[64,16,512]{2,1,0:T(8,128)(2,1)}, u32[]{:S(2)}) %copy-start) | copy-done | bytes 1048600
  1.2 0.0 copy-start.1
  1.2 0.6 %shard_map.75 = (bf16[2,64,512]{2,1,0:T(8,128)(2,1)S(1)}, bf16[2,64,512]{2,1,0:T(8,128)(2,1)S(1)}, bf16[2,64,512]{2,1,0:T(8,128)(2,1)S(1)}, bf16[2,64,512]{2,1,0:T(8,128)(2,1)S(1)}) custom-call(bf16[64,16,512]{2,1,0:T(8,128)(2,1)S(1)} %copy-done), custom_call_target="tpu_custom_call" | custom-call | tf_op jit(solution)/shard_map/pallas_call | solution.py:298
  1.8 0.0 copy-start.4
  1.8 5.1 %collective-permute-start.3 = (bf16[2,64,512]{2,1,0:T(8,128)(2,1)S(1)}, bf16[2,64,512]{2,1,0:T(8,128)(2,1)S(1)}, u32[]{:S(2)}, u32[]{:S(2)}) collective-permute-start(bf16[2,64,512]{2,1,0:T(8,128)(2,1)S(1)} %get-tuple-element.26), channel_id=1, source_target_pairs={{0,24},{8,16},{16,8},{24,0},{1,25},{9,17},{17,9},{25,1},{2,26},{10... | collective-permute-start | bytes 393224 | tf_op jit(solution)/shard_map/ppermute | solution.py:404
  7.0 0.0 collective-permute-start.4
  7.0 0.6 %collective-permute-start.5 = (bf16[2,64,512]{2,1,0:T(8,128)(2,1)S(1)}, bf16[2,64,512]{2,1,0:T(8,128)(2,1)S(1)}, u32[]{:S(2)}, u32[]{:S(2)}) collective-permute-start(bf16[2,64,512]{2,1,0:T(8,128)(2,1)S(1)} %get-tuple-element.28), channel_id=1, source_target_pairs={{0,16},{8,24},{16,0},{24,8},{1,17},{9,25},{17,1},{25,9},{2,18},{10... | collective-permute-start | bytes 393224 | tf_op jit(solution)/shard_map/ppermute | solution.py:404
  7.6 0.0 copy-done.4
  7.6 0.0 copy-start.5
  7.6 0.7 %copy-done.5 = s32[1,1,2048]{2,1,0:T(1,128)S(1)} copy-done((s32[1,1,2048]{2,1,0:T(1,128)S(1)}, s32[1,1,2048]{2,1,0:T(1,128)}, u32[]{:S(2)}) %copy-start.5) | copy-done | bytes 8216
  8.3 0.0 copy-start.6
  8.3 2.3 %shard_map.73 = (s32[16,128]{1,0:T(8,128)S(1)}, s32[16,128]{1,0:T(8,128)S(1)}, s32[16,128]{1,0:T(8,128)S(1)}, s32[16,128]{1,0:T(8,128)S(1)}) custom-call(s32[16,128]{1,0:T(8,128)S(1)} %bitcast.22, s32[16,128]{1,0:T(8,128)S(1)} %bitcast.23), custom_call_target="tpu_custom_call" | custom-call | tf_op jit(solution)/shard_map/pallas_call | solution.py:121
  10.7 0.0 copy-done.1
  10.7 0.6 %shard_map.74 = (bf16[2,64,512]{2,1,0:T(8,128)(2,1)S(1)}, bf16[2,64,512]{2,1,0:T(8,128)(2,1)S(1)}, bf16[2,64,512]{2,1,0:T(8,128)(2,1)S(1)}, bf16[2,64,512]{2,1,0:T(8,128)(2,1)S(1)}) custom-call(bf16[64,16,512]{2,1,0:T(8,128)(2,1)S(1)} %copy-done.1, s32[2048]{0:T(1024)S(1)} %bitcast.17), custom_call_target="tpu_custom_call" | custom-call | tf_op jit(solution)/shard_map/pallas_call | solution.py:298
  11.3 1.5 %collective-permute-start = (bf16[2,64,512]{2,1,0:T(8,128)(2,1)S(1)}, bf16[2,64,512]{2,1,0:T(8,128)(2,1)S(1)}, u32[]{:S(2)}, u32[]{:S(2)}) collective-permute-start(bf16[2,64,512]{2,1,0:T(8,128)(2,1)S(1)} %get-tuple-element.20), channel_id=1, source_target_pairs={{0,8},{8,0},{16,24},{24,16},{1,9},{9,1},{17,25},{25,17},{2,10},{10... | collective-permute-start | bytes 393224 | tf_op jit(solution)/shard_map/ppermute | solution.py:404
  12.7 2.4 %collective-permute-start.1 = (bf16[2,64,512]{2,1,0:T(8,128)(2,1)S(1)}, bf16[2,64,512]{2,1,0:T(8,128)(2,1)S(1)}, u32[]{:S(2)}, u32[]{:S(2)}) collective-permute-start(bf16[2,64,512]{2,1,0:T(8,128)(2,1)S(1)} %get-tuple-element.21), channel_id=1, source_target_pairs={{0,24},{8,16},{16,8},{24,0},{1,25},{9,17},{17,9},{25,1},{2,26},{10... | collective-permute-start | bytes 393224 | tf_op jit(solution)/shard_map/ppermute | solution.py:404
  15.2 0.0 copy-done.6
  15.2 0.1 slice_bitcast_fusion
  15.3 0.0 copy-start.7
  15.3 0.0 collective-permute-done.3.refs_1_
  15.3 0.6 %collective-permute-start.2 = (bf16[2,64,512]{2,1,0:T(8,128)(2,1)S(1)}, bf16[2,64,512]{2,1,0:T(8,128)(2,1)S(1)}, u32[]{:S(2)}, u32[]{:S(2)}) collective-permute-start(bf16[2,64,512]{2,1,0:T(8,128)(2,1)S(1)} %get-tuple-element.22), channel_id=1, source_target_pairs={{0,16},{8,24},{16,0},{24,8},{1,17},{9,25},{17,1},{25,9},{2,18},{10... | collective-permute-start | bytes 393224 | tf_op jit(solution)/shard_map/ppermute | solution.py:404
  15.8 0.1 copy-done.7
  15.9 0.0 collective-permute-done.4.refs_2_
  15.9 3.2 %shard_map.76.refs_5_ = f32[64,32,64]{2,1,0:T(8,128)S(1)} custom-call(s32[2048]{0:T(1024)S(1)} %bitcast.18, bf16[2,64,512]{2,1,0:T(8,128)(2,1)S(1)} %get-tuple-element.25.refs_0_, bf16[2,64,512]{2,1,0:T(8,128)(2,1)S(1)} %collective-permute-done.3.refs_1_, bf16[2,64,512]{2,1,0:T(8,128)(2,1)S(1)} %collective-permute-done.4.refs_2_, ...), custom_call_target="tpu_custom_call" | custom-call | tf_op jit(solution)/shard_map/pallas_call | solution.py:327
  19.2 0.7 %collective-permute-done.5.refs_3_ = bf16[2,64,512]{2,1,0:T(8,128)(2,1)S(1)} collective-permute-done((bf16[2,64,512]{2,1,0:T(8,128)(2,1)S(1)}, bf16[2,64,512]{2,1,0:T(8,128)(2,1)S(1)}, u32[]{:S(2)}, u32[]{:S(2)}) %collective-permute-start.5) | collective-permute-done | bytes 131104 | tf_op jit(solution)/shard_map/ppermute | solution.py:404
  19.8 4.6 %shard_map.77.refs_4_ = f32[64,32,64]{2,1,0:T(8,128)S(1)} custom-call(s32[2048]{0:T(1024)S(1)} %bitcast.21, bf16[2,64,512]{2,1,0:T(8,128)(2,1)S(1)} %get-tuple-element.25.refs_0_, bf16[2,64,512]{2,1,0:T(8,128)(2,1)S(1)} %collective-permute-done.3.refs_1_, bf16[2,64,512]{2,1,0:T(8,128)(2,1)S(1)} %collective-permute-done.4.refs_2_, ...), custom_call_target="tpu_custom_call" | custom-call | tf_op jit(solution)/shard_map/pallas_call | solution.py:327
  24.4 0.0 collective-permute-done.refs_1_
  24.4 0.0 collective-permute-done.1.refs_2_
  24.4 0.0 copy-start.2
  24.4 0.0 copy-start.3
  24.5 3.3 %shard_map.78.refs_5_ = f32[64,32,64]{2,1,0:T(8,128)S(1)} custom-call(s32[2048]{0:T(1024)S(1)} %bitcast.20, bf16[2,64,512]{2,1,0:T(8,128)(2,1)S(1)} %get-tuple-element.19.refs_0_, bf16[2,64,512]{2,1,0:T(8,128)(2,1)S(1)} %collective-permute-done.refs_1_, bf16[2,64,512]{2,1,0:T(8,128)(2,1)S(1)} %collective-permute-done.1.refs_2_, ...), custom_call_target="tpu_custom_call" | custom-call | tf_op jit(solution)/shard_map/pallas_call | solution.py:327
  27.8 1.5 %collective-permute-done.2.refs_3_ = bf16[2,64,512]{2,1,0:T(8,128)(2,1)S(1)} collective-permute-done((bf16[2,64,512]{2,1,0:T(8,128)(2,1)S(1)}, bf16[2,64,512]{2,1,0:T(8,128)(2,1)S(1)}, u32[]{:S(2)}, u32[]{:S(2)}) %collective-permute-start.2) | collective-permute-done | bytes 131104 | tf_op jit(solution)/shard_map/ppermute | solution.py:404
  29.3 0.0 copy-done.2
  29.3 0.0 copy-done.3
  29.3 6.3 %shard_map.79 = bf16[512,256]{1,0:T(8,128)(2,1)} custom-call(s32[2048]{0:T(1024)S(1)} %bitcast.19, bf16[2,64,512]{2,1,0:T(8,128)(2,1)S(1)} %get-tuple-element.19.refs_0_, bf16[2,64,512]{2,1,0:T(8,128)(2,1)S(1)} %collective-permute-done.refs_1_, bf16[2,64,512]{2,1,0:T(8,128)(2,1)S(1)} %collective-permute-done.1.refs_2_, ...), custom_call_target="tpu_custom_call" | custom-call | tf_op jit(solution)/shard_map/pallas_call | solution.py:327
  35.6 5.2 %all-to-all-start = ((bf16[32,16,256]{2,1,0:T(8,128)(2,1)}), bf16[32,16,256]{2,1,0:T(8,128)(2,1)S(1)}, u32[]{:S(2)}, u32[]{:S(2)}) async-start(bf16[32,16,256]{2,1,0:T(8,128)(2,1)} %bitcast.8), calls=%async_computation | async-start | bytes 524288 | tf_op jit(solution)/shard_map/all_to_all | solution.py:419
  40.7 0.1 multiply_reduce_fusion.2
  40.8 0.1 dynamic-slice_multiply_fusion.1
  40.9 0.1 dynamic-slice_multiply_fusion
  41.0 0.1 fusion.9
  41.1 10.3 %all-to-all-done = bf16[32,16,256]{2,1,0:T(8,128)(2,1)S(1)} async-done(((bf16[32,16,256]{2,1,0:T(8,128)(2,1)}), bf16[32,16,256]{2,1,0:T(8,128)(2,1)S(1)}, u32[]{:S(2)}, u32[]{:S(2)}) %all-to-all-start) | async-done | bytes 262176 | tf_op jit(solution)/shard_map/all_to_all | solution.py:419
  51.4 0.6 %fusion = f32[2,16,128]{2,1,0:T(8,128)} fusion(f32[1,16,128]{2,1,0:T(8,128)S(1)} %get-tuple-element.38, f32[1,16,128]{2,1,0:T(8,128)S(1)} %get-tuple-element.39, f32[1,16,128]{2,1,0:T(8,128)S(1)} %get-tuple-element.37, f32[16,128]{1,0:T(8,128)S(1)} %get-tuple-element.36, f32[16,128]{1,0:T(8,128)S(1)} %get-tuple-element.35), kind=kLoop, calls=%fused_computation.4 | loop fusion | flops 20480 | bytes 57344 | tf_op jit(solution)/shard_map/add | solution.py:433
  (5 shorter events, 0.1 us)
Async XLA Ops:
  0.0 1.2 %copy-start = (bf16[64,16,512]{2,1,0:T(8,128)(2,1)S(1)}, bf16[64,16,512]{2,1,0:T(8,128)(2,1)}, u32[]{:S(2)}) copy-start(bf16[64,16,512]{2,1,0:T(8,128)(2,1)} %voltage_ref.3) | copy-start | bytes 3145732
  1.2 9.4 %copy-start.1 = (bf16[64,16,512]{2,1,0:T(8,128)(2,1)S(1)}, bf16[64,16,512]{2,1,0:T(8,128)(2,1)}, u32[]{:S(2)}) copy-start(bf16[64,16,512]{2,1,0:T(8,128)(2,1)} %voltage_ref.3) | copy-start | bytes 3145732
  1.8 5.8 %copy-start.4 = (s32[1,1,2048,1]{2,3,1,0:T(1,128)S(1)}, s32[1,1,2048,1]{2,3,1,0:T(1,128)}, u32[]{:S(2)}) copy-start(s32[1,1,2048,1]{2,3,1,0:T(1,128)} %param.8) | copy-start | bytes 24580
  1.8 13.4 %collective-permute-start.3 = (bf16[2,64,512]{2,1,0:T(8,128)(2,1)S(1)}, bf16[2,64,512]{2,1,0:T(8,128)(2,1)S(1)}, u32[]{:S(2)}, u32[]{:S(2)}) collective-permute-start(bf16[2,64,512]{2,1,0:T(8,128)(2,1)S(1)} %get-tuple-element.26), channel_id=1, source_target_pairs={{0,24},{8,16},{16,8},{24,0},{1,25},{9,17},{17,9},{25,1},{2,26},{10... | collective-permute-start | bytes 393224 | tf_op jit(solution)/shard_map/ppermute | solution.py:404
  7.0 9.0 %collective-permute-start.4 = (bf16[2,64,512]{2,1,0:T(8,128)(2,1)S(1)}, bf16[2,64,512]{2,1,0:T(8,128)(2,1)S(1)}, u32[]{:S(2)}, u32[]{:S(2)}) collective-permute-start(bf16[2,64,512]{2,1,0:T(8,128)(2,1)S(1)} %get-tuple-element.27), channel_id=1, source_target_pairs={{0,8},{8,0},{16,24},{24,16},{1,9},{9,1},{17,25},{25,17},{2,10},{10... | collective-permute-start | bytes 393224 | tf_op jit(solution)/shard_map/ppermute | solution.py:404
  7.0 12.9 %collective-permute-start.5 = (bf16[2,64,512]{2,1,0:T(8,128)(2,1)S(1)}, bf16[2,64,512]{2,1,0:T(8,128)(2,1)S(1)}, u32[]{:S(2)}, u32[]{:S(2)}) collective-permute-start(bf16[2,64,512]{2,1,0:T(8,128)(2,1)S(1)} %get-tuple-element.28), channel_id=1, source_target_pairs={{0,16},{8,24},{16,0},{24,8},{1,17},{9,25},{17,1},{25,9},{2,18},{10... | collective-permute-start | bytes 393224 | tf_op jit(solution)/shard_map/ppermute | solution.py:404
  7.6 0.7 %copy-start.5 = (s32[1,1,2048]{2,1,0:T(1,128)S(1)}, s32[1,1,2048]{2,1,0:T(1,128)}, u32[]{:S(2)}) copy-start(s32[1,1,2048]{2,1,0:T(1,128)} %param.9) | copy-start | bytes 24580
  8.3 6.9 %copy-start.6 = (s32[1,1,2048,128]{3,2,1,0:T(8,128)S(1)}, s32[1,1,2048,128]{3,2,1,0:T(8,128)}, u32[]{:S(2)}) copy-start(s32[1,1,2048,128]{3,2,1,0:T(8,128)} %param.10) | copy-start | bytes 3145732
  11.3 13.1 %collective-permute-start = (bf16[2,64,512]{2,1,0:T(8,128)(2,1)S(1)}, bf16[2,64,512]{2,1,0:T(8,128)(2,1)S(1)}, u32[]{:S(2)}, u32[]{:S(2)}) collective-permute-start(bf16[2,64,512]{2,1,0:T(8,128)(2,1)S(1)} %get-tuple-element.20), channel_id=1, source_target_pairs={{0,8},{8,0},{16,24},{24,16},{1,9},{9,1},{17,25},{25,17},{2,10},{10... | collective-permute-start | bytes 393224 | tf_op jit(solution)/shard_map/ppermute | solution.py:404
  12.7 11.7 %collective-permute-start.1 = (bf16[2,64,512]{2,1,0:T(8,128)(2,1)S(1)}, bf16[2,64,512]{2,1,0:T(8,128)(2,1)S(1)}, u32[]{:S(2)}, u32[]{:S(2)}) collective-permute-start(bf16[2,64,512]{2,1,0:T(8,128)(2,1)S(1)} %get-tuple-element.21), channel_id=1, source_target_pairs={{0,24},{8,16},{16,8},{24,0},{1,25},{9,17},{17,9},{25,1},{2,26},{10... | collective-permute-start | bytes 393224 | tf_op jit(solution)/shard_map/ppermute | solution.py:404
  15.3 0.7 %copy-start.7 = (bf16[2,8]{1,0:T(2,128)(2,1)S(1)}, bf16[2,8]{1,0:T(2,128)(2,1)}, u32[]{:S(2)}) copy-start(bf16[2,8]{1,0:T(2,128)(2,1)} %param.11) | copy-start | bytes 100
  15.3 14.0 %collective-permute-start.2 = (bf16[2,64,512]{2,1,0:T(8,128)(2,1)S(1)}, bf16[2,64,512]{2,1,0:T(8,128)(2,1)S(1)}, u32[]{:S(2)}, u32[]{:S(2)}) collective-permute-start(bf16[2,64,512]{2,1,0:T(8,128)(2,1)S(1)} %get-tuple-element.22), channel_id=1, source_target_pairs={{0,16},{8,24},{16,0},{24,8},{1,17},{9,25},{17,1},{25,9},{2,18},{10... | collective-permute-start | bytes 393224 | tf_op jit(solution)/shard_map/ppermute | solution.py:404
  24.4 4.8 %copy-start.2 = (bf16[2,512,256]{2,1,0:T(8,128)(2,1)S(1)}, bf16[2,512,256]{2,1,0:T(8,128)(2,1)}, u32[]{:S(2)}) copy-start(bf16[2,512,256]{2,1,0:T(8,128)(2,1)} %constant.36.clone.refs_7_) | copy-start | bytes 1572868
  24.4 4.8 %copy-start.3 = (bf16[2,256,128]{2,1,0:T(8,128)(2,1)S(1)}, bf16[2,256,128]{2,1,0:T(8,128)(2,1)}, u32[]{:S(2)}) copy-start(bf16[2,256,128]{2,1,0:T(8,128)(2,1)} %constant.35.clone.refs_6_) | copy-start | bytes 393220
  35.6 15.8 %all-to-all-start = ((bf16[32,16,256]{2,1,0:T(8,128)(2,1)}), bf16[32,16,256]{2,1,0:T(8,128)(2,1)S(1)}, u32[]{:S(2)}, u32[]{:S(2)}) async-start(bf16[32,16,256]{2,1,0:T(8,128)(2,1)} %bitcast.8), calls=%async_computation | async-start | bytes 524288 | tf_op jit(solution)/shard_map/all_to_all | solution.py:419
